TPU v7x, 32 devices: a whole 2x2x4 slice. The times are simulated.
32 devices in a mesh: dp: 4 (over y, x), expert: 2 (over core), tensor: 4 (over z).
Axes of the slice: x: 2, y: 2, z: 4, core: 2. Of those that a mesh axis runs over, the one named last changes fastest.
Arguments:
- tokens: bfloat16 [4096, 2048], P(('dp', 'expert')), may hold values from -6 to 6
- cotangent: bfloat16 [4096, 2048], P(('dp', 'expert')), may hold values from -6 to 6
- route_ids: int32 [4096, 8], P(('dp', 'expert')), may hold values from 0 to 15, all different within a row; in each aligned block of 512 rows (0 to 511, 512 to 1023, ...) at most 320 rows name the same one
- route_weight: float32 [4096, 8], P(('dp', 'expert')), may hold values from 0.05 to 0.5
- lengths: int32 [8], P(('dp', 'expert')), may hold values from 128 to 512, as said below
- attention_norm: bfloat16 [2048], P(('dp', 'expert')), may hold values from 0.5 to 2
- query_weight: bfloat16 [2048, 4096], P(('dp', 'expert'), 'tensor'), may hold values from -0.125 to 0.125
- key_matrix: bfloat16 [2048, 512], P(('dp', 'expert'), 'tensor'), may hold values from -0.125 to 0.125
- value_matrix: bfloat16 [2048, 512], P(('dp', 'expert'), 'tensor'), may hold values from -0.125 to 0.125
- output_weight: bfloat16 [2048, 4096], P(('dp', 'expert'), 'tensor'), may hold values from -0.375 to 0.375
- query_norm: bfloat16 [128], P(('dp', 'expert')), may hold values from 0.5 to 2
- key_norm: bfloat16 [128], P(('dp', 'expert')), may hold values from 0.5 to 2
- experts_norm: bfloat16 [2048], P(('dp', 'expert')), may hold values from 0.5 to 2
- gate_weight: bfloat16 [16, 768, 2048], P('expert', 'tensor', 'dp'), may hold values from -0.125 to 0.125
- up_weight: bfloat16 [16, 768, 2048], P('expert', 'tensor', 'dp'), may hold values from -0.125 to 0.125
- down_weight: bfloat16 [16, 768, 2048], P('expert', 'tensor', 'dp'), may hold values from -0.4375 to 0.4375
Outputs:
- output: bfloat16 [4096, 2048], P(('dp', 'expert'))
- tokens_grad: float32 [4096, 2048], P(('dp', 'expert'))
- attention_norm_grad: float32 [2048], P(('dp', 'expert'))
- query_weight_grad: float32 [2048, 4096], P(('dp', 'expert'), 'tensor')
- key_weight_grad: float32 [2048, 512], P(('dp', 'expert'), 'tensor')
- value_weight_grad: float32 [2048, 512], P(('dp', 'expert'), 'tensor')
- output_weight_grad: float32 [2048, 4096], P(('dp', 'expert'), 'tensor')
- query_norm_grad: float32 [128], P(('dp', 'expert'))
- key_norm_grad: float32 [128], P(('dp', 'expert'))
- experts_norm_grad: float32 [2048], P(('dp', 'expert'))
- gate_weight_grad: float32 [16, 768, 2048], P('expert', 'tensor', 'dp')
- up_weight_grad: float32 [16, 768, 2048], P('expert', 'tensor', 'dp')
- down_weight_grad: float32 [16, 768, 2048], P('expert', 'tensor', 'dp')
Inputs may be any that keep to these rules, and one draw needn't show every extreme that they name: `route_ids`: each row names 8 different experts. In each pack of 512 rows no expert is named by more than 320 rows, and in every draw some expert is named by exactly 320 rows of some pack. `lengths`: positions at or beyond a pack's length are padding whose keys no query reads; in every draw one pack is full.
All inputs are finite; a program needn't handle non-finite values.
Results may differ from a plain program's by a relative error of at most 0.03.
Values may be sent and summed in bfloat16 or wider, within the bound.
A program may use at most 384 MiB of HBM per device.

v0:
```python
import jax
import jax.numpy as jnp
from jax import lax
from jax.experimental import pallas as pl
from jax.experimental.pallas import tpu as pltpu
from jax.sharding import PartitionSpec as P

HEAD_SIZE = 128
TOP = 8
epsilon = 1e-06
f32 = jnp.float32
bf16 = jnp.bfloat16
MESH = pl.DeviceIdType.MESH


def rms_scale(values):
    return lax.rsqrt(jnp.mean(values * values, axis=-1, keepdims=True) + epsilon)


def rope_tables(rows):
    half_dim = HEAD_SIZE // 2
    frequency = jnp.power(f32(1000000.0), -(jnp.arange(half_dim, dtype=f32) * (2.0 / HEAD_SIZE)))
    angles = jnp.arange(rows, dtype=f32)[:, None] * frequency[None, :]
    return (jnp.cos(angles)[:, None, :], jnp.sin(angles)[:, None, :])


def rotate(values, cosine_table, sine_table):
    half_dim = values.shape[-1] // 2
    first_half = values[..., :half_dim]
    second_half = values[..., half_dim:]
    return jnp.concatenate(
        [
            first_half * cosine_table - second_half * sine_table,
            second_half * cosine_table + first_half * sine_table,
        ],
        axis=-1,
    )


def norm_back(grad_hidden, normed, scales, gains):
    grad_normed = grad_hidden * gains
    return scales * (grad_normed - normed * jnp.mean(grad_normed * normed, axis=-1, keepdims=True))


def flip(x, axis, bit):
    n = lax.axis_size(axis)
    return lax.ppermute(x, axis, [(i, i ^ bit) for i in range(n)])


def bits_of(n):
    return [1 << b for b in range(n.bit_length() - 1)]


def xor_gather(x, axis):
    pieces = [x]
    for bit in bits_of(lax.axis_size(axis)):
        pieces = pieces + [flip(p, axis, bit) for p in pieces]
    return pieces


def xor_scatter(parts, axis):
    for bit in reversed(bits_of(lax.axis_size(axis))):
        got = [flip(p, axis, bit) for p in parts[bit:]]
        parts = [
            (a.astype(f32) + r.astype(f32)).astype(a.dtype) for a, r in zip(parts[:bit], got)
        ]
    return parts[0]


def dp_scatter(blocks, axis="dp"):
    n = len(blocks)
    if n != 4:
        return xor_scatter(blocks, axis).astype(f32)
    h = blocks[0].shape[0] // 2
    add = lambda p, q: p.astype(f32) + q.astype(f32)
    done = []
    for rows, first, second in ((slice(0, h), 1, 2), (slice(h, 2 * h), 2, 1)):
        b = [x[rows] for x in blocks]
        got = flip(jnp.concatenate([b[first], b[3]], 0), axis, first)
        on = add(b[second], got[h:]).astype(bf16)
        done.append(add(b[0], got[:h]) + flip(on, axis, second).astype(f32))
    return jnp.concatenate(done, 0)


def all_pieces(x, axis, me):
    got = jnp.stack(xor_gather(x, axis), 0)
    return lane_order(got, 0, got.shape[0], me)


def dp_gather(x, axis="dp"):
    n = lax.axis_size(axis)
    if n != 4:
        return xor_gather(x, axis)
    h = x.shape[0] // 2
    a, b = x[:h], x[h:]
    a1, b2 = flip(a, axis, 1), flip(b, axis, 2)
    a2, b1 = flip(a, axis, 2), flip(b, axis, 1)
    a3, b3 = flip(a1, axis, 2), flip(b2, axis, 1)
    cat = lambda p, q: jnp.concatenate([p, q], 0)
    return [cat(a, b), cat(a1, b1), cat(a2, b2), cat(a3, b3)]


def lane_block(x, axis, n, me, k):
    axis = axis % x.ndim
    size = x.shape[axis] // n
    return lax.dynamic_slice_in_dim(x, (me ^ k) * size, size, axis)


def lane_order(x, axis, n, me):
    return jnp.concatenate([lane_block(x, axis, n, me, k) for k in range(n)], axis)


def block_scores(query_block, key_rot, length):
    query_pos = jnp.arange(query_block.shape[0], dtype=jnp.int32)
    key_pos = jnp.arange(key_rot.shape[0], dtype=jnp.int32)
    allowed = (key_pos[None, :] <= query_pos[:, None]) & (key_pos[None, :] < length)
    scores = jnp.einsum(
        "qkgd,skd->kgqs", query_block, key_rot, preferred_element_type=f32
    ) * HEAD_SIZE ** (-0.5)
    return jnp.where(allowed, scores, -1e30)


def core_rows(pieces, axis="expert"):
    n = lax.axis_size(axis)
    own = jnp.stack(pieces, 0)
    if n == 2:
        other = flip(own, axis, 1)
        first = lax.axis_index(axis) == 0
        both = jnp.stack([jnp.where(first, own, other), jnp.where(first, other, own)], 1)
    else:
        both = lax.all_gather(own, axis, axis=1, tiled=False)
    return both.reshape((-1,) + own.shape[2:])


def dotf(a, b, dims):
    return lax.dot_general(a, b, (dims, ((), ())), preferred_element_type=f32)


def local_plain(
    tokens,
    cotangent,
    route_ids,
    route_weight,
    lengths,
    attention_norm,
    query_weight,
    key_matrix,
    value_matrix,
    output_weight,
    query_norm,
    key_norm,
    experts_norm,
    gate_weight,
    up_weight,
    down_weight,
):
    n_dp = lax.axis_size("dp")
    n_ex = lax.axis_size("expert")
    me_dp = lax.axis_index("dp")
    me_ex = lax.axis_index("expert")
    rows, width = tokens.shape
    group, hidden, part = gate_weight.shape
    length = lengths[0]
    lane = lambda x, axis=-1: lane_order(x, axis, n_dp, me_dp)

    qkv_own = jnp.concatenate([query_weight, key_matrix, value_matrix], 1)
    qkv_pieces = dp_gather(qkv_own)
    wo_own, qkv_pieces = lax.optimization_barrier((output_weight, qkv_pieces))
    wo_pieces = dp_gather(wo_own)
    (gw, uw, dw), wo_pieces = lax.optimization_barrier(
        ((gate_weight, up_weight, down_weight), wo_pieces)
    )
    flat = group * hidden
    gate_up_own = jnp.concatenate([gw.reshape(flat, part), uw.reshape(flat, part)], 0)
    gate_up_pieces = dp_gather(gate_up_own)
    down_own, gate_up_pieces = lax.optimization_barrier((dw.reshape(flat, part), gate_up_pieces))
    down_pieces = dp_gather(down_own)

    na, nq = attention_norm.shape[0], query_norm.shape[0]
    gains = jnp.concatenate([attention_norm, experts_norm, query_norm, key_norm])
    gains = jnp.pad(gains, (0, -gains.size % 128)).reshape(-1, 128)
    gains = all_pieces(all_pieces(gains, "expert", me_ex), "dp", me_dp)
    gains = gains.reshape(n_dp, n_ex, -1).astype(f32)
    gain_attention = lane(gains[:, :, :na].reshape(-1))
    gain_experts = lane(gains[:, :, na : 2 * na].reshape(-1))
    gain_query = gains[:, :, 2 * na : 2 * na + nq].reshape(-1)
    gain_key = gains[:, :, 2 * na + nq : 2 * na + 2 * nq].reshape(-1)

    experts = jnp.arange(group * n_ex, dtype=jnp.int32)
    table = jnp.zeros((rows, group * n_ex), f32)
    for c in range(route_ids.shape[1]):
        table = table + jnp.where(
            route_ids[:, c, None] == experts[None, :], route_weight[:, c, None], 0.0
        )
    table = jnp.concatenate(xor_gather(table, "expert"), 0)
    mine = lax.dynamic_slice_in_dim(table, me_ex * group, group, 1)
    unit_expert = jnp.arange(flat, dtype=jnp.int32) // hidden
    route_scale = jnp.zeros((table.shape[0], flat), f32)
    for j in range(group):
        route_scale = route_scale + jnp.where(unit_expert[None, :] == j, mine[:, j, None], 0.0)

    cosine_table, sine_table = rope_tables(rows)
    inputs = lane(tokens.astype(f32))
    scale_one = rms_scale(inputs)
    normed_one = inputs * scale_one
    first_hidden = (normed_one * gain_attention).astype(bf16)
    upstream_low = lane(cotangent)
    upstream_all = jnp.concatenate(xor_gather(upstream_low, "expert"), 0)

    full_qkv = core_rows(qkv_pieces)
    qkv = jnp.dot(first_hidden, full_qkv, preferred_element_type=f32)
    q_cols, k_cols = query_weight.shape[1], key_matrix.shape[1]
    heads_query, heads_key = q_cols // HEAD_SIZE, k_cols // HEAD_SIZE
    per_group = heads_query // heads_key
    query_raw = qkv[:, :q_cols].reshape(rows, heads_query, HEAD_SIZE)
    key_raw = qkv[:, q_cols : q_cols + k_cols].reshape(rows, heads_key, HEAD_SIZE)
    value_low = qkv[:, q_cols + k_cols :].astype(bf16).reshape(rows, heads_key, HEAD_SIZE)
    scale_query = rms_scale(query_raw)
    normed_query = query_raw * scale_query
    rotated_query = (
        rotate(normed_query * gain_query, cosine_table, sine_table)
        .astype(bf16)
        .reshape(rows, heads_key, per_group, HEAD_SIZE)
    )
    scale_key = rms_scale(key_raw)
    normed_key = key_raw * scale_key
    key_rot = rotate(normed_key * gain_key, cosine_table, sine_table).astype(bf16)
    scores = block_scores(rotated_query, key_rot, length)
    row_peak = jnp.max(scores, axis=-1, keepdims=True)
    shifted = jnp.exp(scores - row_peak)
    totals = jnp.sum(shifted, axis=-1, keepdims=True)
    probs = shifted / totals
    prob_low = probs.astype(bf16)
    attended_low = (
        jnp.einsum("kgqs,skd->qkgd", prob_low, value_low, preferred_element_type=f32)
        .reshape(rows, q_cols)
        .astype(bf16)
    )
    full_output = core_rows(wo_pieces)
    projected = dotf(attended_low, full_output, ((1,), (1,)))
    mixed_rows = inputs + lax.psum(projected.astype(bf16), "tensor").astype(f32)
    scale_two = rms_scale(mixed_rows)
    normed_two = mixed_rows * scale_two
    hidden_two = (normed_two * gain_experts).astype(bf16)

    hidden_all = jnp.concatenate(xor_gather(hidden_two, "expert"), 0)
    gate_up_full = jnp.concatenate(gate_up_pieces, 1)
    down_full = jnp.concatenate(down_pieces, 1)
    gate_up = dotf(hidden_all, gate_up_full, ((1,), (1,)))
    gate_value, up_value = gate_up[:, :flat], gate_up[:, flat:]
    grad_act = lax.optimization_barrier(dotf(upstream_all, down_full, ((1,), (1,)))) * route_scale
    sigmoid_gate = jax.nn.sigmoid(gate_value)
    scaled_act = (gate_value * sigmoid_gate * up_value * route_scale).astype(bf16)
    grad_up_low = (grad_act * gate_value * sigmoid_gate).astype(bf16)
    grad_gate_low = (
        grad_act * up_value * sigmoid_gate * (1.0 + gate_value * (1.0 - sigmoid_gate))
    ).astype(bf16)
    grad_gate_up = jnp.concatenate([grad_gate_low, grad_up_low], 1)
    grad_rows = jnp.dot(grad_gate_up, gate_up_full, preferred_element_type=f32).astype(bf16)
    grad_hidden_two = xor_scatter(jnp.split(grad_rows, n_ex, 0), "expert")
    grad_hidden_two = lax.psum(grad_hidden_two, "tensor")

    expert_out = jnp.dot(scaled_act, down_full, preferred_element_type=f32).astype(bf16)
    combined = xor_scatter(jnp.split(expert_out, n_ex, 0), "expert")
    def expert_grad(low, acts):
        return dotf(low, acts, ((0,), (0,))).astype(bf16)

    grads = [
        expert_grad(scaled_act, upstream_all),
        expert_grad(grad_gate_low, hidden_all),
        expert_grad(grad_up_low, hidden_all),
    ]
    grad_hidden_two, grads = lax.optimization_barrier((grad_hidden_two, grads))
    down_shard, gate_shard, up_shard = (
        dp_scatter(jnp.split(g, n_dp, 1)).reshape(group, hidden, part) for g in grads
    )
    combined, grad_hidden_two = lax.optimization_barrier((combined, grad_hidden_two))
    combined = lax.psum(combined, "tensor")
    output = lane((mixed_rows + combined.astype(f32)).astype(bf16))
    grad_hidden_two = grad_hidden_two.astype(f32)

    def attention_scatter(grad):
        grad = grad.reshape(n_dp, n_ex, width // (n_dp * n_ex), grad.shape[1])
        if n_ex == 2:
            away = lax.dynamic_index_in_dim(grad, 1 - me_ex, 1, keepdims=False)
            own = lax.dynamic_index_in_dim(grad, me_ex, 1, keepdims=False)
            grad = (own.astype(f32) + flip(away, "expert", 1).astype(f32)).astype(bf16)
        else:
            grad = lax.psum_scatter(grad, "expert", scatter_dimension=1, tiled=False)
        return dp_scatter(list(grad))

    upstream = upstream_low.astype(f32)
    experts_gain_grad = jnp.sum(grad_hidden_two * normed_two, axis=0)
    grad_mixed = upstream + norm_back(grad_hidden_two, normed_two, scale_two, gain_experts)
    grad_proj_low = grad_mixed.astype(bf16)
    grad_att_low = (
        jnp.dot(grad_proj_low, full_output, preferred_element_type=f32)
        .astype(bf16)
        .reshape(rows, heads_key, per_group, HEAD_SIZE)
    )
    output_grad = dotf(grad_proj_low, attended_low, ((0,), (0,))).astype(bf16)
    output_shard = attention_scatter(output_grad)
    grad_probs = jnp.einsum("qkgd,skd->kgqs", grad_att_low, value_low, preferred_element_type=f32)
    row_dot = jnp.sum(probs * grad_probs, axis=-1, keepdims=True)
    grad_scores = (probs * (grad_probs - row_dot)).astype(bf16)
    grad_value = jnp.einsum("kgqs,qkgd->skd", prob_low, grad_att_low, preferred_element_type=f32)
    grad_qrot = jnp.einsum(
        "kgqs,skd->qkgd", grad_scores, key_rot, preferred_element_type=f32
    ) * HEAD_SIZE ** (-0.5)
    grad_krot = jnp.einsum(
        "kgqs,qkgd->skd", grad_scores, rotated_query, preferred_element_type=f32
    ) * HEAD_SIZE ** (-0.5)
    grad_qrot = grad_qrot.reshape(rows, heads_query, HEAD_SIZE)
    grad_query_normed = rotate(grad_qrot, cosine_table, -sine_table)
    query_gain_grad = jnp.sum(grad_query_normed * normed_query, axis=(0, 1))
    grad_query_low = (
        norm_back(grad_query_normed, normed_query, scale_query, gain_query)
        .astype(bf16)
        .reshape(rows, q_cols)
    )
    grad_key_normed = rotate(grad_krot, cosine_table, -sine_table)
    key_gain_grad = jnp.sum(grad_key_normed * normed_key, axis=(0, 1))
    grad_key_low = (
        norm_back(grad_key_normed, normed_key, scale_key, gain_key).astype(bf16).reshape(rows, k_cols)
    )
    grad_value_low = grad_value.astype(bf16).reshape(rows, k_cols)
    grad_qkv_low = jnp.concatenate([grad_query_low, grad_key_low, grad_value_low], 1)
    grad_hidden_one = dotf(grad_qkv_low, full_qkv, ((1,), (1,)))
    head_gain_grads = jnp.stack([query_gain_grad, key_gain_grad]).astype(bf16)
    grad_hidden_one, head_gain_grads, _ = lax.optimization_barrier(
        (grad_hidden_one.astype(bf16), head_gain_grads, combined)
    )
    grad_hidden_one, head_gain_grads = lax.psum((grad_hidden_one, head_gain_grads), "tensor")
    grad_hidden_one = grad_hidden_one.astype(f32)
    qkv_grad = dotf(first_hidden, grad_qkv_low, ((0,), (0,))).astype(bf16)
    qkv_shard = attention_scatter(qkv_grad)
    attention_gain_grad = jnp.sum(grad_hidden_one * normed_one, axis=0)
    tokens_grad = grad_mixed + norm_back(grad_hidden_one, normed_one, scale_one, gain_attention)
    tokens_grad = lane(tokens_grad)

    blocks = lambda v: v.reshape(n_dp, n_ex, -1)
    gain_grads = jnp.concatenate(
        [
            blocks(attention_gain_grad),
            blocks(experts_gain_grad),
            lane(blocks(head_gain_grads[0].astype(f32)), 0),
            lane(blocks(head_gain_grads[1].astype(f32)), 0),
        ],
        2,
    )
    gain_grads = lane_order(gain_grads, 1, n_ex, me_ex)
    gain_grads = jnp.pad(gain_grads, ((0, 0), (0, 0), (0, -gain_grads.shape[2] % 128)))
    gain_grads = gain_grads.reshape(n_dp, n_ex, -1, 128)
    gain_grads = xor_scatter([gain_grads[:, k] for k in range(n_ex)], "expert")
    gain_grads = xor_scatter([gain_grads[k] for k in range(n_dp)], "dp").reshape(-1)
    take = lambda start, size: gain_grads[start : start + size]
    return (
        output,
        tokens_grad,
        take(0, na),
        qkv_shard[:, :q_cols],
        qkv_shard[:, q_cols : q_cols + k_cols],
        qkv_shard[:, q_cols + k_cols :],
        output_shard,
        take(2 * na, nq),
        take(2 * na + nq, nq),
        take(na, na),
        gate_shard,
        up_shard,
        down_shard,
    )


CHUNKS = 16


def line_roles(axis):
    p = lax.axis_index(axis)
    return p + 1 - 2 * (p % 2), 3 - p, (p + 1) // 2 == 1


def over(n, f, start=0):
    lax.fori_loop(start, n, lambda c, t: (f(c), t)[1], 0)


def line_sum_steps(x_ref, in_buf, mid_buf, part, out_ref, sems, axis, finish, lag=2):
    a_send, a_recv, b_send, b_recv, c_send, c_recv = sems
    side, mid, inner = line_roles(axis)
    step = x_ref.shape[0] // CHUNKS

    def rows(c):
        return pl.ds(pl.multiple_of(c * step, step), step)

    def copy(src, dst, c, send, recv, to):
        return pltpu.make_async_remote_copy(
            src.at[rows(c)], dst.at[rows(c)], send.at[c], recv.at[c], device_id={axis: to}, device_id_type=MESH
        )

    to_inner = lambda c: copy(x_ref, in_buf, c, a_send, a_recv, side)
    to_middle = lambda c: copy(part, mid_buf, c, b_send, b_recv, mid)
    to_outer = lambda c: copy(out_ref, out_ref, c, c_send, c_recv, side)

    @pl.when(jnp.logical_not(inner))
    def _():
        over(CHUNKS, lambda c: to_inner(c).start())

        def done(c):
            to_outer(c).wait_recv()
            finish(rows(c), c)
            to_inner(c).wait_send()

        over(CHUNKS, done)

    @pl.when(inner)
    def _():
        def first(c):
            to_inner(c).wait_recv()
            r = rows(c)
            part[r] = (x_ref[r].astype(f32) + in_buf[r].astype(f32)).astype(bf16)
            to_middle(c).start()

        def second(c):
            to_middle(c).wait_recv()
            r = rows(c)
            out_ref[r] = (part[r].astype(f32) + mid_buf[r].astype(f32)).astype(bf16)
            to_outer(c).start()
            finish(r, c)

        over(lag, first)
        over(CHUNKS - lag, lambda c: (first(c + lag), second(c))[0])
        over(CHUNKS, second, CHUNKS - lag)

        def done(c):
            to_middle(c).wait_send()
            to_outer(c).wait_send()

        over(CHUNKS, done)


def line_sems():
    return [pltpu.SemaphoreType.DMA((CHUNKS,))] * 6


def plane_partners():
    d, c = lax.axis_index("dp"), lax.axis_index("expert")
    ds = {0: d, 1: d + 1 - 2 * (d % 2), 2: d + 2 - 4 * (d // 2), 3: 3 - d}
    cs = {0: c, 1: 1 - c}
    return {(kd, kc): {"dp": ds[kd], "expert": cs[kc]} for kd in ds for kc in cs}


def remote(src, dst, send, recv, to):
    return pltpu.make_async_remote_copy(src, dst, send, recv, device_id=to, device_id_type=MESH)


def nt(a, b):
    return lax.dot_general(a, b, (((1,), (1,)), ((), ())), preferred_element_type=f32)


def nn(a, b):
    return lax.dot_general(a, b, (((1,), (0,)), ((), ())), preferred_element_type=f32)


def tn(a, b):
    return lax.dot_general(a, b, (((0,), (0,)), ((), ())), preferred_element_type=f32)


def forward_kernel(
    tokens, qkv_own, wo_own, gate_own, up_own, down_own, gains_own, cos, sin, key_ok,
    x2, h2, att, qrot, krot, value, raw, probs, gains, gate, up, down, qkv_out, wo_out,
    qkv, wo, h1, proj, in_buf, mid_buf, part, summed, gain_rows,
    w_send, w_recv, core_send, core_recv, g_send, g_recv, h_send, h_recv, own_sem, out_sem, *line,
):
    c = lax.axis_index("expert")
    to = plane_partners()
    side, mid, inner = line_roles("tensor")
    barrier = pltpu.get_barrier_semaphore()
    others = [k for k in to if k != (0, 0)]
    for k in others:
        pl.semaphore_signal(barrier, inc=1, device_id=to[k], device_id_type=MESH)
    pl.semaphore_signal(barrier, inc=1, device_id={"tensor": side}, device_id_type=MESH)

    @pl.when(inner)
    def _():
        pl.semaphore_signal(barrier, inc=1, device_id={"tensor": mid}, device_id_type=MESH)
        pl.semaphore_wait(barrier, len(others) + 2)

    @pl.when(jnp.logical_not(inner))
    def _():
        pl.semaphore_wait(barrier, len(others) + 1)

    rows, width = tokens.shape
    piece = qkv_own.shape[0]
    half = piece // 2
    tall = gate_own.shape[0] // 2
    wide = gate_own.shape[1]

    def small_slot(full):
        return lambda k, h: full.at[pl.ds(pl.multiple_of((k * 2 + c) * piece + h * half, half), half)]

    def big_slot(full):
        return lambda k, h: full.at[pl.ds(h * tall, tall), pl.ds(k * wide, wide)]

    mats = [
        (lambda h: qkv_own.at[pl.ds(h * half, half)], small_slot(qkv)),
        (lambda h: wo_own.at[pl.ds(h * half, half)], small_slot(wo)),
    ] + [
        (lambda h, own=own: own.at[pl.ds(h * tall, tall)], big_slot(full))
        for own, full in ((gate_own, gate), (up_own, up), (down_own, down))
    ]

    def move(m, i):
        own, slot = mats[m]
        src, dst, way = (
            (own(0), slot(1, 0), 1), (own(1), slot(2, 1), 2), (own(0), slot(2, 0), 2), (own(1), slot(1, 1), 1),
            (slot(1, 0), slot(3, 0), 2), (slot(2, 1), slot(3, 1), 1),
        )[i]
        return remote(src, dst, w_send.at[m, i], w_recv.at[m, i], to[way, 0])

    def begin(m):
        for i in range(4):
            move(m, i).start()

    def pass_on(m):
        for i in (0, 1):
            move(m, i).wait_recv()
            move(m, 4 + i).start()

    def arrived(m):
        for i in (2, 3, 4, 5):
            move(m, i).wait_recv()

    def core_move(m, k):
        full = (qkv, wo)[m]
        block = full.at[pl.ds(pl.multiple_of((k * 2 + c) * piece, piece), piece)]
        return remote(block, block, core_send.at[m, k], core_recv.at[m, k], to[0, 1])

    def gain_move(j):
        kd, kc = others[j]
        return remote(gains_own, gains.at[kd, c], g_send.at[j], g_recv.at[j], to[kd, kc])

    own_copies = [
        pltpu.make_async_copy(qkv_own, qkv.at[pl.ds(pl.multiple_of(c * piece, piece), piece)], own_sem.at[0]),
        pltpu.make_async_copy(wo_own, wo.at[pl.ds(pl.multiple_of(c * piece, piece), piece)], own_sem.at[1]),
    ] + [
        pltpu.make_async_copy(own, full.at[:, pl.ds(0, wide)], own_sem.at[2 + i])
        for i, (own, full) in enumerate(((gate_own, gate), (up_own, up), (down_own, down)))
    ]

    begin(0)
    for j in range(len(others)):
        gain_move(j).start()
    own_copies[0].start()
    own_copies[1].start()
    gains[pl.ds(0, 1), pl.ds(c, 1)] = gains_own[...].reshape(1, 1, 8, 128)
    own_copies[0].wait()
    core_move(0, 0).start()
    own_copies[1].wait()
    core_move(1, 0).start()
    for j in range(len(others)):
        gain_move(j).wait_recv()
    for kd in range(4):
        for kc in range(2):
            g = gains[kd, kc]
            for j in range(2):
                col = (kd * 2 + kc) * 256 + j * 128
                gain_rows[0:1, col : col + 128] = g[j : j + 1]
                gain_rows[1:2, col : col + 128] = g[2 + j : 3 + j]
    heads = jnp.sum(gains[...].reshape(8, 8, 128), axis=0)
    gain_query, gain_key = heads[4:5], heads[5:6]

    def hidden_one(i):
        r = pl.ds(pl.multiple_of(i * 64, 64), 64)
        x = tokens[r].astype(f32)
        scale = lax.rsqrt(jnp.mean(x * x, axis=-1, keepdims=True) + epsilon)
        h1[r] = (x * scale * gain_rows[0:1]).astype(bf16)

    over(rows // 64, hidden_one)

    pass_on(0)
    begin(1)
    for k, waits in ((1, (3,)), (2, (2,)), (3, (4, 5))):
        for i in waits:
            move(0, i).wait_recv()
        core_move(0, k).start()
    pass_on(1)
    for m in (2, 3, 4):
        begin(m)
        own_copies[m].start()
    for k in range(4):
        core_move(0, k).wait_recv()
    save_qkv = pltpu.make_async_copy(qkv, qkv_out, out_sem.at[0])
    save_qkv.start()

    def project(j):
        col = pl.ds(pl.multiple_of(j * 256, 256), 256)
        raw[:, col] = nn(h1[...], qkv[:, col])

    over(qkv.shape[1] // 256, project)
    q_cols = att.shape[1]

    def spin(u):
        return u * cos[...] + pltpu.roll(u, 64, 1) * sin[...]

    def unit(u):
        return u * lax.rsqrt(jnp.mean(u * u, axis=-1, keepdims=True) + epsilon)

    krot[...] = spin(unit(raw[:, pl.ds(q_cols, 128)]) * gain_key).astype(bf16)
    value[...] = raw[:, pl.ds(q_cols + 128, 128)].astype(bf16)
    block = rows // 2

    def head(h):
        col = pl.ds(pl.multiple_of(h * 128, 128), 128)
        qrot[:, col] = spin(unit(raw[:, col]) * gain_query).astype(bf16)
        for i in range(2):
            r, n = slice(i * block, (i + 1) * block), (i + 1) * block
            s = nt(qrot[r, col], krot[0:n]) * 128 ** (-0.5)
            row = lax.broadcasted_iota(jnp.int32, (block, n), 0) + i * block
            key = lax.broadcasted_iota(jnp.int32, (block, n), 1)
            s = jnp.where((key <= row) & (key_ok[:, 0:n] > 0), s, -1e30)
            e = jnp.exp(s - jnp.max(s, axis=-1, keepdims=True))
            p = (e / jnp.sum(e, axis=-1, keepdims=True)).astype(bf16)
            probs[h, r, 0:n] = p
            att[r, col] = nn(p, value[0:n]).astype(bf16)
        probs[h, 0:block, block:] = jnp.zeros((block, block), bf16)

    over(q_cols // 128, head)

    for k, waits in ((1, (3,)), (2, (2,)), (3, (4, 5))):
        for i in waits:
            move(1, i).wait_recv()
        core_move(1, k).start()
    for k in range(4):
        core_move(1, k).wait_recv()
    save_wo = pltpu.make_async_copy(wo, wo_out, out_sem.at[1])
    save_wo.start()

    def out_project(j):
        r = pl.ds(pl.multiple_of(j * 256, 256), 256)
        proj[:, r] = nt(att[...], wo[r]).astype(bf16)

    over(width // 256, out_project)
    pass_on(2)

    def give(i):
        n = rows // CHUNKS
        src = h2.at[pl.ds(pl.multiple_of(i * n, n), n)]
        dst = h2.at[pl.ds(pl.multiple_of(rows + i * n, n), n)]
        return remote(src, dst, h_send.at[i], h_recv.at[i], to[0, 1])

    def finish(r, i):
        mixed = tokens[r].astype(f32) + summed[r].astype(f32)
        x2[r] = mixed
        scale = lax.rsqrt(jnp.mean(mixed * mixed, axis=-1, keepdims=True) + epsilon)
        h2[r] = (mixed * scale * gain_rows[1:2]).astype(bf16)
        give(i).start()

    line_sum_steps(proj, in_buf, mid_buf, part, summed, line, "tensor", finish)
    pass_on(3)
    pass_on(4)
    over(CHUNKS, lambda i: give(i).wait())
    for m in (2, 3, 4):
        arrived(m)
        own_copies[m].wait()
    save_qkv.wait()
    save_wo.wait()
    for m in range(5):
        for i in range(6):
            move(m, i).wait_send()
    for m in range(2):
        for k in range(4):
            core_move(m, k).wait_send()
    for j in range(len(others)):
        gain_move(j).wait_send()


def forward_call(tokens, qkv_own, wo_own, gate_own, up_own, down_own, gains_own, cos, sin, key_ok):
    rows, width = tokens.shape
    qkv_cols, q_cols = qkv_own.shape[1], wo_own.shape[1]
    tall = gate_own.shape[0]
    vmem, anyspace = pl.BlockSpec(memory_space=pltpu.VMEM), pl.BlockSpec(memory_space=pl.ANY)
    shape = jax.ShapeDtypeStruct
    outs = [
        (shape((rows, width), f32), vmem),
        (shape((2 * rows, width), bf16), vmem),
        (shape((rows, q_cols), bf16), vmem),
        (shape((rows, q_cols), bf16), vmem),
        (shape((rows, 128), bf16), vmem),
        (shape((rows, 128), bf16), vmem),
        (shape((rows, qkv_cols), f32), vmem),
        (shape((q_cols // 128, rows, rows), bf16), vmem),
        (shape((4, 2, 8, 128), f32), vmem),
        (shape((tall, width), bf16), anyspace),
        (shape((tall, width), bf16), anyspace),
        (shape((tall, width), bf16), anyspace),
        (shape((width, qkv_cols), bf16), anyspace),
        (shape((width, q_cols), bf16), anyspace),
    ]
    dma = pltpu.SemaphoreType.DMA
    big = pltpu.VMEM((rows, width), bf16)
    return pl.pallas_call(
        forward_kernel,
        out_shape=[o[0] for o in outs],
        in_specs=[vmem] + [anyspace] * 5 + [vmem] * 4,
        out_specs=[o[1] for o in outs],
        scratch_shapes=[
            pltpu.VMEM((width, qkv_cols), bf16),
            pltpu.VMEM((width, q_cols), bf16),
            big, big, big, big, big, big,
            pltpu.VMEM((2, width), f32),
            dma((5, 6)), dma((5, 6)), dma((2, 4)), dma((2, 4)), dma((7,)), dma((7,)),
            dma((CHUNKS,)), dma((CHUNKS,)), dma((5,)), dma((2,)),
        ] + line_sems(),
        compiler_params=pltpu.CompilerParams(
            collective_id=1, has_side_effects=True, vmem_limit_bytes=60 * 2**20
        ),
        cost_estimate=pl.CostEstimate(flops=8 * 10**9, bytes_accessed=60 * 10**6, transcendentals=2 * 10**6),
        name="forward_to_experts",
    )(tokens, qkv_own, wo_own, gate_own, up_own, down_own, gains_own, cos, sin, key_ok)


def local_fast(
    tokens,
    cotangent,
    route_ids,
    route_weight,
    lengths,
    attention_norm,
    query_weight,
    key_matrix,
    value_matrix,
    output_weight,
    query_norm,
    key_norm,
    experts_norm,
    gate_weight,
    up_weight,
    down_weight,
):
    n_dp = lax.axis_size("dp")
    n_ex = lax.axis_size("expert")
    me_dp = lax.axis_index("dp")
    me_ex = lax.axis_index("expert")
    rows, width = tokens.shape
    group, hidden, part = gate_weight.shape
    length = lengths[0]
    lane = lambda x, axis=-1: lane_order(x, axis, n_dp, me_dp)

    flat = group * hidden
    na, nq = attention_norm.shape[0], query_norm.shape[0]
    q_cols, k_cols = query_weight.shape[1], key_matrix.shape[1]
    heads_query, heads_key = q_cols // HEAD_SIZE, k_cols // HEAD_SIZE
    per_group = heads_query // heads_key
    own_place = (me_dp * n_ex + me_ex) * nq
    placed = lambda v: lax.dynamic_update_slice(jnp.zeros((128,), f32), v.astype(f32), (own_place,))
    gains_own = jnp.concatenate(
        [
            attention_norm.astype(f32).reshape(-1, 128),
            experts_norm.astype(f32).reshape(-1, 128),
            placed(query_norm)[None],
            placed(key_norm)[None],
            jnp.zeros((2, 128), f32),
        ],
        0,
    )
    cosine_table, sine_table = rope_tables(rows)
    cos2 = jnp.concatenate([cosine_table[:, 0], cosine_table[:, 0]], 1)
    sin2 = jnp.concatenate([-sine_table[:, 0], sine_table[:, 0]], 1)
    key_ok = (jnp.arange(rows, dtype=jnp.int32) < length).astype(f32)[None]
    inputs_low = lane(tokens)
    inputs = inputs_low.astype(f32)
    (
        mixed_rows, hidden_all, attended_low, rotated_query, key_rot, value_low, raw, prob_low,
        gains, gate_full, up_full, down_full, full_qkv, full_output,
    ) = forward_call(
        inputs_low,
        jnp.concatenate([query_weight, key_matrix, value_matrix], 1),
        output_weight,
        gate_weight.reshape(flat, part),
        up_weight.reshape(flat, part),
        down_weight.reshape(flat, part),
        gains_own,
        cos2,
        sin2,
        key_ok,
    )
    gain_attention = gains[:, :, 0:2].reshape(-1)
    gain_experts = gains[:, :, 2:4].reshape(-1)
    gain_query = jnp.sum(gains[:, :, 4], (0, 1))
    gain_key = jnp.sum(gains[:, :, 5], (0, 1))

    experts = jnp.arange(group * n_ex, dtype=jnp.int32)
    table = jnp.zeros((rows, group * n_ex), f32)
    for c in range(route_ids.shape[1]):
        table = table + jnp.where(
            route_ids[:, c, None] == experts[None, :], route_weight[:, c, None], 0.0
        )
    table = jnp.concatenate(xor_gather(table, "expert"), 0)
    mine = lax.dynamic_slice_in_dim(table, me_ex * group, group, 1)
    unit_expert = jnp.arange(flat, dtype=jnp.int32) // hidden
    route_scale = jnp.zeros((table.shape[0], flat), f32)
    for j in range(group):
        route_scale = route_scale + jnp.where(unit_expert[None, :] == j, mine[:, j, None], 0.0)

    scale_one = rms_scale(inputs)
    normed_one = inputs * scale_one
    first_hidden = (normed_one * gain_attention).astype(bf16)
    upstream_low = lane(cotangent)
    upstream_all = jnp.concatenate(xor_gather(upstream_low, "expert"), 0)

    query_raw = raw[:, :q_cols].reshape(rows, heads_query, HEAD_SIZE)
    key_raw = raw[:, q_cols : q_cols + k_cols].reshape(rows, heads_key, HEAD_SIZE)
    value_low = value_low.reshape(rows, heads_key, HEAD_SIZE)
    rotated_query = rotated_query.reshape(rows, heads_key, per_group, HEAD_SIZE)
    key_rot = key_rot.reshape(rows, heads_key, HEAD_SIZE)
    prob_low = prob_low[None]
    probs = prob_low.astype(f32)
    scale_query = rms_scale(query_raw)
    normed_query = query_raw * scale_query
    scale_key = rms_scale(key_raw)
    normed_key = key_raw * scale_key
    scale_two = rms_scale(mixed_rows)
    normed_two = mixed_rows * scale_two

    gate_value = dotf(hidden_all, gate_full, ((1,), (1,)))
    up_value = dotf(hidden_all, up_full, ((1,), (1,)))
    grad_act = lax.optimization_barrier(dotf(upstream_all, down_full, ((1,), (1,)))) * route_scale
    sigmoid_gate = jax.nn.sigmoid(gate_value)
    scaled_act = (gate_value * sigmoid_gate * up_value * route_scale).astype(bf16)
    grad_up_low = (grad_act * gate_value * sigmoid_gate).astype(bf16)
    grad_gate_low = (
        grad_act * up_value * sigmoid_gate * (1.0 + gate_value * (1.0 - sigmoid_gate))
    ).astype(bf16)
    grad_rows = jnp.dot(grad_gate_low, gate_full, preferred_element_type=f32)
    grad_rows = (grad_rows + jnp.dot(grad_up_low, up_full, preferred_element_type=f32)).astype(bf16)
    grad_hidden_two = xor_scatter(jnp.split(grad_rows, n_ex, 0), "expert")
    grad_hidden_two = lax.psum(grad_hidden_two, "tensor")

    expert_out = jnp.dot(scaled_act, down_full, preferred_element_type=f32).astype(bf16)
    combined = xor_scatter(jnp.split(expert_out, n_ex, 0), "expert")
    def expert_grad(low, acts):
        return dotf(low, acts, ((0,), (0,))).astype(bf16)

    grads = [
        expert_grad(scaled_act, upstream_all),
        expert_grad(grad_gate_low, hidden_all),
        expert_grad(grad_up_low, hidden_all),
    ]
    grad_hidden_two, grads = lax.optimization_barrier((grad_hidden_two, grads))
    down_shard, gate_shard, up_shard = (
        dp_scatter(jnp.split(g, n_dp, 1)).reshape(group, hidden, part) for g in grads
    )
    combined, grad_hidden_two = lax.optimization_barrier((combined, grad_hidden_two))
    combined = lax.psum(combined, "tensor")
    output = lane((mixed_rows + combined.astype(f32)).astype(bf16))
    grad_hidden_two = grad_hidden_two.astype(f32)

    def attention_scatter(grad):
        grad = grad.reshape(n_dp, n_ex, width // (n_dp * n_ex), grad.shape[1])
        if n_ex == 2:
            away = lax.dynamic_index_in_dim(grad, 1 - me_ex, 1, keepdims=False)
            own = lax.dynamic_index_in_dim(grad, me_ex, 1, keepdims=False)
            grad = (own.astype(f32) + flip(away, "expert", 1).astype(f32)).astype(bf16)
        else:
            grad = lax.psum_scatter(grad, "expert", scatter_dimension=1, tiled=False)
        return dp_scatter(list(grad))

    upstream = upstream_low.astype(f32)
    experts_gain_grad = jnp.sum(grad_hidden_two * normed_two, axis=0)
    grad_mixed = upstream + norm_back(grad_hidden_two, normed_two, scale_two, gain_experts)
    grad_proj_low = grad_mixed.astype(bf16)
    grad_att_low = (
        jnp.dot(grad_proj_low, full_output, preferred_element_type=f32)
        .astype(bf16)
        .reshape(rows, heads_key, per_group, HEAD_SIZE)
    )
    output_grad = dotf(grad_proj_low, attended_low, ((0,), (0,))).astype(bf16)
    output_shard = attention_scatter(output_grad)
    grad_probs = jnp.einsum("qkgd,skd->kgqs", grad_att_low, value_low, preferred_element_type=f32)
    row_dot = jnp.sum(probs * grad_probs, axis=-1, keepdims=True)
    grad_scores = (probs * (grad_probs - row_dot)).astype(bf16)
    grad_value = jnp.einsum("kgqs,qkgd->skd", prob_low, grad_att_low, preferred_element_type=f32)
    grad_qrot = jnp.einsum(
        "kgqs,skd->qkgd", grad_scores, key_rot, preferred_element_type=f32
    ) * HEAD_SIZE ** (-0.5)
    grad_krot = jnp.einsum(
        "kgqs,qkgd->skd", grad_scores, rotated_query, preferred_element_type=f32
    ) * HEAD_SIZE ** (-0.5)
    grad_qrot = grad_qrot.reshape(rows, heads_query, HEAD_SIZE)
    grad_query_normed = rotate(grad_qrot, cosine_table, -sine_table)
    query_gain_grad = jnp.sum(grad_query_normed * normed_query, axis=(0, 1))
    grad_query_low = (
        norm_back(grad_query_normed, normed_query, scale_query, gain_query)
        .astype(bf16)
        .reshape(rows, q_cols)
    )
    grad_key_normed = rotate(grad_krot, cosine_table, -sine_table)
    key_gain_grad = jnp.sum(grad_key_normed * normed_key, axis=(0, 1))
    grad_key_low = (
        norm_back(grad_key_normed, normed_key, scale_key, gain_key).astype(bf16).reshape(rows, k_cols)
    )
    grad_value_low = grad_value.astype(bf16).reshape(rows, k_cols)
    grad_qkv_low = jnp.concatenate([grad_query_low, grad_key_low, grad_value_low], 1)
    grad_hidden_one = dotf(grad_qkv_low, full_qkv, ((1,), (1,)))
    head_gain_grads = jnp.stack([query_gain_grad, key_gain_grad]).astype(bf16)
    grad_hidden_one, head_gain_grads, _ = lax.optimization_barrier(
        (grad_hidden_one.astype(bf16), head_gain_grads, combined)
    )
    grad_hidden_one, head_gain_grads = lax.psum((grad_hidden_one, head_gain_grads), "tensor")
    grad_hidden_one = grad_hidden_one.astype(f32)
    qkv_grad = dotf(first_hidden, grad_qkv_low, ((0,), (0,))).astype(bf16)
    qkv_shard = attention_scatter(qkv_grad)
    attention_gain_grad = jnp.sum(grad_hidden_one * normed_one, axis=0)
    tokens_grad = grad_mixed + norm_back(grad_hidden_one, normed_one, scale_one, gain_attention)
    tokens_grad = lane(tokens_grad)

    blocks = lambda v: v.reshape(n_dp, n_ex, -1)
    gain_grads = jnp.concatenate(
        [
            blocks(attention_gain_grad),
            blocks(experts_gain_grad),
            lane(blocks(head_gain_grads[0].astype(f32)), 0),
            lane(blocks(head_gain_grads[1].astype(f32)), 0),
        ],
        2,
    )
    gain_grads = lane_order(gain_grads, 1, n_ex, me_ex)
    gain_grads = jnp.pad(gain_grads, ((0, 0), (0, 0), (0, -gain_grads.shape[2] % 128)))
    gain_grads = gain_grads.reshape(n_dp, n_ex, -1, 128)
    gain_grads = xor_scatter([gain_grads[:, k] for k in range(n_ex)], "expert")
    gain_grads = xor_scatter([gain_grads[k] for k in range(n_dp)], "dp").reshape(-1)
    take = lambda start, size: gain_grads[start : start + size]
    return (
        output,
        tokens_grad,
        take(0, na),
        qkv_shard[:, :q_cols],
        qkv_shard[:, q_cols : q_cols + k_cols],
        qkv_shard[:, q_cols + k_cols :],
        output_shard,
        take(2 * na, nq),
        take(2 * na + nq, nq),
        take(na, na),
        gate_shard,
        up_shard,
        down_shard,
    )


def local(*args):
    sizes = [lax.axis_size(a) for a in ("dp", "expert", "tensor")]
    return local_fast(*args) if sizes == [4, 2, 4] else local_plain(*args)


def solution(mesh):
    both = ("dp", "expert")
    rows2, rows1, mats = P(both, None), P(both), P(both, "tensor")
    experts = P("expert", "tensor", "dp")
    return jax.shard_map(
        local,
        mesh=mesh,
        in_specs=(rows2, rows2, rows2, rows2, rows1, rows1, mats, mats, mats, mats, rows1, rows1, rows1)
        + (experts,) * 3,
        out_specs=(rows2, rows2, rows1, mats, mats, mats, mats, rows1, rows1, rows1) + (experts,) * 3,
        check_vma=False,
    )
```

profile of v0, /device:TPU:0, one launch (start us, length us, event | category | flops | bytes accessed | tf_op | source)
XLA Modules:
  0.0 766.0 jit_solution(6365902893276199014)
XLA Ops:
  7.3 3.4 constant_dynamic-slice_fusion.21
  23.8 2.5 fusion.17
  26.9 209.6 %forward_to_experts.1 = (f32[512,2048]{1,0:T(8,128)}, bf16[1024,2048]{1,0:T(8,128)(2,1)}, bf16[512,1024]{1,0:T(8,128)(2,1)}, bf16[512,1024]{1,0:T(8,128)(2,1)}, ...) custom-call(bf16[512,2048]{1,0:T(8,128)(2,1)} %get-tuple-element.68., ...), custom_call_target="tpu_custom_call" | custom-call | flops 8000000000 | bytes 60000000 | tf_op jit(solution)/shard_map/forward_to_experts/pallas_call | solution.py:700
  247.8 12.4 %fusion.90 = f32[1024,1536]{1,0:T(8,128)} fusion(bf16[1024,2048]{1,0:T(8,128)(2,1)} %get-tuple-element.36, bf16[1536,2048]{1,0:T(8,128)(2,1)} %get-tuple-element.37), kind=kOutput, calls=%fused_computation.275 | convolution fusion | flops 6442450944 | bytes 16777216 | tf_op jit(solution)/shard_map/dot_general | solution.py:136
  260.2 10.5 %fusion.91 = f32[1024,1536]{1,0:T(8,128)} fusion(bf16[1024,2048]{1,0:T(8,128)(2,1)S(1)} %copy-done.64, bf16[1536,2048]{1,0:T(8,128)(2,1)} %get-tuple-element.38), kind=kOutput, calls=%fused_computation.276 | convolution fusion | flops 6442450944 | bytes 16777216 | tf_op jit(solution)/shard_map/dot_general | solution.py:136
  275.0 2.5 copy.146
  280.4 16.6 %fusion.81 = f32[1024,1536]{1,0:T(8,128)} fusion(bf16[1536,2048]{1,0:T(8,128)(2,1)} %get-tuple-element.39, bf16[512,2048]{1,0:T(8,128)(2,1)} %collective-permute-done.2, bf16[512,512]{1,0:T(8,128)(2,1)} %copy-done.13, bf16[512,512]{1,0:T(8,128)(2,1)} %copy-done.15, bf16[512,512]{1,0:T(8,128)(2,1)S(1)} %get-tuple-element.119, ...), kind=kOutput, calls=%fused_computation.266 | convolution fusion | flops 6463422464 | bytes 16777216 | tf_op jit(solution)/shard_map/dot_general | solution.py:136
  297.2 12.4 %multiply_convert_fusion = (bf16[1024,1536]{1,0:T(8,128)(2,1)S(1)}, bf16[1024,1536]{1,0:T(8,128)(2,1)S(1)}, bf16[1024,1536]{1,0:T(8,128)(2,1)S(1)}) fusion(f32[1024,1536]{1,0:T(8,128)S(1)} %bitcast.267, f32[1024,1536]{1,0:T(8,128)} %fusion.81, f32[1024]{0:T(1024)S(1)} %bitcast.295, pred[1536]{0:T(1024)(128)(4,1)S(1)} %copy-done.45, f32[1024]{0:T(1024)S(1)} %bitcast.289, ...), kind=kLoop, calls=%fused_computation.10 | loop fusion | flops 51904512 | bytes 28356608 | tf_op jit(solution)/shard_map/convert_element_type | solution.py:829
  309.6 11.1 %fusion.92 = f32[1024,2048]{1,0:T(8,128)S(1)} fusion(bf16[1024,1536]{1,0:T(8,128)(2,1)S(1)} %get-tuple-element.70, bf16[1536,2048]{1,0:T(8,128)(2,1)} %get-tuple-element.37), kind=kOutput, calls=%fused_computation.277 | convolution fusion | flops 6442450944 | bytes 17825792 | tf_op jit(solution)/shard_map/dot_general | solution.py:833
  320.7 8.8 %add_convert_fusion = bf16[1024,2048]{1,0:T(8,128)(2,1)S(1)} fusion(f32[1024,2048]{1,0:T(8,128)S(1)} %fusion.92, bf16[1024,1536]{1,0:T(8,128)(2,1)S(1)} %get-tuple-element.69, bf16[1536,2048]{1,0:T(8,128)(2,1)} %get-tuple-element.38), kind=kOutput, calls=%fused_computation.5 | convolution fusion | flops 6446645248 | bytes 22020096 | tf_op jit(solution)/shard_map/dot_general | solution.py:834
  329.8 9.0 %convolution_convert_fusion.4 = bf16[1024,2048]{1,0:T(8,128)(2,1)S(1)} fusion(bf16[1024,1536]{1,0:T(8,128)(2,1)S(1)} %get-tuple-element.71, bf16[1536,2048]{1,0:T(8,128)(2,1)} %get-tuple-element.39), kind=kOutput, calls=%fused_computation.53 | convolution fusion | flops 6444548096 | bytes 13631488 | tf_op jit(solution)/shard_map/dot_general | solution.py:838
  343.8 8.8 %convolution_convert_fusion.2 = bf16[1536,2048]{1,0:T(8,128)(2,1)} fusion(bf16[1024,1536]{1,0:T(8,128)(2,1)S(1)} %get-tuple-element.70, bf16[1024,2048]{1,0:T(8,128)(2,1)S(1)} %copy-done.65), kind=kOutput, calls=%fused_computation.8 | convolution fusion | flops 6445596672 | bytes 13631488 | tf_op jit(solution)/shard_map/dot_general | solution.py:136
  354.9 11.4 %convolution_convert_fusion.1 = bf16[1536,2048]{1,0:T(8,128)(2,1)} fusion(bf16[1024,1536]{1,0:T(8,128)(2,1)} %copy-done.23, bf16[1024,2048]{1,0:T(8,128)(2,1)} %get-tuple-element.36), kind=kOutput, calls=%fused_computation.7 | convolution fusion | flops 6445596672 | bytes 13631488 | tf_op jit(solution)/shard_map/dot_general | solution.py:136
  366.3 20.4 %convolution_convert_fusion.3 = bf16[1536,2048]{1,0:T(8,128)(2,1)} fusion(bf16[1024,1536]{1,0:T(8,128)(2,1)S(1)} %copy-done.22, bf16[512,2048]{1,0:T(8,128)(2,1)} %collective-permute-done.2, bf16[512,512]{1,0:T(8,128)(2,1)S(1)} %copy-done.14, bf16[512,512]{1,0:T(8,128)(2,1)S(1)} %copy-done.16, bf16[512,512]{1,0:T(8,128)(2,1)S(1)} %get-tuple-element.119, ...), kind=kOutput, calls=%fused_computation.9 | convolution fusion | flops 6466568192 | bytes 13631488 | tf_op jit(solution)/shard_map/dot_general | solution.py:136
  386.7 3.8 add_convert_fusion.3
  390.5 51.3 %all-reduce.5.cloned.1.call-done = bf16[512,2048]{1,0:T(8,128)(2,1)} async-done(((bf16[512,2048]{1,0:T(8,128)(2,1)}), bf16[512,2048]{1,0:T(8,128)(2,1)}) %all-reduce.5.cloned.1.call-update) | async-done | bytes 2097168 | tf_op jit(solution)/shard_map/psum | solution.py:836
  443.4 3.3 fusion.14
  450.5 2.4 fusion.83
  461.6 24.8 %collective-permute-done.18 = bf16[1536,512]{1,0:T(8,128)(2,1)S(1)} collective-permute-done((bf16[1536,512]{1,0:T(8,128)(2,1)S(1)}, bf16[1536,512]{1,0:T(8,128)(2,1)S(1)}, u32[]{:S(2)}, u32[]{:S(2)}) %collective-permute-start.18) | collective-permute-done | bytes 1572896 | tf_op jit(solution)/shard_map/ppermute | solution.py:47
  490.0 30.0 %collective-permute-done.22 = bf16[1536,512]{1,0:T(8,128)(2,1)S(1)} collective-permute-done((bf16[1536,512]{1,0:T(8,128)(2,1)S(1)}, bf16[1536,512]{1,0:T(8,128)(2,1)S(1)}, u32[]{:S(2)}, u32[]{:S(2)}) %collective-permute-start.22) | collective-permute-done | bytes 1572896 | tf_op jit(solution)/shard_map/ppermute | solution.py:47
  523.8 28.8 %collective-permute-done.26 = bf16[1536,512]{1,0:T(8,128)(2,1)S(1)} collective-permute-done((bf16[1536,512]{1,0:T(8,128)(2,1)S(1)}, bf16[1536,512]{1,0:T(8,128)(2,1)S(1)}, u32[]{:S(2)}, u32[]{:S(2)}) %collective-permute-start.26) | collective-permute-done | bytes 1572896 | tf_op jit(solution)/shard_map/ppermute | solution.py:47
  555.3 5.2 fusion.13
  564.1 3.2 fusion.47
  570.0 2.9 fusion.41
  579.8 2.9 copy.137
  584.4 2.8 multiply_reduce_fusion.1
  588.2 6.8 convolution_convert_fusion.6
  595.0 6.3 convolution_convert_fusion
  601.3 2.4 convolution_convert_fusion.5
  607.5 10.8 %psum.31 = bf16[2,128]{1,0:T(2,128)(2,1)S(1)} all-reduce(bf16[2,128]{1,0:T(2,128)(2,1)S(1)} %pad_maximum_fusion.28), channel_id=1, replica_groups=mesh['dp'=4,'expert'=2,'tensor'=4] {'tensor'}, use_global_device_ids=true, to_apply=%region_19.20 | all-reduce | flops 256 | bytes 1024 | tf_op jit(solution)/shard_map/psum | solution.py:908
  618.3 2.8 pad_maximum_fusion.7
  621.1 3.4 dynamic-slice_bitcast_fusion
  625.9 3.9 convert_add_fusion.7
  631.6 3.8 convert_add_fusion.5
  636.0 4.9 collective-permute-done.27
  640.9 3.9 convert_add_fusion.3
  646.3 4.3 collective-permute-done.21
  652.6 14.9 %collective-permute-done.25 = bf16[768,512]{1,0:T(8,128)(2,1)} collective-permute-done((bf16[768,512]{1,0:T(8,128)(2,1)}, bf16[768,512]{1,0:T(8,128)(2,1)}, u32[]{:S(2)}, u32[]{:S(2)}) %collective-permute-start.25) | collective-permute-done | bytes 786464 | tf_op jit(solution)/shard_map/ppermute | solution.py:47
  669.4 14.1 %collective-permute-done.29 = bf16[768,512]{1,0:T(8,128)(2,1)} collective-permute-done((bf16[768,512]{1,0:T(8,128)(2,1)}, bf16[768,512]{1,0:T(8,128)(2,1)}, u32[]{:S(2)}, u32[]{:S(2)}) %collective-permute-start.29) | collective-permute-done | bytes 786464 | tf_op jit(solution)/shard_map/ppermute | solution.py:47
  691.4 2.9 fusion.18
  694.6 4.1 fusion.10
  700.8 2.5 fusion.20
  709.3 2.4 pad_maximum_fusion.1
  711.7 8.3 %collective-permute-done.5 = f32[5,128]{1,0:T(8,128)S(1)} collective-permute-done((f32[5,128]{1,0:T(8,128)S(1)}, f32[5,128]{1,0:T(8,128)S(1)}, u32[]{:S(2)}, u32[]{:S(2)}) %collective-permute-start.5) | collective-permute-done | bytes 2592 | tf_op jit(solution)/shard_map/ppermute | solution.py:47
  726.0 14.3 %collective-permute-done.11 = bf16[256,1280]{1,0:T(8,128)(2,1)S(1)} collective-permute-done((bf16[256,1280]{1,0:T(8,128)(2,1)S(1)}, bf16[256,1280]{1,0:T(8,128)(2,1)S(1)}, u32[]{:S(2)}, u32[]{:S(2)}) %collective-permute-start.11) | collective-permute-done | bytes 655392 | tf_op jit(solution)/shard_map/ppermute | solution.py:47
  741.5 2.4 collective-permute-done.15
  744.8 5.2 collective-permute-done.12
  754.3 3.0 collective-permute-done.10
  (325 shorter events, 122.0 us)
Async XLA Ops:
  7.2 434.6 %all-reduce.5.cloned.1.call-start = ((), (), s32[]{:S(2)}) async-start(), calls=%async_computation | async-start | bytes 4194304 | tf_op jit(solution)/shard_map/psum | solution.py:836
  13.1 267.3 %collective-permute-start.2 = (bf16[512,2048]{1,0:T(8,128)(2,1)}, bf16[512,2048]{1,0:T(8,128)(2,1)}, u32[]{:S(2)}, u32[]{:S(2)}) collective-permute-start(bf16[512,2048]{1,0:T(8,128)(2,1)} %pad_maximum_fusion.6), channel_id=1, source_target_pairs={{0,4},{4,0},{1,5},{5,1},{2,6},{6,2},{3,7},{7,3},{8,12},{12,8},{9,1... | collective-permute-start | bytes 6291464 | tf_op jit(solution)/shard_map/ppermute | solution.py:47
  14.2 265.3 %collective-permute-start = (f32[512,16]{0,1:T(8,128)}, f32[512,16]{0,1:T(8,128)}, u32[]{:S(2)}, u32[]{:S(2)}) collective-permute-start(f32[512,16]{0,1:T(8,128)} %select_add_fusion.1), channel_id=1, source_target_pairs={{0,4},{4,0},{1,5},{5,1},{2,6},{6,2},{3,7},{7,3},{8,12},{12,8},{9,1... | collective-permute-start | bytes 98312 | tf_op jit(solution)/shard_map/ppermute | solution.py:47
  280.3 16.8 %slice-start.2 = ((s8[6291456]{0:T(1024)(128)(4,1)}), s8[4194304]{0:T(1024)(128)(4,1)S(1)}, s32[]{:S(2)}) async-start(s8[6291456]{0:T(1024)(128)(4,1)} %bitcast.266), calls=%async_computation.5 | async-start | bytes 8388608
  280.3 16.7 %slice-start.4 = ((s8[6291456]{0:T(1024)(128)(4,1)}), s8[4194304]{0:T(1024)(128)(4,1)S(1)}, s32[]{:S(2)}) async-start(s8[6291456]{0:T(1024)(128)(4,1)} %bitcast.268), calls=%async_computation.7 | async-start | bytes 8388608
  280.3 16.7 %slice-start.3 = ((s8[6291456]{0:T(1024)(128)(4,1)}), s8[2097152]{0:T(1024)(128)(4,1)S(1)}, s32[]{:S(2)}) async-start(s8[6291456]{0:T(1024)(128)(4,1)} %bitcast.266), calls=%async_computation.6 | async-start | bytes 4194304
  280.3 16.7 %slice-start.5 = ((s8[6291456]{0:T(1024)(128)(4,1)}), s8[2097152]{0:T(1024)(128)(4,1)S(1)}, s32[]{:S(2)}) async-start(s8[6291456]{0:T(1024)(128)(4,1)} %bitcast.268), calls=%async_computation.8 | async-start | bytes 4194304
  280.4 16.7 %copy-start.45 = (pred[1536]{0:T(1024)(128)(4,1)S(1)}, pred[1536]{0:T(1024)(128)(4,1)}, u32[]{:S(2)}) copy-start(pred[1536]{0:T(1024)(128)(4,1)} %get-tuple-element.177) | copy-start | bytes 4612
  280.4 16.7 %copy-start.46 = (pred[1536]{0:T(1024)(128)(4,1)S(1)}, pred[1536]{0:T(1024)(128)(4,1)}, u32[]{:S(2)}) copy-start(pred[1536]{0:T(1024)(128)(4,1)} %get-tuple-element.178) | copy-start | bytes 4612
  280.4 16.7 %copy-start.47 = (pred[1536]{0:T(1024)(128)(4,1)S(1)}, pred[1536]{0:T(1024)(128)(4,1)}, u32[]{:S(2)}) copy-start(pred[1536]{0:T(1024)(128)(4,1)} %get-tuple-element.179) | copy-start | bytes 4612
  280.4 16.7 %copy-start.48 = (pred[1536]{0:T(1024)(128)(4,1)S(1)}, pred[1536]{0:T(1024)(128)(4,1)}, u32[]{:S(2)}) copy-start(pred[1536]{0:T(1024)(128)(4,1)} %get-tuple-element.180) | copy-start | bytes 4612
  309.6 20.2 %copy-start.21 = (bf16[1024,1536]{1,0:T(8,128)(2,1)}, bf16[1024,1536]{1,0:T(8,128)(2,1)S(1)}, u32[]{:S(2)}) copy-start(bf16[1024,1536]{1,0:T(8,128)(2,1)S(1)} %get-tuple-element.71) | copy-start | bytes 9437188
  329.7 22.9 %collective-permute-start.3 = (bf16[512,2048]{1,0:T(8,128)(2,1)S(1)}, bf16[512,2048]{1,0:T(8,128)(2,1)S(1)}, u32[]{:S(2)}, u32[]{:S(2)}) collective-permute-start(bf16[512,2048]{1,0:T(8,128)(2,1)S(1)} %split.15), channel_id=1, source_target_pairs={{0,4},{4,0},{1,5},{5,1},{2,6},{6,2},{3,7},{7,3},{8,12},{12,8},{9,1... | collective-permute-start | bytes 6291464 | tf_op jit(solution)/shard_map/ppermute | solution.py:47
  342.3 44.4 %collective-permute-start.1 = (bf16[512,2048]{1,0:T(8,128)(2,1)}, bf16[512,2048]{1,0:T(8,128)(2,1)}, u32[]{:S(2)}, u32[]{:S(2)}) collective-permute-start(bf16[512,2048]{1,0:T(8,128)(2,1)} %split.13), channel_id=1, source_target_pairs={{0,4},{4,0},{1,5},{5,1},{2,6},{6,2},{3,7},{7,3},{8,12},{12,8},{9,1... | collective-permute-start | bytes 6291464 | tf_op jit(solution)/shard_map/ppermute | solution.py:47
  354.8 200.5 %all-reduce.7.cloned.1.call-start = ((), (), s32[]{:S(2)}) async-start(), calls=%async_computation.1 | async-start | bytes 4194304 | tf_op jit(solution)/shard_map/psum | solution.py:853
  366.3 20.4 %copy-start.20 = (bf16[1024,2048]{1,0:T(8,128)(2,1)S(1)}, bf16[1024,2048]{1,0:T(8,128)(2,1)}, u32[]{:S(2)}) copy-start(bf16[1024,2048]{1,0:T(8,128)(2,1)} %copy-done.19) | copy-start | bytes 12582916
  386.7 55.2 %copy-start.36 = (f32[4,2,2,128]{3,2,1,0:T(2,128)S(1)}, f32[4,2,2,128]{3,2,1,0:T(2,128)}, u32[]{:S(2)}) copy-start(f32[4,2,2,128]{3,2,1,0:T(2,128)} %get-tuple-element.131) | copy-start | bytes 24580
  386.7 55.2 %copy-start.41 = (f32[512]{0:T(512)S(1)}, f32[512]{0:T(512)}, u32[]{:S(2)}) copy-start(f32[512]{0:T(512)} %add_rsqrt_fusion.3) | copy-start | bytes 6148
  441.8 249.5 %all-reduce.9.cloned.1.call-start = ((), (), s32[]{:S(2)}) async-start(), calls=%async_computation.2 | async-start | bytes 4194304 | tf_op jit(solution)/shard_map/psum | solution.py:908
  449.0 37.3 %collective-permute-start.18 = (bf16[1536,512]{1,0:T(8,128)(2,1)S(1)}, bf16[1536,512]{1,0:T(8,128)(2,1)S(1)}, u32[]{:S(2)}, u32[]{:S(2)}) collective-permute-start(bf16[1536,512]{1,0:T(8,128)(2,1)S(1)} %pad_maximum_fusion.9), channel_id=1, source_target_pairs={{0,8},{8,0},{16,24},{24,16},{1,9},{9,1},{17,25},{25,17},{2,10},{10... | collective-permute-start | bytes 4718600 | tf_op jit(solution)/shard_map/ppermute | solution.py:47
  453.1 67.0 %collective-permute-start.22 = (bf16[1536,512]{1,0:T(8,128)(2,1)S(1)}, bf16[1536,512]{1,0:T(8,128)(2,1)S(1)}, u32[]{:S(2)}, u32[]{:S(2)}) collective-permute-start(bf16[1536,512]{1,0:T(8,128)(2,1)S(1)} %pad_maximum_fusion.11), channel_id=1, source_target_pairs={{0,8},{8,0},{16,24},{24,16},{1,9},{9,1},{17,25},{25,17},{2,10},{10... | collective-permute-start | bytes 4718600 | tf_op jit(solution)/shard_map/ppermute | solution.py:47
  454.5 98.1 %collective-permute-start.26 = (bf16[1536,512]{1,0:T(8,128)(2,1)S(1)}, bf16[1536,512]{1,0:T(8,128)(2,1)S(1)}, u32[]{:S(2)}, u32[]{:S(2)}) collective-permute-start(bf16[1536,512]{1,0:T(8,128)(2,1)S(1)} %pad_maximum_fusion.13), channel_id=1, source_target_pairs={{0,8},{8,0},{16,24},{24,16},{1,9},{9,1},{17,25},{25,17},{2,10},{10... | collective-permute-start | bytes 4718600 | tf_op jit(solution)/shard_map/ppermute | solution.py:47
  457.0 167.5 %collective-permute-start.20 = (bf16[1536,512]{1,0:T(8,128)(2,1)}, bf16[1536,512]{1,0:T(8,128)(2,1)}, u32[]{:S(2)}, u32[]{:S(2)}) collective-permute-start(bf16[1536,512]{1,0:T(8,128)(2,1)} %pad_maximum_fusion.10), channel_id=1, source_target_pairs={{0,16},{8,24},{16,0},{24,8},{1,17},{9,25},{17,1},{25,9},{2,18},{10... | collective-permute-start | bytes 4718600 | tf_op jit(solution)/shard_map/ppermute | solution.py:47
  459.9 169.9 %collective-permute-start.24 = (bf16[1536,512]{1,0:T(8,128)(2,1)}, bf16[1536,512]{1,0:T(8,128)(2,1)}, u32[]{:S(2)}, u32[]{:S(2)}) collective-permute-start(bf16[1536,512]{1,0:T(8,128)(2,1)} %pad_maximum_fusion.12), channel_id=1, source_target_pairs={{0,16},{8,24},{16,0},{24,8},{1,17},{9,25},{17,1},{25,9},{2,18},{10... | collective-permute-start | bytes 4718600 | tf_op jit(solution)/shard_map/ppermute | solution.py:47
  486.3 67.7 %copy-start.29 = (bf16[1536,512]{1,0:T(8,128)(2,1)}, bf16[1536,512]{1,0:T(8,128)(2,1)S(1)}, u32[]{:S(2)}) copy-start(bf16[1536,512]{1,0:T(8,128)(2,1)S(1)} %collective-permute-done.18) | copy-start | bytes 4718596
  486.3 149.1 %collective-permute-start.28 = (bf16[1536,512]{1,0:T(8,128)(2,1)}, bf16[1536,512]{1,0:T(8,128)(2,1)}, u32[]{:S(2)}, u32[]{:S(2)}) collective-permute-start(bf16[1536,512]{1,0:T(8,128)(2,1)} %pad_maximum_fusion.14), channel_id=1, source_target_pairs={{0,16},{8,24},{16,0},{24,8},{1,17},{9,25},{17,1},{25,9},{2,18},{10... | collective-permute-start | bytes 4718600 | tf_op jit(solution)/shard_map/ppermute | solution.py:47
  520.0 32.6 %copy-start.27 = (bf16[1536,512]{1,0:T(8,128)(2,1)}, bf16[1536,512]{1,0:T(8,128)(2,1)S(1)}, u32[]{:S(2)}) copy-start(bf16[1536,512]{1,0:T(8,128)(2,1)S(1)} %collective-permute-done.22) | copy-start | bytes 4718596
  520.0 105.7 %collective-permute-start.19 = (bf16[768,512]{1,0:T(8,128)(2,1)}, bf16[768,512]{1,0:T(8,128)(2,1)}, u32[]{:S(2)}, u32[]{:S(2)}) collective-permute-start(bf16[768,512]{1,0:T(8,128)(2,1)} %add_convert_fusion.9), channel_id=1, source_target_pairs={{0,16},{8,24},{16,0},{24,8},{1,17},{9,25},{17,1},{25,9},{2,18},{10... | collective-permute-start | bytes 2359304 | tf_op jit(solution)/shard_map/ppermute | solution.py:47
  552.6 77.5 %collective-permute-start.23 = (bf16[768,512]{1,0:T(8,128)(2,1)}, bf16[768,512]{1,0:T(8,128)(2,1)}, u32[]{:S(2)}, u32[]{:S(2)}) collective-permute-start(bf16[768,512]{1,0:T(8,128)(2,1)} %add_convert_fusion.7), channel_id=1, source_target_pairs={{0,16},{8,24},{16,0},{24,8},{1,17},{9,25},{17,1},{25,9},{2,18},{10... | collective-permute-start | bytes 2359304 | tf_op jit(solution)/shard_map/ppermute | solution.py:47
  624.5 16.4 %collective-permute-start.27 = (bf16[768,512]{1,0:T(8,128)(2,1)}, bf16[768,512]{1,0:T(8,128)(2,1)}, u32[]{:S(2)}, u32[]{:S(2)}) collective-permute-start(bf16[768,512]{1,0:T(8,128)(2,1)} %add_convert_fusion.5), channel_id=1, source_target_pairs={{0,16},{8,24},{16,0},{24,8},{1,17},{9,25},{17,1},{25,9},{2,18},{10... | collective-permute-start | bytes 2359304 | tf_op jit(solution)/shard_map/ppermute | solution.py:47
  625.8 94.2 %collective-permute-start.8 = (bf16[4,256,1280]{2,1,0:T(8,128)(2,1)}, bf16[4,256,1280]{2,1,0:T(8,128)(2,1)}, u32[]{:S(2)}, u32[]{:S(2)}) collective-permute-start(bf16[4,256,1280]{2,1,0:T(8,128)(2,1)} %dynamic-slice_bitcast_fusion), channel_id=1, source_target_pairs={{0,4},{4,0},{1,5},{5,1},{2,6},{6,2},{3,7},{7,3},{8,12},{12,8},{9,1... | collective-permute-start | bytes 7864328 | tf_op jit(solution)/shard_map/ppermute | solution.py:47
  629.7 69.4 %collective-permute-start.13 = (bf16[4,256,1024]{2,1,0:T(8,128)(2,1)}, bf16[4,256,1024]{2,1,0:T(8,128)(2,1)}, u32[]{:S(2)}, u32[]{:S(2)}) collective-permute-start(bf16[4,256,1024]{2,1,0:T(8,128)(2,1)} %dynamic-slice_bitcast_fusion.1), channel_id=1, source_target_pairs={{0,4},{4,0},{1,5},{5,1},{2,6},{6,2},{3,7},{7,3},{8,12},{12,8},{9,1... | collective-permute-start | bytes 6291464 | tf_op jit(solution)/shard_map/ppermute | solution.py:47
  630.1 20.5 %collective-permute-start.21 = (bf16[768,512]{1,0:T(8,128)(2,1)S(1)}, bf16[768,512]{1,0:T(8,128)(2,1)}, u32[]{:S(2)}, u32[]{:S(2)}) collective-permute-start(bf16[768,512]{1,0:T(8,128)(2,1)S(1)} %get-tuple-element.87), channel_id=1, source_target_pairs={{0,8},{8,0},{16,24},{24,16},{1,9},{9,1},{17,25},{25,17},{2,10},{10... | collective-permute-start | bytes 2359304 | tf_op jit(solution)/shard_map/ppermute | solution.py:47
  635.5 32.0 %collective-permute-start.25 = (bf16[768,512]{1,0:T(8,128)(2,1)}, bf16[768,512]{1,0:T(8,128)(2,1)}, u32[]{:S(2)}, u32[]{:S(2)}) collective-permute-start(bf16[768,512]{1,0:T(8,128)(2,1)} %get-tuple-element.81), channel_id=1, source_target_pairs={{0,8},{8,0},{16,24},{24,16},{1,9},{9,1},{17,25},{25,17},{2,10},{10... | collective-permute-start | bytes 2359304 | tf_op jit(solution)/shard_map/ppermute | solution.py:47
  644.8 38.8 %collective-permute-start.29 = (bf16[768,512]{1,0:T(8,128)(2,1)}, bf16[768,512]{1,0:T(8,128)(2,1)}, u32[]{:S(2)}, u32[]{:S(2)}) collective-permute-start(bf16[768,512]{1,0:T(8,128)(2,1)} %get-tuple-element.75), channel_id=1, source_target_pairs={{0,8},{8,0},{16,24},{24,16},{1,9},{9,1},{17,25},{25,17},{2,10},{10... | collective-permute-start | bytes 2359304 | tf_op jit(solution)/shard_map/ppermute | solution.py:47
  652.6 32.9 %copy-start.10 = (f32[768,512]{1,0:T(8,128)S(1)}, f32[768,512]{1,0:T(8,128)}, u32[]{:S(2)}) copy-start(f32[768,512]{1,0:T(8,128)} %get-tuple-element.86) | copy-start | bytes 4718596
  694.5 10.6 %collective-permute-start.4 = (f32[4,5,128]{2,1,0:T(8,128)S(1)}, f32[4,5,128]{2,1,0:T(8,128)S(1)}, u32[]{:S(2)}, u32[]{:S(2)}) collective-permute-start(f32[4,5,128]{2,1,0:T(8,128)S(1)} %slice_bitcast_fusion.17), channel_id=1, source_target_pairs={{0,4},{4,0},{1,5},{5,1},{2,6},{6,2},{3,7},{7,3},{8,12},{12,8},{9,1... | collective-permute-start | bytes 30728 | tf_op jit(solution)/shard_map/ppermute | solution.py:47
  703.5 21.4 %collective-permute-start.14 = (bf16[256,1024]{1,0:T(8,128)(2,1)S(1)}, bf16[256,1024]{1,0:T(8,128)(2,1)S(1)}, u32[]{:S(2)}, u32[]{:S(2)}) collective-permute-start(bf16[256,1024]{1,0:T(8,128)(2,1)S(1)} %pad_maximum_fusion.22), channel_id=1, source_target_pairs={{0,8},{8,0},{16,24},{24,16},{1,9},{9,1},{17,25},{25,17},{2,10},{10... | collective-permute-start | bytes 1572872 | tf_op jit(solution)/shard_map/ppermute | solution.py:47
  705.1 3.7 collective-permute-start.6
  706.0 35.5 %collective-permute-start.16 = (bf16[256,1024]{1,0:T(8,128)(2,1)S(1)}, bf16[256,1024]{1,0:T(8,128)(2,1)S(1)}, u32[]{:S(2)}, u32[]{:S(2)}) collective-permute-start(bf16[256,1024]{1,0:T(8,128)(2,1)S(1)} %pad_maximum_fusion.23), channel_id=1, source_target_pairs={{0,16},{8,24},{16,0},{24,8},{1,17},{9,25},{17,1},{25,9},{2,18},{10... | collective-permute-start | bytes 1572872 | tf_op jit(solution)/shard_map/ppermute | solution.py:47
  707.3 12.7 %collective-permute-start.5 = (f32[5,128]{1,0:T(8,128)S(1)}, f32[5,128]{1,0:T(8,128)S(1)}, u32[]{:S(2)}, u32[]{:S(2)}) collective-permute-start(f32[5,128]{1,0:T(8,128)S(1)} %get-tuple-element.142), channel_id=1, source_target_pairs={{0,16},{8,24},{16,0},{24,8},{1,17},{9,25},{17,1},{25,9},{2,18},{10... | collective-permute-start | bytes 7688 | tf_op jit(solution)/shard_map/ppermute | solution.py:47
  708.8 11.2 %collective-permute-start.7 = (f32[5,128]{1,0:T(8,128)S(1)}, f32[5,128]{1,0:T(8,128)S(1)}, u32[]{:S(2)}, u32[]{:S(2)}) collective-permute-start(f32[5,128]{1,0:T(8,128)S(1)} %fusion.76), channel_id=1, source_target_pairs={{0,8},{8,0},{16,24},{24,16},{1,9},{9,1},{17,25},{25,17},{2,10},{10... | collective-permute-start | bytes 7688 | tf_op jit(solution)/shard_map/ppermute | solution.py:47
  722.5 17.7 %collective-permute-start.11 = (bf16[256,1280]{1,0:T(8,128)(2,1)S(1)}, bf16[256,1280]{1,0:T(8,128)(2,1)S(1)}, u32[]{:S(2)}, u32[]{:S(2)}) collective-permute-start(bf16[256,1280]{1,0:T(8,128)(2,1)S(1)} %pad_maximum_fusion.19), channel_id=1, source_target_pairs={{0,16},{8,24},{16,0},{24,8},{1,17},{9,25},{17,1},{25,9},{2,18},{10... | collective-permute-start | bytes 1966088 | tf_op jit(solution)/shard_map/ppermute | solution.py:47
  724.3 20.4 %collective-permute-start.9 = (bf16[256,1280]{1,0:T(8,128)(2,1)S(1)}, bf16[256,1280]{1,0:T(8,128)(2,1)S(1)}, u32[]{:S(2)}, u32[]{:S(2)}) collective-permute-start(bf16[256,1280]{1,0:T(8,128)(2,1)S(1)} %pad_maximum_fusion.18), channel_id=1, source_target_pairs={{0,8},{8,0},{16,24},{24,16},{1,9},{9,1},{17,25},{25,17},{2,10},{10... | collective-permute-start | bytes 1966088 | tf_op jit(solution)/shard_map/ppermute | solution.py:47
  725.0 18.9 %collective-permute-start.15 = (bf16[128,1024]{1,0:T(8,128)(2,1)S(1)}, bf16[128,1024]{1,0:T(8,128)(2,1)S(1)}, u32[]{:S(2)}, u32[]{:S(2)}) collective-permute-start(bf16[128,1024]{1,0:T(8,128)(2,1)S(1)} %fusion.62), channel_id=1, source_target_pairs={{0,16},{8,24},{16,0},{24,8},{1,17},{9,25},{17,1},{25,9},{2,18},{10... | collective-permute-start | bytes 786440 | tf_op jit(solution)/shard_map/ppermute | solution.py:47
  740.3 9.6 %collective-permute-start.12 = (bf16[128,1280]{1,0:T(8,128)(2,1)S(1)}, bf16[128,1280]{1,0:T(8,128)(2,1)S(1)}, u32[]{:S(2)}, u32[]{:S(2)}) collective-permute-start(bf16[128,1280]{1,0:T(8,128)(2,1)S(1)} %fusion.56), channel_id=1, source_target_pairs={{0,8},{8,0},{16,24},{24,16},{1,9},{9,1},{17,25},{25,17},{2,10},{10... | collective-permute-start | bytes 983048 | tf_op jit(solution)/shard_map/ppermute | solution.py:47
  744.2 8.9 %collective-permute-start.17 = (bf16[128,1024]{1,0:T(8,128)(2,1)S(1)}, bf16[128,1024]{1,0:T(8,128)(2,1)S(1)}, u32[]{:S(2)}, u32[]{:S(2)}) collective-permute-start(bf16[128,1024]{1,0:T(8,128)(2,1)S(1)} %get-tuple-element.107), channel_id=1, source_target_pairs={{0,8},{8,0},{16,24},{24,16},{1,9},{9,1},{17,25},{25,17},{2,10},{10... | collective-permute-start | bytes 786440 | tf_op jit(solution)/shard_map/ppermute | solution.py:47
  750.1 7.1 collective-permute-start.10
  (59 other events, 361.3 us)
Sparse Core Ops, SparseCore 0:
  354.9 86.8 all-reduce.4
  444.9 85.4 all-reduce.6
  595.1 85.6 all-reduce.8
where the time goes:
time: 772 us; the launch traced here: 766 us
  Pallas kernels  210 us (27%)
  waiting for transfers between devices  209 us (27%)
  matrix products  136 us (18%)
  other arithmetic  108 us (14%)
  local copies, waits for them, and re-layouts  50.1 us (6%)
  starting transfers between devices  26.8 us (3%)
  between operations  15.9 us (2%)
  blocking collectives  10.8 us (1%)
    pallas_call x1, Pallas kernels, forward_call(): pl.pallas_call(forward_kernel, out_shape=[o[0] for o in outs], in_specs=[...  210 us
    ppermute x30, waiting for transfers between devices, flip(): return lax.ppermute(x, axis, [(i, i ^ bit) for i in range(n)])  157 us
    dot_general x9, matrix products, dotf(): return lax.dot_general(a, b, (dims, ((), ())), preferred_element_type=f32)  95.6 us
    psum x1, waiting for transfers between devices, local_fast(): grad_hidden_two = lax.psum(grad_hidden_two, 'tensor')  51.3 us
    ppermute x30, starting transfers between devices, flip(): return lax.ppermute(x, axis, [(i, i ^ bit) for i in range(n)])  26.7 us
    add x10, other arithmetic, dp_scatter(): done.append(add(b[0], got[:h]) + flip(on, axis, second).astype(f32))  17.9 us
    unnamed x152, local copies, waits for them, and re-layouts  17.1 us
  transfers between devices with their start and end apart: 33, of which 15 were waited for; matrix products, arithmetic and copies ran while one was open for 29% of the time, Pallas kernels for 27%

commit v1 on v0

--- a/solution.py
+++ b/solution.py
@@ -718,6 +718,746 @@
     )(tokens, qkv_own, wo_own, gate_own, up_own, down_own, gains_own, cos, sin, key_ok)
 
 
+def expert_kernel(
+    h2, g, mine, gate_in, up_in, down_in,
+    grad_h2, out, grads, got,
+    gate, up, down, acts, drow, rbuf, in_buf, mid_buf, stage,
+    load_sem, x_send, x_recv, s_send, s_recv, keep_sem, out_sem, *line,
+):
+    to = plane_partners()
+    side, mid, inner = line_roles("tensor")
+    barrier = pltpu.get_barrier_semaphore()
+    near = [(1, 0), (2, 0), (0, 1)]
+    for k in near:
+        pl.semaphore_signal(barrier, inc=1, device_id=to[k], device_id_type=MESH)
+    pl.semaphore_signal(barrier, inc=1, device_id={"tensor": side}, device_id_type=MESH)
+
+    @pl.when(inner)
+    def _():
+        pl.semaphore_signal(barrier, inc=1, device_id={"tensor": mid}, device_id_type=MESH)
+        pl.semaphore_wait(barrier, len(near) + 2)
+
+    @pl.when(jnp.logical_not(inner))
+    def _():
+        pl.semaphore_wait(barrier, len(near) + 1)
+
+    tall, width = down.shape
+    rows = drow.shape[0] // 2
+    hidden = mine.shape[1]
+    tiles = tall // 256
+    wide = width // 4
+    tile = lambda t: pl.ds(pl.multiple_of(t * 256, 256), 256)
+    order = lambda i: i // 2 + (tiles // 2) * (i % 2)
+
+    def load(t, j):
+        src, dst = ((gate_in, gate), (up_in, up), (down_in, down))[j]
+        return pltpu.make_async_copy(src.at[tile(t)], dst.at[tile(t)], load_sem.at[t, j])
+
+    def start_loads(i):
+        for j in range(3):
+            load(order(i), j).start()
+
+    over(tiles, start_loads)
+
+    def keep(m, t, slot):
+        return pltpu.make_async_copy(stage.at[slot], grads.at[m, tile(t)], keep_sem.at[slot])
+
+    def send(m, t, j, way):
+        src = grads.at[m, tile(t), pl.ds((3 if j else way) * wide, wide)]
+        dst = got.at[m, tile(t), pl.ds(j * wide, wide)]
+        return remote(src, dst, s_send.at[m, t, j], s_recv.at[m, t, j], to[way, 0])
+
+    def send_tile(u):
+        m, i = u // tiles, u % tiles
+        t = order(i)
+        keep(m, t, u % 2).wait()
+        for way in (1, 2):
+
+            @pl.when(i % 2 == way - 1)
+            def _(way=way):
+                for j in range(2):
+                    send(m, t, j, way).start()
+
+    def grad_tile(u, rhs):
+        m, i = u // tiles, u % tiles
+        t = order(i)
+        low = acts[m, :, tile(t)]
+        for k in range(4):
+            cols = slice(k * wide, (k + 1) * wide)
+            stage[u % 2, :, cols] = tn(low, rhs[:, cols]).astype(bf16)
+        keep(m, t, u % 2).start()
+
+        @pl.when(u > 0)
+        def _():
+            send_tile(u - 1)
+
+    units = tall // 8
+
+    def hidden_tile(i):
+        t = order(i)
+        for j in range(3):
+            load(t, j).wait()
+        first = (t * 256) // units
+        edge = (first + 1) * units - t * 256
+        lanes = lax.broadcasted_iota(jnp.int32, mine.shape, 1)
+        pick = lambda e: jnp.sum(jnp.where(lanes == e, mine[...], 0.0), axis=1, keepdims=True)
+        column = lax.broadcasted_iota(jnp.int32, (2 * rows, 256), 1)
+        scale = jnp.where(column < edge, pick(first), pick(first + 1))
+        gate_value = nt(h2[...], gate[tile(t)])
+        up_value = nt(h2[...], up[tile(t)])
+        grad_act = nt(g[...], down[tile(t)]) * scale
+        sig = jax.nn.sigmoid(gate_value)
+        silu = gate_value * sig
+        acts[0, :, tile(t)] = (silu * up_value * scale).astype(bf16)
+        acts[2, :, tile(t)] = (grad_act * silu).astype(bf16)
+        acts[1, :, tile(t)] = (grad_act * up_value * sig * (1.0 + gate_value * (1.0 - sig))).astype(bf16)
+        grad_tile(i, g)
+
+    over(tiles, hidden_tile)
+
+    step = rows // CHUNKS
+
+    def give(i):
+        src = drow.at[pl.ds(pl.multiple_of(rows + i * step, step), step)]
+        dst = rbuf.at[pl.ds(pl.multiple_of(i * step, step), step)]
+        return remote(src, dst, x_send.at[i], x_recv.at[i], to[0, 1])
+
+    for part_rows in (slice(rows, 2 * rows), slice(0, rows)):
+
+        def row_grads(j, part_rows=part_rows):
+            col = pl.ds(pl.multiple_of(j * 256, 256), 256)
+            drow[part_rows, col] = (
+                nn(acts[1, part_rows, :], gate[:, col]) + nn(acts[2, part_rows, :], up[:, col])
+            ).astype(bf16)
+
+        over(width // 256, row_grads)
+        if part_rows.start:
+            over(CHUNKS, lambda i: give(i).start())
+
+    def add_other(c):
+        give(c).wait_recv()
+        r = pl.ds(pl.multiple_of(c * step, step), step)
+        drow[r] = (drow[r].astype(f32) + rbuf[r].astype(f32)).astype(bf16)
+
+    def out_copy(j):
+        col = pl.ds(pl.multiple_of(j * 256, 256), 256)
+        return pltpu.make_async_copy(gate.at[pl.ds(0, 2 * rows), col], out.at[:, col], out_sem.at[j])
+
+    def work(i):
+        @pl.when(i < 2 * tiles)
+        def _():
+            grad_tile(tiles + i, h2)
+
+        @pl.when(i == 2 * tiles)
+        def _():
+            send_tile(3 * tiles - 1)
+
+        @pl.when(i >= 2 * tiles)
+        def _():
+            j = i - 2 * tiles
+            col = pl.ds(pl.multiple_of(j * 256, 256), 256)
+            gate[0 : 2 * rows, col] = nn(acts[0], down[:, col]).astype(bf16)
+            out_copy(j).start()
+
+    line_sum_work(
+        drow, in_buf, mid_buf, drow, grad_h2, line, "tensor", rows, add_other, lambda r, c: None, work,
+        2 * tiles + width // 256,
+    )
+    over(width // 256, lambda j: out_copy(j).wait())
+    over(CHUNKS, lambda i: give(i).wait_send())
+
+    def finish_tile(u):
+        m, i = u // tiles, u % tiles
+        for way in (1, 2):
+
+            @pl.when(i % 2 == way - 1)
+            def _(way=way):
+                for j in range(2):
+                    send(m, order(i), j, way).wait()
+
+    over(3 * tiles, finish_tile)
+
+
+def line_sum_work(x_ref, in_buf, mid_buf, part, out_ref, sems, axis, n_rows, ready, finish, work, n_work):
+    a_send, a_recv, b_send, b_recv, c_send, c_recv = sems
+    side, mid, inner = line_roles(axis)
+    step = n_rows // CHUNKS
+    steps = max(n_work, CHUNKS + 4)
+
+    def rows(c):
+        return pl.ds(pl.multiple_of(c * step, step), step)
+
+    def copy(src, dst, c, send, recv, to):
+        return pltpu.make_async_remote_copy(
+            src.at[rows(c)], dst.at[rows(c)], send.at[c], recv.at[c], device_id={axis: to}, device_id_type=MESH
+        )
+
+    to_inner = lambda c: copy(x_ref, in_buf, c, a_send, a_recv, side)
+    to_middle = lambda c: copy(part, mid_buf, c, b_send, b_recv, mid)
+    to_outer = lambda c: copy(out_ref, out_ref, c, c_send, c_recv, side)
+
+    @pl.when(jnp.logical_not(inner))
+    def _():
+        def begin(c):
+            ready(c)
+            to_inner(c).start()
+
+        over(CHUNKS, begin)
+
+        def one(i):
+            @pl.when((i >= 4) & (i < CHUNKS + 4))
+            def _():
+                to_outer(i - 4).wait_recv()
+                finish(rows(i - 4), i - 4)
+
+            @pl.when(i < n_work)
+            def _():
+                work(i)
+
+        over(steps, one)
+        over(CHUNKS, lambda c: to_inner(c).wait_send())
+
+    @pl.when(inner)
+    def _():
+        def first(c):
+            ready(c)
+            to_inner(c).wait_recv()
+            r = rows(c)
+            part[r] = (x_ref[r].astype(f32) + in_buf[r].astype(f32)).astype(bf16)
+            to_middle(c).start()
+
+        def second(c):
+            to_middle(c).wait_recv()
+            r = rows(c)
+            out_ref[r] = (part[r].astype(f32) + mid_buf[r].astype(f32)).astype(bf16)
+            to_outer(c).start()
+            finish(r, c)
+
+        def one(i):
+            @pl.when(i < CHUNKS)
+            def _():
+                first(i)
+
+            @pl.when((i >= 2) & (i < CHUNKS + 2))
+            def _():
+                second(i - 2)
+
+            @pl.when(i < n_work)
+            def _():
+                work(i)
+
+        over(steps, one)
+
+        def done(c):
+            to_middle(c).wait_send()
+            to_outer(c).wait_send()
+
+        over(CHUNKS, done)
+
+
+def expert_call(h2, g, mine, gate, up, down):
+    tall, width = down.shape
+    rows = h2.shape[0] // 2
+    vmem, anyspace = pl.BlockSpec(memory_space=pltpu.VMEM), pl.BlockSpec(memory_space=pl.ANY)
+    shape = jax.ShapeDtypeStruct
+    dma = pltpu.SemaphoreType.DMA
+    tiles = tall // 256
+    return pl.pallas_call(
+        expert_kernel,
+        out_shape=[
+            shape((rows, width), bf16),
+            shape((2 * rows, width), bf16),
+            shape((3, tall, width), bf16),
+            shape((3, tall, width // 2), bf16),
+        ],
+        in_specs=[vmem, vmem, vmem, anyspace, anyspace, anyspace],
+        out_specs=[vmem, anyspace, anyspace, anyspace],
+        scratch_shapes=[pltpu.VMEM((tall, width), bf16)] * 3
+        + [
+            pltpu.VMEM((3, 2 * rows, tall), bf16),
+            pltpu.VMEM((2 * rows, width), bf16),
+            pltpu.VMEM((rows, width), bf16),
+            pltpu.VMEM((rows, width), bf16),
+            pltpu.VMEM((rows, width), bf16),
+            pltpu.VMEM((2, 256, width), bf16),
+            dma((tiles, 3)), dma((CHUNKS,)), dma((CHUNKS,)), dma((3, tiles, 2)), dma((3, tiles, 2)),
+            dma((2,)), dma((width // 256,)),
+        ]
+        + line_sems(),
+        compiler_params=pltpu.CompilerParams(
+            collective_id=2, has_side_effects=True, vmem_limit_bytes=62 * 2**20
+        ),
+        cost_estimate=pl.CostEstimate(flops=58 * 10**9, bytes_accessed=60 * 10**6, transcendentals=2 * 10**6),
+        name="experts",
+    )(h2, g, mine, gate, up, down)
+
+
+def plane_barrier(to, z_others):
+    barrier = pltpu.get_barrier_semaphore()
+    others = [k for k in to if k != (0, 0)]
+    for k in others:
+        pl.semaphore_signal(barrier, inc=1, device_id=to[k], device_id_type=MESH)
+    for z in z_others:
+        pl.semaphore_signal(barrier, inc=1, device_id={"tensor": z}, device_id_type=MESH)
+    pl.semaphore_wait(barrier, len(others) + len(z_others))
+    return others
+
+
+def z_partners():
+    p = lax.axis_index("tensor")
+    return [p + 1 - 2 * (p % 2), p + 2 - 4 * (p // 2), 3 - p]
+
+
+def gain_vectors(gains, gain_rows):
+    for kd in range(4):
+        for kc in range(2):
+            g = gains[kd, kc]
+            for j in range(2):
+                col = (kd * 2 + kc) * 256 + j * 128
+                gain_rows[0:1, col : col + 128] = g[j : j + 1]
+                gain_rows[1:2, col : col + 128] = g[2 + j : 3 + j]
+    heads = jnp.sum(gains[...].reshape(8, 8, 128), axis=0)
+    return heads[4:5], heads[5:6]
+
+
+def attention_back_kernel(
+    grad_h2, x2, cot, qrot, krot, value, raw, gains, cos, sin, probs, wo_in, qkv_in, out_part, grads, got,
+    output, dx2, low, grad_qkv, grad_h1, gain_grads, got2,
+    wo, qkv, own_out, rbuf, in_buf, mid_buf, summed, datt, pbuf, dk, dv, gain_rows, load_a, load_b, on_buf,
+    w_sem, p_sem, l_sem, x_send, x_recv, s_send, s_recv, *line,
+):
+    to = plane_partners()
+    plane_barrier(to, z_partners())
+    places = [to[k, 0]["dp"] for k in range(4)]
+    rows, width = x2.shape
+    wide = width // 4
+    tiles = grads.shape[1] // 256
+    q_cols = qrot.shape[1]
+    n_heads = q_cols // 128
+    step = rows // CHUNKS
+    rate = 128 ** (-0.5)
+    order = lambda i: i // 2 + (tiles // 2) * (i % 2)
+    tile = lambda t: pl.ds(pl.multiple_of(t * 256, 256), 256)
+
+    def give(i):
+        src = out_part.at[pl.ds(pl.multiple_of(rows + i * step, step), step)]
+        dst = rbuf.at[pl.ds(pl.multiple_of(i * step, step), step)]
+        return remote(src, dst, x_send.at[i], x_recv.at[i], to[0, 1])
+
+    over(CHUNKS, lambda i: give(i).start())
+    weights = [
+        pltpu.make_async_copy(wo_in, wo, w_sem.at[0]),
+        pltpu.make_async_copy(qkv_in, qkv, w_sem.at[1]),
+        pltpu.make_async_copy(out_part.at[pl.ds(0, rows)], own_out, w_sem.at[2]),
+    ]
+    for w in weights:
+        w.start()
+
+    def load_probs(h):
+        return pltpu.make_async_copy(probs.at[h], pbuf.at[h % 2], p_sem.at[h % 2])
+
+    def loads(u, first):
+        m, t = u // tiles, order(u % tiles)
+        slot = u % 2
+        return (
+            pltpu.make_async_copy(
+                grads.at[m, tile(t), pl.ds((3 - first) * wide, wide)], load_a.at[slot], l_sem.at[slot, 0]
+            ),
+            pltpu.make_async_copy(got.at[m, tile(t), pl.ds(wide, wide)], load_b.at[slot], l_sem.at[slot, 1]),
+        )
+
+    def by_half(u, f):
+        for first in (1, 2):
+
+            @pl.when((u % tiles) % 2 == first - 1)
+            def _(first=first):
+                f(first)
+
+    def start_loads(u):
+        by_half(u, lambda first: [x.start() for x in loads(u, first)])
+
+    def pass_on(u, first):
+        m, t = u // tiles, order(u % tiles)
+        return remote(on_buf.at[u], got2.at[m, tile(t)], s_send.at[u], s_recv.at[u], to[3 - first, 0])
+
+    def second_tile(u):
+        def f(first):
+            for x in loads(u, first):
+                x.wait()
+            on_buf[u] = (load_a[u % 2].astype(f32) + load_b[u % 2].astype(f32)).astype(bf16)
+            pass_on(u, first).start()
+
+        by_half(u, f)
+
+        @pl.when(u + 2 < 3 * tiles)
+        def _():
+            start_loads(u + 2)
+
+    start_loads(0)
+    start_loads(1)
+    load_probs(0).start()
+    gain_query, gain_key = gain_vectors(gains, gain_rows)
+    gain_grads[...] = jnp.zeros_like(gain_grads)
+    dk[...] = jnp.zeros_like(dk)
+    dv[...] = jnp.zeros_like(dv)
+
+    def mixed_rows(i):
+        r = pl.ds(pl.multiple_of(i * 64, 64), 64)
+        x = x2[r]
+        scale = lax.rsqrt(jnp.mean(x * x, axis=-1, keepdims=True) + epsilon)
+        normed = x * scale
+        grad = grad_h2[r].astype(f32)
+        gain_grads[0:1, :] += jnp.sum(grad * normed, axis=0, keepdims=True)
+        n = grad * gain_rows[1:2]
+        d = cot[r].astype(f32) + scale * (n - normed * jnp.mean(n * normed, axis=-1, keepdims=True))
+        dx2[r] = d
+        low[r] = d.astype(bf16)
+
+    def att_grads(j):
+        col = pl.ds(pl.multiple_of(j * 256, 256), 256)
+        datt[:, col] = nn(low[...], wo[:, col]).astype(bf16)
+
+    def unspin(u):
+        return u * cos[...] - pltpu.roll(u, 64, 1) * sin[...]
+
+    def norm_grads(x, rotated, gain, row):
+        scale = lax.rsqrt(jnp.mean(x * x, axis=-1, keepdims=True) + epsilon)
+        normed = x * scale
+        du = unspin(rotated)
+        gain_grads[row : row + 1, 0:128] += jnp.sum(du * normed, axis=0, keepdims=True)
+        n = du * gain
+        return (scale * (n - normed * jnp.mean(n * normed, axis=-1, keepdims=True))).astype(bf16)
+
+    block = rows // 2
+
+    def head(h):
+        load_probs(h).wait()
+
+        @pl.when(h + 1 < n_heads)
+        def _():
+            load_probs(h + 1).start()
+
+        col = pl.ds(pl.multiple_of(h * 128, 128), 128)
+        dq = []
+        for i in range(2):
+            r, n = slice(i * block, (i + 1) * block), (i + 1) * block
+            p_low = pbuf[h % 2, r, 0:n]
+            p = p_low.astype(f32)
+            dp = nt(datt[r, col], value[0:n])
+            ds = (p * (dp - jnp.sum(p * dp, axis=-1, keepdims=True))).astype(bf16)
+            dq.append(nn(ds, krot[0:n]) * rate)
+            dk[0:n] += tn(ds, qrot[r, col])
+            dv[0:n] += tn(p_low, datt[r, col])
+        grad_qkv[:, col] = norm_grads(raw[:, col], jnp.concatenate(dq, 0), gain_query, 1)
+
+    def key_value():
+        grad_qkv[:, pl.ds(q_cols, 128)] = norm_grads(raw[:, pl.ds(q_cols, 128)], dk[...] * rate, gain_key, 2)
+        grad_qkv[:, pl.ds(q_cols + 128, 128)] = dv[...].astype(bf16)
+
+    def input_grads(j):
+        r = pl.ds(pl.multiple_of(j * 256, 256), 256)
+        grad_h1[:, r] = nt(grad_qkv[...], qkv[r]).astype(bf16)
+
+    def work(i):
+        @pl.when(i < 3 * tiles)
+        def _():
+            second_tile(i)
+
+        @pl.when(i < 4)
+        def _():
+            mixed_rows(2 * i)
+            mixed_rows(2 * i + 1)
+
+        @pl.when(i == 4)
+        def _():
+            weights[0].wait()
+
+        @pl.when((i >= 4) & (i < 6))
+        def _():
+            att_grads(2 * (i - 4))
+            att_grads(2 * (i - 4) + 1)
+
+        @pl.when((i >= 6) & (i < 6 + n_heads))
+        def _():
+            head(i - 6)
+
+        @pl.when(i == 6 + n_heads)
+        def _():
+            key_value()
+            weights[1].wait()
+
+        @pl.when((i > 6 + n_heads) & (i <= 10 + n_heads))
+        def _():
+            j = 2 * (i - 7 - n_heads)
+            input_grads(j)
+            input_grads(j + 1)
+
+    def ready(c):
+        @pl.when(c == 0)
+        def _():
+            weights[2].wait()
+
+        give(c).wait_recv()
+        r = pl.ds(pl.multiple_of(c * step, step), step)
+        own_out[r] = (own_out[r].astype(f32) + rbuf[r].astype(f32)).astype(bf16)
+
+    def finish(r, c):
+        done = (x2[r] + summed[r].astype(f32)).astype(bf16)
+        for k in range(4):
+            output[r, pl.ds(pl.multiple_of(places[k] * wide, wide), wide)] = done[:, k * wide : (k + 1) * wide]
+
+    line_sum_work(
+        own_out, in_buf, mid_buf, own_out, summed, line, "tensor", rows, ready, finish, work, 11 + n_heads
+    )
+    over(CHUNKS, lambda i: give(i).wait_send())
+    over(3 * tiles, lambda u: by_half(u, lambda first: pass_on(u, first).wait()))
+
+
+def attention_back_call(grad_h2, x2, cot, qrot, krot, value, raw, gains, cos, sin, probs, wo, qkv, out_part, grads, got):
+    rows, width = x2.shape
+    q_cols, qkv_cols = wo.shape[1], qkv.shape[1]
+    tall = grads.shape[1]
+    wide = width // 4
+    vmem, anyspace = pl.BlockSpec(memory_space=pltpu.VMEM), pl.BlockSpec(memory_space=pl.ANY)
+    shape = jax.ShapeDtypeStruct
+    dma = pltpu.SemaphoreType.DMA
+    tiles = tall // 256
+    big = pltpu.VMEM((rows, width), bf16)
+    return pl.pallas_call(
+        attention_back_kernel,
+        out_shape=[
+            shape((rows, width), bf16),
+            shape((rows, width), f32),
+            shape((rows, width), bf16),
+            shape((rows, qkv_cols), bf16),
+            shape((rows, width), bf16),
+            shape((8, width), f32),
+            shape((3, tall, wide), bf16),
+        ],
+        in_specs=[vmem] * 10 + [anyspace] * 6,
+        out_specs=[vmem] * 6 + [anyspace],
+        scratch_shapes=[
+            pltpu.VMEM((width, q_cols), bf16),
+            pltpu.VMEM((width, qkv_cols), bf16),
+            big, big, big, big, big,
+            pltpu.VMEM((rows, q_cols), bf16),
+            pltpu.VMEM((2, rows, rows), bf16),
+            pltpu.VMEM((rows, 128), f32),
+            pltpu.VMEM((rows, 128), f32),
+            pltpu.VMEM((2, width), f32),
+            pltpu.VMEM((2, 256, wide), bf16),
+            pltpu.VMEM((2, 256, wide), bf16),
+            pltpu.VMEM((3 * tiles, 256, wide), bf16),
+            dma((3,)), dma((2,)), dma((2, 2)), dma((CHUNKS,)), dma((CHUNKS,)), dma((3 * tiles,)), dma((3 * tiles,)),
+        ]
+        + line_sems(),
+        compiler_params=pltpu.CompilerParams(
+            collective_id=3, has_side_effects=True, vmem_limit_bytes=62 * 2**20
+        ),
+        cost_estimate=pl.CostEstimate(flops=9 * 10**9, bytes_accessed=60 * 10**6, transcendentals=10**5),
+        name="attention_backward",
+    )(grad_h2, x2, cot, qrot, krot, value, raw, gains, cos, sin, probs, wo, qkv, out_part, grads, got)
+
+
+def last_kernel(
+    part, dx2, tokens, grad_qkv, low, att, gains, gain_grads,
+    tokens_grad, qkv_shard, wo_shard, gain_sum,
+    h1, in_buf, mid_buf, half_sum, summed, gain_rows, wo_all, qkv_all, wo_core, qkv_core, wo_one, qkv_one, wo_two, qkv_two,
+    ga, z_got, g_out, g_got,
+    z_send, z_recv, c_send, c_recv, f_send, f_recv, t_send, t_recv, g_send, g_recv, *line,
+):
+    c = lax.axis_index("expert")
+    to = plane_partners()
+    zs = z_partners()
+    others = plane_barrier(to, zs)
+    places = [to[k, 0]["dp"] for k in range(4)]
+    rows, width = tokens.shape
+    wide = width // 4
+    piece = wide // 2
+    half = piece // 2
+
+    def z_move(j):
+        return remote(gain_grads.at[pl.ds(0, 8), pl.ds(0, 128)], z_got.at[j], z_send.at[j], z_recv.at[j], {"tensor": zs[j]})
+
+    for j in range(3):
+        z_move(j).start()
+    gain_vectors(gains, gain_rows)
+    ga[...] = jnp.zeros_like(ga)
+
+    def unit_rows(r):
+        x = tokens[r].astype(f32)
+        scale = lax.rsqrt(jnp.mean(x * x, axis=-1, keepdims=True) + epsilon)
+        return x * scale, scale
+
+    def hidden_one(i):
+        r = pl.ds(pl.multiple_of(i * 64, 64), 64)
+        h1[r] = (unit_rows(r)[0] * gain_rows[0:1]).astype(bf16)
+
+    mats = [
+        (low, att, wo_all, wo_core, wo_one, wo_two),
+        (h1, grad_qkv, qkv_all, qkv_core, qkv_one, qkv_two),
+    ]
+
+    def block(k, core):
+        return pl.ds(pl.multiple_of((k * 2 + core) * piece, piece), piece)
+
+    def core_move(m, k):
+        return remote(mats[m][2].at[block(k, 1 - c)], mats[m][3].at[k], c_send.at[m, k], c_recv.at[m, k], to[0, 1])
+
+    def product(m, k, core):
+        left, right, full = mats[m][:3]
+        full[block(k, core)] = tn(left[:, block(k, core)], right[...]).astype(bf16)
+
+    def away(k):
+        for m in range(2):
+            product(m, k, 1 - c)
+            core_move(m, k).start()
+
+    def home(k):
+        for m in range(2):
+            product(m, k, c)
+            full, came = mats[m][2:4]
+            core_move(m, k).wait_recv()
+            full[block(k, c)] = (full[block(k, c)].astype(f32) + came[k].astype(f32)).astype(bf16)
+
+    def slot(m, k, h):
+        return mats[m][2].at[pl.ds(pl.multiple_of((k * 2 + c) * piece + h * half, half), half)]
+
+    def first_move(m, h, j):
+        way = 1 + h
+        src = slot(m, 3 if j else way, h)
+        return remote(src, mats[m][4].at[h, j], f_send.at[m, h, j], f_recv.at[m, h, j], to[way, 0])
+
+    def second_move(m, h):
+        return remote(slot(m, 2 - h, h), mats[m][5].at[h], t_send.at[m, h], t_recv.at[m, h], to[2 - h, 0])
+
+    def add_first(m, h, j, k):
+        full, one = mats[m][2], mats[m][4]
+        r = pl.ds(pl.multiple_of((k * 2 + c) * piece + h * half, half), half)
+        first_move(m, h, j).wait_recv()
+        full[r] = (full[r].astype(f32) + one[h, j].astype(f32)).astype(bf16)
+
+    def work(i):
+        @pl.when(i == 0)
+        def _():
+            over(rows // 64, hidden_one)
+
+        for n, k in enumerate((3, 1, 2, 0)):
+
+            @pl.when(i == 1 + n)
+            def _(k=k):
+                away(k)
+
+            @pl.when(i == 5 + n)
+            def _(k=k, n=n):
+                home(k)
+                if n in (1, 2):
+                    for m in range(2):
+                        for j in range(2):
+                            first_move(m, n - 1, j).start()
+
+        for h in range(2):
+
+            @pl.when(i == 17 + h)
+            def _(h=h):
+                for m in range(2):
+                    add_first(m, h, 1, 2 - h)
+                    second_move(m, h).start()
+
+    def finish(r, i):
+        grad = summed[r].astype(f32)
+        normed, scale = unit_rows(r)
+        ga[0:1, :] += jnp.sum(grad * normed, axis=0, keepdims=True)
+        n = grad * gain_rows[0:1]
+        d = dx2[r] + scale * (n - normed * jnp.mean(n * normed, axis=-1, keepdims=True))
+        for k in range(4):
+            tokens_grad[r, pl.ds(pl.multiple_of(places[k] * wide, wide), wide)] = d[:, k * wide : (k + 1) * wide]
+
+    line_sum_work(part, in_buf, mid_buf, half_sum, summed, line, "tensor", rows, lambda k: None, finish, work, 20)
+
+    head_rows = gain_grads[1:3, 0:128]
+    for j in range(3):
+        z_move(j).wait()
+        head_rows += z_got[j, 1:3]
+    for kd in range(4):
+        for kc in range(2):
+            for j in range(2):
+                col = slice((kd * 2 + kc) * piece + j * 128, (kd * 2 + kc) * piece + (j + 1) * 128)
+                g_out[kd, kc, j : j + 1] = ga[0:1, col]
+                g_out[kd, kc, 2 + j : 3 + j] = gain_grads[0:1, col]
+            g_out[kd, kc, 4:6] = head_rows
+
+    def gain_move(j):
+        kd, kc = others[j]
+        core = c if kc == 0 else 1 - c
+        return remote(g_out.at[kd, core], g_got.at[j], g_send.at[j], g_recv.at[j], to[kd, kc])
+
+    for j in range(len(others)):
+        gain_move(j).start()
+    for m, shard in ((0, wo_shard), (1, qkv_shard)):
+        full, two = mats[m][2], mats[m][5]
+        for h in range(2):
+            add_first(m, h, 0, 0)
+            second_move(m, h).wait_recv()
+            r = pl.ds(pl.multiple_of(c * piece + h * half, half), half)
+            shard[h * half : (h + 1) * half] = full[r].astype(f32) + two[h].astype(f32)
+    total = g_out[0, pl.ds(c, 1)].reshape(8, 128)
+    for j in range(len(others)):
+        gain_move(j).wait_recv()
+        total += g_got[j]
+    gain_sum[...] = total
+    for m in range(2):
+        for k in range(4):
+            core_move(m, k).wait_send()
+        for h in range(2):
+            for j in range(2):
+                first_move(m, h, j).wait_send()
+            second_move(m, h).wait_send()
+    for j in range(len(others)):
+        gain_move(j).wait_send()
+
+
+def last_call(part, dx2, tokens, grad_qkv, low, att, gains, gain_grads):
+    rows, width = tokens.shape
+    q_cols, qkv_cols = att.shape[1], grad_qkv.shape[1]
+    piece = width // 8
+    vmem = pl.BlockSpec(memory_space=pltpu.VMEM)
+    shape = jax.ShapeDtypeStruct
+    dma = pltpu.SemaphoreType.DMA
+    big = pltpu.VMEM((rows, width), bf16)
+    both = lambda *lead: [pltpu.VMEM(lead + (n,), bf16) for n in (q_cols, qkv_cols)]
+    return pl.pallas_call(
+        last_kernel,
+        out_shape=[
+            shape((rows, width), f32),
+            shape((piece, qkv_cols), f32),
+            shape((piece, q_cols), f32),
+            shape((8, 128), f32),
+        ],
+        in_specs=[vmem] * 8,
+        out_specs=[vmem] * 4,
+        scratch_shapes=[big, big, big, big, big, pltpu.VMEM((2, width), f32)]
+        + both(width)
+        + both(4, piece)
+        + both(2, 2, piece // 2)
+        + both(2, piece // 2)
+        + [
+            pltpu.VMEM((8, width), f32),
+            pltpu.VMEM((3, 8, 128), f32),
+            pltpu.VMEM((4, 2, 8, 128), f32),
+            pltpu.VMEM((7, 8, 128), f32),
+            dma((3,)), dma((3,)), dma((2, 4)), dma((2, 4)), dma((2, 2, 2)), dma((2, 2, 2)), dma((2, 2)), dma((2, 2)),
+            dma((7,)), dma((7,)),
+        ]
+        + line_sems(),
+        compiler_params=pltpu.CompilerParams(
+            collective_id=4, has_side_effects=True, vmem_limit_bytes=62 * 2**20
+        ),
+        cost_estimate=pl.CostEstimate(flops=5 * 10**9, bytes_accessed=40 * 10**6, transcendentals=10**5),
+        name="input_gradients",
+    )(part, dx2, tokens, grad_qkv, low, att, gains, gain_grads)
+
+
 def local_fast(
     tokens,
     cotangent,
@@ -783,11 +1523,6 @@
         sin2,
         key_ok,
     )
-    gain_attention = gains[:, :, 0:2].reshape(-1)
-    gain_experts = gains[:, :, 2:4].reshape(-1)
-    gain_query = jnp.sum(gains[:, :, 4], (0, 1))
-    gain_key = jnp.sum(gains[:, :, 5], (0, 1))
-
     experts = jnp.arange(group * n_ex, dtype=jnp.int32)
     table = jnp.zeros((rows, group * n_ex), f32)
     for c in range(route_ids.shape[1]):
@@ -796,150 +1531,34 @@
         )
     table = jnp.concatenate(xor_gather(table, "expert"), 0)
     mine = lax.dynamic_slice_in_dim(table, me_ex * group, group, 1)
-    unit_expert = jnp.arange(flat, dtype=jnp.int32) // hidden
-    route_scale = jnp.zeros((table.shape[0], flat), f32)
-    for j in range(group):
-        route_scale = route_scale + jnp.where(unit_expert[None, :] == j, mine[:, j, None], 0.0)
-
-    scale_one = rms_scale(inputs)
-    normed_one = inputs * scale_one
-    first_hidden = (normed_one * gain_attention).astype(bf16)
+    mine = jnp.pad(mine, ((0, 0), (0, 128 - group)))
     upstream_low = lane(cotangent)
     upstream_all = jnp.concatenate(xor_gather(upstream_low, "expert"), 0)
 
-    query_raw = raw[:, :q_cols].reshape(rows, heads_query, HEAD_SIZE)
-    key_raw = raw[:, q_cols : q_cols + k_cols].reshape(rows, heads_key, HEAD_SIZE)
-    value_low = value_low.reshape(rows, heads_key, HEAD_SIZE)
-    rotated_query = rotated_query.reshape(rows, heads_key, per_group, HEAD_SIZE)
-    key_rot = key_rot.reshape(rows, heads_key, HEAD_SIZE)
-    prob_low = prob_low[None]
-    probs = prob_low.astype(f32)
-    scale_query = rms_scale(query_raw)
-    normed_query = query_raw * scale_query
-    scale_key = rms_scale(key_raw)
-    normed_key = key_raw * scale_key
-    scale_two = rms_scale(mixed_rows)
-    normed_two = mixed_rows * scale_two
-
-    gate_value = dotf(hidden_all, gate_full, ((1,), (1,)))
-    up_value = dotf(hidden_all, up_full, ((1,), (1,)))
-    grad_act = lax.optimization_barrier(dotf(upstream_all, down_full, ((1,), (1,)))) * route_scale
-    sigmoid_gate = jax.nn.sigmoid(gate_value)
-    scaled_act = (gate_value * sigmoid_gate * up_value * route_scale).astype(bf16)
-    grad_up_low = (grad_act * gate_value * sigmoid_gate).astype(bf16)
-    grad_gate_low = (
-        grad_act * up_value * sigmoid_gate * (1.0 + gate_value * (1.0 - sigmoid_gate))
-    ).astype(bf16)
-    grad_rows = jnp.dot(grad_gate_low, gate_full, preferred_element_type=f32)
-    grad_rows = (grad_rows + jnp.dot(grad_up_low, up_full, preferred_element_type=f32)).astype(bf16)
-    grad_hidden_two = xor_scatter(jnp.split(grad_rows, n_ex, 0), "expert")
-    grad_hidden_two = lax.psum(grad_hidden_two, "tensor")
-
-    expert_out = jnp.dot(scaled_act, down_full, preferred_element_type=f32).astype(bf16)
-    combined = xor_scatter(jnp.split(expert_out, n_ex, 0), "expert")
-    def expert_grad(low, acts):
-        return dotf(low, acts, ((0,), (0,))).astype(bf16)
-
-    grads = [
-        expert_grad(scaled_act, upstream_all),
-        expert_grad(grad_gate_low, hidden_all),
-        expert_grad(grad_up_low, hidden_all),
-    ]
-    grad_hidden_two, grads = lax.optimization_barrier((grad_hidden_two, grads))
-    down_shard, gate_shard, up_shard = (
-        dp_scatter(jnp.split(g, n_dp, 1)).reshape(group, hidden, part) for g in grads
-    )
-    combined, grad_hidden_two = lax.optimization_barrier((combined, grad_hidden_two))
-    combined = lax.psum(combined, "tensor")
-    output = lane((mixed_rows + combined.astype(f32)).astype(bf16))
-    grad_hidden_two = grad_hidden_two.astype(f32)
-
-    def attention_scatter(grad):
-        grad = grad.reshape(n_dp, n_ex, width // (n_dp * n_ex), grad.shape[1])
-        if n_ex == 2:
-            away = lax.dynamic_index_in_dim(grad, 1 - me_ex, 1, keepdims=False)
-            own = lax.dynamic_index_in_dim(grad, me_ex, 1, keepdims=False)
-            grad = (own.astype(f32) + flip(away, "expert", 1).astype(f32)).astype(bf16)
-        else:
-            grad = lax.psum_scatter(grad, "expert", scatter_dimension=1, tiled=False)
-        return dp_scatter(list(grad))
-
-    upstream = upstream_low.astype(f32)
-    experts_gain_grad = jnp.sum(grad_hidden_two * normed_two, axis=0)
-    grad_mixed = upstream + norm_back(grad_hidden_two, normed_two, scale_two, gain_experts)
-    grad_proj_low = grad_mixed.astype(bf16)
-    grad_att_low = (
-        jnp.dot(grad_proj_low, full_output, preferred_element_type=f32)
-        .astype(bf16)
-        .reshape(rows, heads_key, per_group, HEAD_SIZE)
-    )
-    output_grad = dotf(grad_proj_low, attended_low, ((0,), (0,))).astype(bf16)
-    output_shard = attention_scatter(output_grad)
-    grad_probs = jnp.einsum("qkgd,skd->kgqs", grad_att_low, value_low, preferred_element_type=f32)
-    row_dot = jnp.sum(probs * grad_probs, axis=-1, keepdims=True)
-    grad_scores = (probs * (grad_probs - row_dot)).astype(bf16)
-    grad_value = jnp.einsum("kgqs,qkgd->skd", prob_low, grad_att_low, preferred_element_type=f32)
-    grad_qrot = jnp.einsum(
-        "kgqs,skd->qkgd", grad_scores, key_rot, preferred_element_type=f32
-    ) * HEAD_SIZE ** (-0.5)
-    grad_krot = jnp.einsum(
-        "kgqs,qkgd->skd", grad_scores, rotated_query, preferred_element_type=f32
-    ) * HEAD_SIZE ** (-0.5)
-    grad_qrot = grad_qrot.reshape(rows, heads_query, HEAD_SIZE)
-    grad_query_normed = rotate(grad_qrot, cosine_table, -sine_table)
-    query_gain_grad = jnp.sum(grad_query_normed * normed_query, axis=(0, 1))
-    grad_query_low = (
-        norm_back(grad_query_normed, normed_query, scale_query, gain_query)
-        .astype(bf16)
-        .reshape(rows, q_cols)
-    )
-    grad_key_normed = rotate(grad_krot, cosine_table, -sine_table)
-    key_gain_grad = jnp.sum(grad_key_normed * normed_key, axis=(0, 1))
-    grad_key_low = (
-        norm_back(grad_key_normed, normed_key, scale_key, gain_key).astype(bf16).reshape(rows, k_cols)
-    )
-    grad_value_low = grad_value.astype(bf16).reshape(rows, k_cols)
-    grad_qkv_low = jnp.concatenate([grad_query_low, grad_key_low, grad_value_low], 1)
-    grad_hidden_one = dotf(grad_qkv_low, full_qkv, ((1,), (1,)))
-    head_gain_grads = jnp.stack([query_gain_grad, key_gain_grad]).astype(bf16)
-    grad_hidden_one, head_gain_grads, _ = lax.optimization_barrier(
-        (grad_hidden_one.astype(bf16), head_gain_grads, combined)
-    )
-    grad_hidden_one, head_gain_grads = lax.psum((grad_hidden_one, head_gain_grads), "tensor")
-    grad_hidden_one = grad_hidden_one.astype(f32)
-    qkv_grad = dotf(first_hidden, grad_qkv_low, ((0,), (0,))).astype(bf16)
-    qkv_shard = attention_scatter(qkv_grad)
-    attention_gain_grad = jnp.sum(grad_hidden_one * normed_one, axis=0)
-    tokens_grad = grad_mixed + norm_back(grad_hidden_one, normed_one, scale_one, gain_attention)
-    tokens_grad = lane(tokens_grad)
-
-    blocks = lambda v: v.reshape(n_dp, n_ex, -1)
-    gain_grads = jnp.concatenate(
-        [
-            blocks(attention_gain_grad),
-            blocks(experts_gain_grad),
-            lane(blocks(head_gain_grads[0].astype(f32)), 0),
-            lane(blocks(head_gain_grads[1].astype(f32)), 0),
-        ],
-        2,
-    )
-    gain_grads = lane_order(gain_grads, 1, n_ex, me_ex)
-    gain_grads = jnp.pad(gain_grads, ((0, 0), (0, 0), (0, -gain_grads.shape[2] % 128)))
-    gain_grads = gain_grads.reshape(n_dp, n_ex, -1, 128)
-    gain_grads = xor_scatter([gain_grads[:, k] for k in range(n_ex)], "expert")
-    gain_grads = xor_scatter([gain_grads[k] for k in range(n_dp)], "dp").reshape(-1)
-    take = lambda start, size: gain_grads[start : start + size]
+    grad_hidden_two, expert_out, grads, got = expert_call(
+        hidden_all, upstream_all, mine, gate_full, up_full, down_full
+    )
+    output, grad_mixed, grad_proj_low, grad_qkv_low, grad_hidden_one, gain_grads, got2 = attention_back_call(
+        grad_hidden_two, mixed_rows, upstream_low, rotated_query, key_rot, value_low, raw, gains, cos2, sin2,
+        prob_low, full_output, full_qkv, expert_out, grads, got,
+    )
+    tokens_grad, qkv_shard, output_shard, gain_sum = last_call(
+        grad_hidden_one, grad_mixed, inputs_low, grad_qkv_low, grad_proj_low, attended_low, gains, gain_grads
+    )
+    shards = grads[:, :, :part].astype(f32) + got[:, :, :part].astype(f32) + got2.astype(f32)
+    down_shard, gate_shard, up_shard = (x.reshape(group, hidden, part) for x in shards)
+    own_head = lambda row: lax.dynamic_slice_in_dim(gain_sum[row], own_place, nq, 0)
     return (
         output,
         tokens_grad,
-        take(0, na),
+        gain_sum[0:2].reshape(-1),
         qkv_shard[:, :q_cols],
         qkv_shard[:, q_cols : q_cols + k_cols],
         qkv_shard[:, q_cols + k_cols :],
         output_shard,
-        take(2 * na, nq),
-        take(2 * na + nq, nq),
-        take(na, na),
+        own_head(4),
+        own_head(5),
+        gain_sum[2:4].reshape(-1),
         gate_shard,
         up_shard,
         down_shard,

time: 772 us -> 581 us (0.75)
  Pallas kernels: 210 us -> 520 us
  waiting for transfers between devices: 209 us -> 0.01 us
  matrix products: 136 us -> 0 us
  other arithmetic: 108 us -> 24.7 us
  starting transfers between devices: 26.8 us -> 0.64 us
  local copies, waits for them, and re-layouts: 50.1 us -> 26 us
  between operations: 15.9 us -> 2.08 us
  blocking collectives: 10.8 us -> 0 us
    pallas_call x0 -> x3, Pallas kernels: none -> 311 us  [the longest x1 152 us: expert_call(): pl.pallas_call(expert_kernel, out_shape=[shape((rows, width), bf16), shap...]
    ppermute x30 -> x2, waiting for transfers between devices: 157 us -> 0.01 us  [flip(): return lax.ppermute(x, axis, [(i, i ^ bit) for i in range(n)])]
    dot_general x17 -> x0, matrix products: 136 us -> none  [the longest x9 95.6 us: dotf(): return lax.dot_general(a, b, (dims, ((), ())), preferred_element_type=f32)]
    psum x3 -> x0, waiting for transfers between devices: 51.3 us -> none  [the longest x1 51.3 us: local_fast(): grad_hidden_two = lax.psum(grad_hidden_two, 'tensor')]
    convert_element_type x12 -> x0, other arithmetic: 29.4 us -> none  [the longest x1 12.4 us: local_fast(): grad_up_low = (grad_act * gate_value * sigmoid_gate).astype(bf16)]
    ppermute x30 -> x2, starting transfers between devices: 26.7 us -> 0.64 us  [flip(): return lax.ppermute(x, axis, [(i, i ^ bit) for i in range(n)])]
    add x15 -> x1, other arithmetic: 27.2 us -> 7.15 us  [local_fast(): grads[:, :, :part].astype(f32) + got[:, :, :part].astype(f32)]
    reduce_sum x10 -> x0, other arithmetic: 16 us -> none  [the longest x4 5.23 us: rms_scale(): jnp.mean(values * values, axis=-1, keepdims=True) + epsilon]
  transfers between devices with their start and end apart: 33 -> 2, of which waited for: 15 -> 0; matrix products, arithmetic and copies ran while one was open for 29% -> 3% of each run, Pallas kernels for 27% -> 37%
where the time goes in v1:
time: 581 us; the launch traced here: 574 us
  Pallas kernels  520 us (90%)
  local copies, waits for them, and re-layouts  26 us (4%)
  other arithmetic  24.7 us (4%)
    pallas_call x1, Pallas kernels, forward_call(): pl.pallas_call(forward_kernel, out_shape=[o[0] for o in outs], in_specs=[...  210 us
    pallas_call x1, Pallas kernels, expert_call(): pl.pallas_call(expert_kernel, out_shape=[shape((rows, width), bf16), shap...  152 us
    pallas_call x1, Pallas kernels, last_call(): pl.pallas_call(last_kernel, out_shape=[shape((rows, width), f32), shape((...  81.1 us
    pallas_call x1, Pallas kernels, attention_back_call(): pl.pallas_call(attention_back_kernel, out_shape=[shape((rows, width), bf1...  77.9 us
  transfers between devices with their start and end apart: 2, of which 0 were waited for; matrix products, arithmetic and copies ran while one was open for 3% of the time, Pallas kernels for 37%

profile of v1, /device:TPU:0, one launch (start us, length us, event | category | flops | bytes accessed | tf_op | source)
XLA Modules:
  0.0 573.6 jit_solution(3426211693295898076)
XLA Ops:
  0.6 1.0 fusion.8
  1.7 1.0 fusion.9
  2.7 0.5 collective-permute-start.1
  3.3 3.8 constant_dynamic-slice_fusion.5
  7.1 0.0 copy-start.8
  7.1 0.0 copy-start.9
  7.1 0.0 copy-start.11
  7.1 0.0 copy-start.6
  7.1 0.0 copy-start.7
  7.1 0.7 copy-done.1
  7.8 0.3 pad_maximum_fusion.2.cot
  8.1 0.0 copy-done.2
  8.2 0.0 copy-start
  8.2 0.1 collective-permute-start
  8.3 0.0 copy-done.10
  8.3 0.0 copy-done.8
  8.3 0.0 copy-done.9
  8.3 0.0 copy-done.11
  9.0 0.1 dynamic_update_slice.8
  9.2 0.1 dynamic_update_slice.9
  9.4 0.6 concatenate.26.gains_own
  10.0 0.6 compare_convert_fusion.key_ok
  10.6 1.0 fusion.2
  11.6 1.0 pad_maximum_fusion.4
  12.6 0.0 copy-done.6
  12.6 0.0 copy-done.7
  12.6 1.9 pad_maximum_fusion.3.qkv_own
  14.5 3.1 pad_maximum_fusion.1.tokens
  17.6 209.5 %forward_to_experts.1 = (f32[512,2048]{1,0:T(8,128)}, bf16[1024,2048]{1,0:T(8,128)(2,1)}, bf16[512,1024]{1,0:T(8,128)(2,1)}, bf16[512,1024]{1,0:T(8,128)(2,1)}, ...) custom-call(bf16[512,2048]{1,0:T(8,128)(2,1)} %pad_maximum_fusion.1., ...), custom_call_target="tpu_custom_call" | custom-call | flops 8000000000 | bytes 60000000 | tf_op jit(solution)/shard_map/forward_to_experts/pallas_call | solution.py:700
  227.1 0.0 collective-permute-done.1
  227.2 1.0 copy.30
  228.2 1.9 pad.4.mine
  230.0 0.0 collective-permute-done
  230.0 9.6 %pad_maximum_fusion.g = bf16[1024,2048]{1,0:T(8,128)(2,1)} fusion(bf16[512,2048]{1,0:T(8,128)(2,1)} %collective-permute-done, bf16[512,512]{1,0:T(8,128)(2,1)} %copy-done.1, bf16[512,512]{1,0:T(8,128)(2,1)} %copy-done.2, bf16[512,512]{1,0:T(8,128)(2,1)S(1)} %get-tuple-element.75, bf16[512,512]{1,0:T(8,128)(2,1)S(1)} %get-tuple-element.74), kind=kLoop, calls=%fused_computation.1 | loop fusion | flops 20971520 | bytes 8388608 | tf_op jit(solution)/shard_map/concatenate | solution.py:1536
  239.6 151.7 %experts.1 = (bf16[512,2048]{1,0:T(8,128)(2,1)}, bf16[1024,2048]{1,0:T(8,128)(2,1)}, bf16[3,1536,2048]{2,1,0:T(8,128)(2,1)}, bf16[3,1536,1024]{2,1,0:T(8,128)(2,1)}) custom-call(bf16[1024,2048]{1,0:T(8,128)(2,1)} %get-tuple-element.42.h2, bf16[1024,2048]{1,0:T(8,128)(2,1)} %pad_maximum_fusion.g, f32[1024,128]{1,0:T(8,128)} %pad.4.mine, ...), custom_call_target="tpu_custom_call" | custom-call | flops 57999998976 | bytes 60000000 | tf_op jit(solution)/shard_map/experts/pallas_call | solution.py:965
  391.3 77.9 %attention_backward.1 = (bf16[512,2048]{1,0:T(8,128)(2,1)}, f32[512,2048]{1,0:T(8,128)}, bf16[512,2048]{1,0:T(8,128)(2,1)}, bf16[512,1280]{1,0:T(8,128)(2,1)}, b...) custom-call(bf16[512,2048]{1,0:T(8,128)(2,1)} %get-tuple-element.46.grad_h2, ...), custom_call_target="tpu_custom_call" | custom-call | flops 8999999488 | bytes 60000000 | tf_op jit(solution)/shard_map/attention_backward/pallas_call | solution.py:1226
  469.2 81.1 %input_gradients.1 = (f32[512,2048]{1,0:T(8,128)}, f32[256,1280]{1,0:T(8,128)}, f32[256,1024]{1,0:T(8,128)}, f32[8,128]{1,0:T(8,128)}) custom-call(bf16[512,2048]{1,0:T(8,128)(2,1)} %get-tuple-element.60.part, f32[512,2048]{1,0:T(8,128)} %get-tuple-element.61.dx2, bf16[512,2048]{1,0:T(8,128)(2,1)} %pad_maximum_fusion.1.tokens, ...), custom_call_target="tpu_custom_call" | custom-call | flops 5000000000 | bytes 40000000 | tf_op jit(solution)/shard_map/input_gradients/pallas_call | solution.py:1429
  550.4 0.8 fusion.10
  551.1 1.3 slice_bitcast_fusion
  552.4 1.7 fusion.7
  554.1 2.3 slice.92
  556.4 7.2 %convert_add_fusion = f32[3,1536,512]{2,1,0:T(8,128)S(1)} fusion(bf16[3,1536,512]{2,1,0:T(8,128)(2,1)} %get-tuple-element.70, bf16[3,1536,1024]{2,1,0:T(8,128)(2,1)} %get-tuple-element.58.got, bf16[3,1536,2048]{2,1,0:T(8,128)(2,1)} %get-tuple-element.57.grads), kind=kLoop, calls=%fused_computation | loop fusion | flops 11796480 | bytes 23592960 | tf_op jit(solution)/shard_map/add | solution.py:1548
  563.6 4.0 fusion.6
  567.6 0.6 fusion.5
  568.2 0.6 fusion.4
  568.8 1.3 copy.38
  570.1 2.0 copy.39
  572.1 1.0 copy.40
  (19 shorter events, 0.1 us)
Async XLA Ops:
  2.7 224.4 %collective-permute-start.1 = (f32[512,16]{0,1:T(8,128)S(1)}, f32[512,16]{0,1:T(8,128)S(1)}, u32[]{:S(2)}, u32[]{:S(2)}) collective-permute-start(f32[512,16]{0,1:T(8,128)S(1)} %select_add_fusion), channel_id=1, source_target_pairs={{0,4},{4,0},{1,5},{5,1},{2,6},{6,2},{3,7},{7,3},{8,12},{12,8},{9,1... | collective-permute-start | bytes 98312 | tf_op jit(solution)/shard_map/ppermute | solution.py:47
  7.0 0.8 copy-start.1
  7.0 1.1 copy-start.2
  7.0 1.2 copy-start.10
  7.1 1.2 copy-start.8
  7.1 1.2 copy-start.9
  7.1 1.2 copy-start.11
  7.1 5.5 copy-start.6
  7.1 5.5 copy-start.7
  8.2 219.0 %copy-start = (bf16[512,2048]{1,0:T(8,128)(2,1)}, bf16[512,2048]{1,0:T(8,128)(2,1)S(1)}, u32[]{:S(2)}) copy-start(bf16[512,2048]{1,0:T(8,128)(2,1)S(1)} %pad_maximum_fusion.2.cot) | copy-start | bytes 6291460
  8.2 221.9 %collective-permute-start = (bf16[512,2048]{1,0:T(8,128)(2,1)S(1)}, bf16[512,2048]{1,0:T(8,128)(2,1)}, u32[]{:S(2)}, u32[]{:S(2)}) collective-permute-start(bf16[512,2048]{1,0:T(8,128)(2,1)S(1)} %pad_maximum_fusion.2.cot), channel_id=1, source_target_pairs={{0,4},{4,0},{1,5},{5,1},{2,6},{6,2},{3,7},{7,3},{8,12},{12,8},{9,1... | collective-permute-start | bytes 6291464 | tf_op jit(solution)/shard_map/ppermute | solution.py:47
  563.6 5.2 copy-start.4
  567.6 2.5 copy-start.3
  570.1 2.0 copy-start.5

commit v2 on v1

--- a/solution.py
+++ b/solution.py
@@ -448,6 +448,17 @@
     return {(kd, kc): {"dp": ds[kd], "expert": cs[kc]} for kd in ds for kc in cs}
 
 
+def lane_copies(src, dst, sems, to):
+    wide = src.shape[1] // 4
+    places = [to[k, 0]["dp"] for k in range(4)]
+    return [
+        pltpu.make_async_copy(
+            src.at[:, pl.ds(pl.multiple_of(places[k] * wide, wide), wide)], dst.at[:, pl.ds(k * wide, wide)], sems[k]
+        )
+        for k in range(4)
+    ]
+
+
 def remote(src, dst, send, recv, to):
     return pltpu.make_async_remote_copy(src, dst, send, recv, device_id=to, device_id_type=MESH)
 
@@ -465,10 +476,10 @@
 
 
 def forward_kernel(
-    tokens, qkv_own, wo_own, gate_own, up_own, down_own, gains_own, cos, sin, key_ok,
-    x2, h2, att, qrot, krot, value, raw, probs, gains, gate, up, down, qkv_out, wo_out,
+    tokens_in, cot_in, ids, weight, q_own, k_own, v_own, wo_own, gate_own, up_own, down_own, gains_own, cos, sin, key_ok,
+    tokens, cot, table, x2, h2, att, qrot, krot, value, raw, probs, gains, gate, up, down, qkv_out, wo_out,
     qkv, wo, h1, proj, in_buf, mid_buf, part, summed, gain_rows,
-    w_send, w_recv, core_send, core_recv, g_send, g_recv, h_send, h_recv, own_sem, out_sem, *line,
+    w_send, w_recv, core_send, core_recv, g_send, g_recv, h_send, h_recv, own_sem, out_sem, r_send, r_recv, t_sem, *line,
 ):
     c = lax.axis_index("expert")
     to = plane_partners()
@@ -489,22 +500,40 @@
         pl.semaphore_wait(barrier, len(others) + 1)
 
     rows, width = tokens.shape
-    piece = qkv_own.shape[0]
+    piece = wo_own.shape[0]
     half = piece // 2
     tall = gate_own.shape[0] // 2
     wide = gate_own.shape[1]
+    q_cols, k_cols = q_own.shape[1], k_own.shape[1]
+    places = [to[k, 0]["dp"] for k in range(4)]
+
+    def lanes(k):
+        return pl.ds(pl.multiple_of(places[k] * wide, wide), wide)
+
+    fetch = lane_copies(tokens_in, tokens, [t_sem.at[k] for k in range(4)], to)
+
+    def cot_away(k):
+        dst = cot.at[:, pl.ds(k * wide, wide)]
+        return remote(cot_in.at[:, lanes(k)], dst, r_send.at[k], r_recv.at[k], to[0, 1])
+
+    def table_away():
+        return remote(
+            table.at[pl.ds(0, rows)], table.at[pl.ds(rows, rows)], r_send.at[4], r_recv.at[4], to[0, 1]
+        )
 
     def small_slot(full):
         return lambda k, h: full.at[pl.ds(pl.multiple_of((k * 2 + c) * piece + h * half, half), half)]
 
+    early = tall // 3 * 2
+
     def big_slot(full):
-        return lambda k, h: full.at[pl.ds(h * tall, tall), pl.ds(k * wide, wide)]
+        return lambda k, h: full.at[pl.ds(h * tall, early), pl.ds(k * wide, wide)]
 
     mats = [
-        (lambda h: qkv_own.at[pl.ds(h * half, half)], small_slot(qkv)),
+        (lambda h: small_slot(qkv)(0, h), small_slot(qkv)),
         (lambda h: wo_own.at[pl.ds(h * half, half)], small_slot(wo)),
     ] + [
-        (lambda h, own=own: own.at[pl.ds(h * tall, tall)], big_slot(full))
+        (lambda h, own=own: own.at[pl.ds(h * tall, early)], big_slot(full))
         for own, full in ((gate_own, gate), (up_own, up), (down_own, down))
     ]
 
@@ -538,22 +567,35 @@
         kd, kc = others[j]
         return remote(gains_own, gains.at[kd, c], g_send.at[j], g_recv.at[j], to[kd, kc])
 
+    own_rows = pl.ds(pl.multiple_of(c * piece, piece), piece)
+    own_qkv = [
+        pltpu.make_async_copy(own, qkv.at[own_rows, pl.ds(col, own.shape[1])], own_sem.at[5 + i])
+        for i, (own, col) in enumerate(((q_own, 0), (k_own, q_cols), (v_own, q_cols + k_cols)))
+    ]
     own_copies = [
-        pltpu.make_async_copy(qkv_own, qkv.at[pl.ds(pl.multiple_of(c * piece, piece), piece)], own_sem.at[0]),
+        None,
         pltpu.make_async_copy(wo_own, wo.at[pl.ds(pl.multiple_of(c * piece, piece), piece)], own_sem.at[1]),
-    ] + [
-        pltpu.make_async_copy(own, full.at[:, pl.ds(0, wide)], own_sem.at[2 + i])
-        for i, (own, full) in enumerate(((gate_own, gate), (up_own, up), (down_own, down)))
     ]
 
+    for x in own_qkv + [own_copies[1]] + fetch:
+        x.start()
+    for k in range(4):
+        cot_away(k).start()
+    for x in own_qkv:
+        x.wait()
     begin(0)
     for j in range(len(others)):
         gain_move(j).start()
-    own_copies[0].start()
-    own_copies[1].start()
     gains[pl.ds(0, 1), pl.ds(c, 1)] = gains_own[...].reshape(1, 1, 8, 128)
-    own_copies[0].wait()
     core_move(0, 0).start()
+    lane_index = lax.broadcasted_iota(jnp.int32, (rows, 128), 1)
+    routes = jnp.zeros((rows, 128), f32)
+    for j in range(ids.shape[1]):
+        routes += jnp.where(lane_index == ids[:, j : j + 1], weight[:, j : j + 1], 0.0)
+    table[0:rows] = routes
+    table_away().start()
+    for k in range(4):
+        fetch[k].wait()
     own_copies[1].wait()
     core_move(1, 0).start()
     for j in range(len(others)):
@@ -585,7 +627,6 @@
     pass_on(1)
     for m in (2, 3, 4):
         begin(m)
-        own_copies[m].start()
     for k in range(4):
         core_move(0, k).wait_recv()
     save_qkv = pltpu.make_async_copy(qkv, qkv_out, out_sem.at[0])
@@ -596,7 +637,6 @@
         raw[:, col] = nn(h1[...], qkv[:, col])
 
     over(qkv.shape[1] // 256, project)
-    q_cols = att.shape[1]
 
     def spin(u):
         return u * cos[...] + pltpu.roll(u, 64, 1) * sin[...]
@@ -624,7 +664,6 @@
         probs[h, 0:block, block:] = jnp.zeros((block, block), bf16)
 
     over(q_cols // 128, head)
-
     for k, waits in ((1, (3,)), (2, (2,)), (3, (4, 5))):
         for i in waits:
             move(1, i).wait_recv()
@@ -660,9 +699,11 @@
     over(CHUNKS, lambda i: give(i).wait())
     for m in (2, 3, 4):
         arrived(m)
-        own_copies[m].wait()
     save_qkv.wait()
     save_wo.wait()
+    for k in range(4):
+        cot_away(k).wait()
+    table_away().wait()
     for m in range(5):
         for i in range(6):
             move(m, i).wait_send()
@@ -673,13 +714,17 @@
         gain_move(j).wait_send()
 
 
-def forward_call(tokens, qkv_own, wo_own, gate_own, up_own, down_own, gains_own, cos, sin, key_ok):
+def forward_call(tokens, cot, ids, weight, q_own, k_own, v_own, wo_own, gate_own, up_own, down_own, gains_own, cos, sin, key_ok):
     rows, width = tokens.shape
-    qkv_cols, q_cols = qkv_own.shape[1], wo_own.shape[1]
+    q_cols = q_own.shape[1]
+    qkv_cols = q_cols + k_own.shape[1] + v_own.shape[1]
     tall = gate_own.shape[0]
     vmem, anyspace = pl.BlockSpec(memory_space=pltpu.VMEM), pl.BlockSpec(memory_space=pl.ANY)
     shape = jax.ShapeDtypeStruct
     outs = [
+        (shape((rows, width), bf16), vmem),
+        (shape((rows, width), bf16), anyspace),
+        (shape((2 * rows, 128), f32), vmem),
         (shape((rows, width), f32), vmem),
         (shape((2 * rows, width), bf16), vmem),
         (shape((rows, q_cols), bf16), vmem),
@@ -700,7 +745,7 @@
     return pl.pallas_call(
         forward_kernel,
         out_shape=[o[0] for o in outs],
-        in_specs=[vmem] + [anyspace] * 5 + [vmem] * 4,
+        in_specs=[anyspace] * 2 + [vmem] * 2 + [anyspace] * 7 + [vmem] * 4,
         out_specs=[o[1] for o in outs],
         scratch_shapes=[
             pltpu.VMEM((width, qkv_cols), bf16),
@@ -708,21 +753,77 @@
             big, big, big, big, big, big,
             pltpu.VMEM((2, width), f32),
             dma((5, 6)), dma((5, 6)), dma((2, 4)), dma((2, 4)), dma((7,)), dma((7,)),
-            dma((CHUNKS,)), dma((CHUNKS,)), dma((5,)), dma((2,)),
+            dma((CHUNKS,)), dma((CHUNKS,)), dma((8,)), dma((2,)), dma((5,)), dma((5,)), dma((4,)),
         ] + line_sems(),
         compiler_params=pltpu.CompilerParams(
             collective_id=1, has_side_effects=True, vmem_limit_bytes=60 * 2**20
         ),
         cost_estimate=pl.CostEstimate(flops=8 * 10**9, bytes_accessed=60 * 10**6, transcendentals=2 * 10**6),
         name="forward_to_experts",
-    )(tokens, qkv_own, wo_own, gate_own, up_own, down_own, gains_own, cos, sin, key_ok)
+    )(tokens, cot, ids, weight, q_own, k_own, v_own, wo_own, gate_own, up_own, down_own, gains_own, cos, sin, key_ok)
+
+
+def turn(i):
+    return i // 2 + 3 * (i % 2)
+
+
+def tile(t):
+    return pl.ds(pl.multiple_of(t * 256, 256), 256)
+
+
+def by_half(t, f):
+    for first in (1, 2):
+
+        @pl.when(t // 3 == first - 1)
+        def _(first=first):
+            f(first)
+
+
+def first_exchange(m, t, j, first, grad, came, send, recv, to, wide):
+    return remote(
+        grad.at[m, tile(t), pl.ds((3 if j else first) * wide, wide)], came(t, pl.ds(j * wide, wide)), send, recv,
+        to[first, 0],
+    )
+
+
+def second_exchange(count, grad_at, came_at, dst_at, load_a, load_b, on_buf, l_sem, s_send, s_recv, to, wide):
+    def loads(u, first):
+        slot = u % 2
+        return (
+            pltpu.make_async_copy(grad_at(u, pl.ds((3 - first) * wide, wide)), load_a.at[slot], l_sem.at[slot, 0]),
+            pltpu.make_async_copy(came_at(u, pl.ds(wide, wide)), load_b.at[slot], l_sem.at[slot, 1]),
+        )
+
+    def pass_on(u, first):
+        return remote(on_buf.at[u], dst_at(u), s_send.at[u], s_recv.at[u], to[3 - first, 0])
+
+    def start(u):
+        by_half(turn(u % 6), lambda first: [x.start() for x in loads(u, first)])
+
+    def step(u):
+        def f(first):
+            for x in loads(u, first):
+                x.wait()
+            on_buf[u] = (load_a[u % 2].astype(f32) + load_b[u % 2].astype(f32)).astype(bf16)
+            pass_on(u, first).start()
+
+        by_half(turn(u % 6), f)
+
+        @pl.when(u + 2 < count)
+        def _():
+            start(u + 2)
+
+    def finish():
+        over(count, lambda u: by_half(turn(u % 6), lambda first: pass_on(u, first).wait()))
+
+    return start, step, finish
 
 
 def expert_kernel(
-    h2, g, mine, gate_in, up_in, down_in,
+    h2, g_own, g_other, mine, gate_own, up_own, down_own, gate_in, up_in, down_in,
     grad_h2, out, grads, got,
-    gate, up, down, acts, drow, rbuf, in_buf, mid_buf, stage,
-    load_sem, x_send, x_recv, s_send, s_recv, keep_sem, out_sem, *line,
+    g, g_sem, gate, up, down, acts, drow, rbuf, in_buf, mid_buf, stage,
+    load_sem, rest_sem, w_send, w_recv, x_send, x_recv, s_send, s_recv, keep_sem, out_sem, *line,
 ):
     to = plane_partners()
     side, mid, inner = line_roles("tensor")
@@ -743,77 +844,135 @@
 
     tall, width = down.shape
     rows = drow.shape[0] // 2
-    hidden = mine.shape[1]
-    tiles = tall // 256
+    first_expert = 8 * lax.axis_index("expert")
     wide = width // 4
-    tile = lambda t: pl.ds(pl.multiple_of(t * 256, 256), 256)
-    order = lambda i: i // 2 + (tiles // 2) * (i % 2)
-
-    def load(t, j):
-        src, dst = ((gate_in, gate), (up_in, up), (down_in, down))[j]
-        return pltpu.make_async_copy(src.at[tile(t)], dst.at[tile(t)], load_sem.at[t, j])
-
-    def start_loads(i):
+    units = tall // 8
+    late = 4 * 256
+    mats = ((gate_own, gate_in, gate), (up_own, up_in, up), (down_own, down_in, down))
+
+    def shard_move(j, n):
+        shard, _, full = mats[j]
+        own = lambda i: shard.at[tile(turn(i))]
+        slot = lambda k, i: full.at[tile(i), pl.ds(k * wide, wide)]
+        a, b = 4, 5
+        src, dst, way = (
+            (own(a), slot(1, a), 1), (own(b), slot(2, b), 2), (own(a), slot(2, a), 2), (own(b), slot(1, b), 1),
+            (slot(1, a), slot(3, a), 2), (slot(2, b), slot(3, b), 1),
+        )[n]
+        return remote(src, dst, w_send.at[j, n], w_recv.at[j, n], to[way, 0])
+
+    for j in range(3):
+        for n in range(4):
+            shard_move(j, n).start()
+
+    def load_own(i, j):
+        return pltpu.make_async_copy(
+            mats[j][0].at[tile(turn(i))], mats[j][2].at[tile(i), pl.ds(0, wide)], load_sem.at[i, j]
+        )
+
+    def load_rest(i, j):
+        cols = pl.ds(wide, 3 * wide)
+        return pltpu.make_async_copy(
+            mats[j][1].at[tile(turn(i)), cols], mats[j][2].at[tile(i), cols], rest_sem.at[i, j]
+        )
+
+    load_g = lane_copies(g_own, g.at[pl.ds(0, rows)], [g_sem.at[k] for k in range(4)], to) + [
+        pltpu.make_async_copy(g_other, g.at[pl.ds(rows, rows)], g_sem.at[4])
+    ]
+    for x in load_g:
+        x.start()
+    over(4, lambda i: [x(i, j).start() for x in (load_own, load_rest) for j in range(3)])
+    for i in (4, 5):
         for j in range(3):
-            load(order(i), j).start()
-
-    over(tiles, start_loads)
-
-    def keep(m, t, slot):
-        return pltpu.make_async_copy(stage.at[slot], grads.at[m, tile(t)], keep_sem.at[slot])
-
-    def send(m, t, j, way):
-        src = grads.at[m, tile(t), pl.ds((3 if j else way) * wide, wide)]
-        dst = got.at[m, tile(t), pl.ds(j * wide, wide)]
-        return remote(src, dst, s_send.at[m, t, j], s_recv.at[m, t, j], to[way, 0])
-
-    def send_tile(u):
-        m, i = u // tiles, u % tiles
-        t = order(i)
-        keep(m, t, u % 2).wait()
-        for way in (1, 2):
-
-            @pl.when(i % 2 == way - 1)
-            def _(way=way):
-                for j in range(2):
-                    send(m, t, j, way).start()
-
-    def grad_tile(u, rhs):
-        m, i = u // tiles, u % tiles
-        t = order(i)
-        low = acts[m, :, tile(t)]
-        for k in range(4):
-            cols = slice(k * wide, (k + 1) * wide)
-            stage[u % 2, :, cols] = tn(low, rhs[:, cols]).astype(bf16)
-        keep(m, t, u % 2).start()
-
-        @pl.when(u > 0)
-        def _():
-            send_tile(u - 1)
-
-    units = tall // 8
+            load_own(i, j).start()
+    for x in load_g:
+        x.wait()
 
     def hidden_tile(i):
-        t = order(i)
-        for j in range(3):
-            load(t, j).wait()
+        t = turn(i)
         first = (t * 256) // units
         edge = (first + 1) * units - t * 256
         lanes = lax.broadcasted_iota(jnp.int32, mine.shape, 1)
-        pick = lambda e: jnp.sum(jnp.where(lanes == e, mine[...], 0.0), axis=1, keepdims=True)
+        pick = lambda e: jnp.sum(jnp.where(lanes == e + first_expert, mine[...], 0.0), axis=1, keepdims=True)
         column = lax.broadcasted_iota(jnp.int32, (2 * rows, 256), 1)
         scale = jnp.where(column < edge, pick(first), pick(first + 1))
-        gate_value = nt(h2[...], gate[tile(t)])
-        up_value = nt(h2[...], up[tile(t)])
-        grad_act = nt(g[...], down[tile(t)]) * scale
+        gate_value = nt(h2[...], gate[tile(i)])
+        up_value = nt(h2[...], up[tile(i)])
+        grad_act = nt(g[...], down[tile(i)]) * scale
         sig = jax.nn.sigmoid(gate_value)
         silu = gate_value * sig
-        acts[0, :, tile(t)] = (silu * up_value * scale).astype(bf16)
-        acts[2, :, tile(t)] = (grad_act * silu).astype(bf16)
-        acts[1, :, tile(t)] = (grad_act * up_value * sig * (1.0 + gate_value * (1.0 - sig))).astype(bf16)
-        grad_tile(i, g)
-
-    over(tiles, hidden_tile)
+        acts[0, :, tile(i)] = (silu * up_value * scale).astype(bf16)
+        acts[2, :, tile(i)] = (grad_act * silu).astype(bf16)
+        acts[1, :, tile(i)] = (grad_act * up_value * sig * (1.0 + gate_value * (1.0 - sig))).astype(bf16)
+
+    def parts(v):
+        return v // 6, (v % 6) // 2, 1 - v % 2
+
+    def keep(v, ab):
+        m, q, s = parts(v)
+        cols = pl.ds(pl.multiple_of(s * 2 * wide, 2 * wide), 2 * wide)
+        return pltpu.make_async_copy(
+            stage.at[v % 2, pl.ds(ab * 256, 256)], grads.at[m, tile(q + 3 * ab), cols], keep_sem.at[v % 2, ab]
+        )
+
+    def send(m, t, j, first):
+        came = lambda t, cols: got.at[m, tile(t), cols]
+        return first_exchange(m, t, j, first, grads, came, s_send.at[m, t, j], s_recv.at[m, t, j], to, wide)
+
+    def flush(v):
+        m, q, s = parts(v)
+        for ab in range(2):
+            keep(v, ab).wait()
+
+        @pl.when((m < 2) & (s == 1))
+        def _():
+            send(m, q, 1, 1).start()
+            send(m, q + 3, 0, 2).start()
+            send(m, q + 3, 1, 2).start()
+
+        @pl.when((m < 2) & (s == 0))
+        def _():
+            send(m, q, 0, 1).start()
+
+    def grad_unit(v, rhs):
+        m, q, s = parts(v)
+        low = acts[m, :, pl.ds(pl.multiple_of(q * 512, 512), 512)]
+        for n in range(2):
+            cols = pl.ds(pl.multiple_of((2 * s + n) * wide, wide), wide)
+            stage[v % 2, :, n * wide : (n + 1) * wide] = tn(low, rhs[:, cols]).astype(bf16)
+        for ab in range(2):
+            keep(v, ab).start()
+
+        @pl.when(v > 0)
+        def _():
+            flush(v - 1)
+
+    def early_tile(i):
+        for x in (load_own, load_rest):
+            for j in range(3):
+                x(i, j).wait()
+        hidden_tile(i)
+
+    over(4, early_tile)
+
+    def early_rows(j):
+        col = pl.ds(pl.multiple_of(j * 256, 256), 256)
+        drow[:, col] = (nn(acts[1, :, 0:late], gate[0:late, col]) + nn(acts[2, :, 0:late], up[0:late, col])).astype(bf16)
+
+    over(width // 256, early_rows)
+    over(2, lambda v: grad_unit(v, g))
+    for j in range(3):
+        for n in (0, 1):
+            shard_move(j, n).wait_recv()
+            shard_move(j, 4 + n).start()
+    over(4, lambda v: grad_unit(v, g), 2)
+    for i in (4, 5):
+        for j in range(3):
+            load_own(i, j).wait()
+    for j in range(3):
+        for n in (2, 3, 4, 5):
+            shard_move(j, n).wait_recv()
+    over(6, hidden_tile, 4)
 
     step = rows // CHUNKS
 
@@ -822,16 +981,15 @@
         dst = rbuf.at[pl.ds(pl.multiple_of(i * step, step), step)]
         return remote(src, dst, x_send.at[i], x_recv.at[i], to[0, 1])
 
-    for part_rows in (slice(rows, 2 * rows), slice(0, rows)):
-
-        def row_grads(j, part_rows=part_rows):
+    for some in (slice(rows, 2 * rows), slice(0, rows)):
+
+        def late_rows(j, some=some):
             col = pl.ds(pl.multiple_of(j * 256, 256), 256)
-            drow[part_rows, col] = (
-                nn(acts[1, part_rows, :], gate[:, col]) + nn(acts[2, part_rows, :], up[:, col])
-            ).astype(bf16)
-
-        over(width // 256, row_grads)
-        if part_rows.start:
+            more = nn(acts[1, some, late:], gate[late:, col]) + nn(acts[2, some, late:], up[late:, col])
+            drow[some, col] = (drow[some, col].astype(f32) + more).astype(bf16)
+
+        over(width // 256, late_rows)
+        if some.start:
             over(CHUNKS, lambda i: give(i).start())
 
     def add_other(c):
@@ -844,38 +1002,38 @@
         return pltpu.make_async_copy(gate.at[pl.ds(0, 2 * rows), col], out.at[:, col], out_sem.at[j])
 
     def work(i):
-        @pl.when(i < 2 * tiles)
-        def _():
-            grad_tile(tiles + i, h2)
-
-        @pl.when(i == 2 * tiles)
-        def _():
-            send_tile(3 * tiles - 1)
-
-        @pl.when(i >= 2 * tiles)
-        def _():
-            j = i - 2 * tiles
+        @pl.when(i < 2)
+        def _():
+            grad_unit(4 + i, g)
+
+        @pl.when((i >= 2) & (i < 14))
+        def _():
+            grad_unit(4 + i, h2)
+
+        @pl.when(i == 14)
+        def _():
+            flush(17)
+
+        @pl.when(i >= 14)
+        def _():
+            j = i - 14
             col = pl.ds(pl.multiple_of(j * 256, 256), 256)
             gate[0 : 2 * rows, col] = nn(acts[0], down[:, col]).astype(bf16)
             out_copy(j).start()
 
     line_sum_work(
         drow, in_buf, mid_buf, drow, grad_h2, line, "tensor", rows, add_other, lambda r, c: None, work,
-        2 * tiles + width // 256,
+        14 + width // 256,
     )
     over(width // 256, lambda j: out_copy(j).wait())
     over(CHUNKS, lambda i: give(i).wait_send())
-
-    def finish_tile(u):
-        m, i = u // tiles, u % tiles
-        for way in (1, 2):
-
-            @pl.when(i % 2 == way - 1)
-            def _(way=way):
-                for j in range(2):
-                    send(m, order(i), j, way).wait()
-
-    over(3 * tiles, finish_tile)
+    for j in range(3):
+        for n in range(6):
+            shard_move(j, n).wait_send()
+    for m in range(2):
+        for t in range(6):
+            for j in range(2):
+                send(m, t, j, 1 + t // 3).wait()
 
 
 def line_sum_work(x_ref, in_buf, mid_buf, part, out_ref, sems, axis, n_rows, ready, finish, work, n_work):
@@ -955,33 +1113,33 @@
         over(CHUNKS, done)
 
 
-def expert_call(h2, g, mine, gate, up, down):
+def expert_call(h2, g_own, g_other, mine, gate_own, up_own, down_own, gate, up, down):
     tall, width = down.shape
     rows = h2.shape[0] // 2
     vmem, anyspace = pl.BlockSpec(memory_space=pltpu.VMEM), pl.BlockSpec(memory_space=pl.ANY)
     shape = jax.ShapeDtypeStruct
     dma = pltpu.SemaphoreType.DMA
-    tiles = tall // 256
     return pl.pallas_call(
         expert_kernel,
         out_shape=[
             shape((rows, width), bf16),
             shape((2 * rows, width), bf16),
             shape((3, tall, width), bf16),
-            shape((3, tall, width // 2), bf16),
+            shape((2, tall, width // 2), bf16),
         ],
-        in_specs=[vmem, vmem, vmem, anyspace, anyspace, anyspace],
+        in_specs=[vmem, anyspace, anyspace, vmem] + [anyspace] * 6,
         out_specs=[vmem, anyspace, anyspace, anyspace],
-        scratch_shapes=[pltpu.VMEM((tall, width), bf16)] * 3
+        scratch_shapes=[pltpu.VMEM((2 * rows, width), bf16), dma((5,))]
+        + [pltpu.VMEM((tall, width), bf16)] * 3
         + [
             pltpu.VMEM((3, 2 * rows, tall), bf16),
             pltpu.VMEM((2 * rows, width), bf16),
             pltpu.VMEM((rows, width), bf16),
             pltpu.VMEM((rows, width), bf16),
             pltpu.VMEM((rows, width), bf16),
-            pltpu.VMEM((2, 256, width), bf16),
-            dma((tiles, 3)), dma((CHUNKS,)), dma((CHUNKS,)), dma((3, tiles, 2)), dma((3, tiles, 2)),
-            dma((2,)), dma((width // 256,)),
+            pltpu.VMEM((2, 512, width // 2), bf16),
+            dma((6, 3)), dma((4, 3)), dma((3, 6)), dma((3, 6)), dma((CHUNKS,)), dma((CHUNKS,)), dma((2, 6, 2)), dma((2, 6, 2)),
+            dma((2, 2)), dma((width // 256,)),
         ]
         + line_sems(),
         compiler_params=pltpu.CompilerParams(
@@ -989,7 +1147,7 @@
         ),
         cost_estimate=pl.CostEstimate(flops=58 * 10**9, bytes_accessed=60 * 10**6, transcendentals=2 * 10**6),
         name="experts",
-    )(h2, g, mine, gate, up, down)
+    )(h2, g_own, g_other, mine, gate_own, up_own, down_own, gate, up, down)
 
 
 def plane_barrier(to, z_others):
@@ -1021,23 +1179,28 @@
 
 
 def attention_back_kernel(
-    grad_h2, x2, cot, qrot, krot, value, raw, gains, cos, sin, probs, wo_in, qkv_in, out_part, grads, got,
-    output, dx2, low, grad_qkv, grad_h1, gain_grads, got2,
-    wo, qkv, own_out, rbuf, in_buf, mid_buf, summed, datt, pbuf, dk, dv, gain_rows, load_a, load_b, on_buf,
-    w_sem, p_sem, l_sem, x_send, x_recv, s_send, s_recv, *line,
+    gains, cos, sin, grad_h2_in, x2_in, cot_in, qrot_in, krot_in, value_in, raw_in, probs, wo_in, qkv_in, out_part,
+    grads, got,
+    output, dx2, low, grad_qkv, grad_h1, gain_grads, got2, got_up,
+    grad_h2, x2, cot, qrot, krot, value, raw, f_sem, wo, qkv, own_out, rbuf, in_buf, mid_buf, summed, datt, pbuf, dk, dv, gain_rows, load_a, load_b, on_buf,
+    w_sem, p_sem, l_sem, x_send, x_recv, s_send, s_recv, u_send, u_recv, *line,
 ):
     to = plane_partners()
+    fetch = [
+        pltpu.make_async_copy(src, dst, f_sem.at[i])
+        for i, (src, dst) in enumerate(
+            ((x2_in, x2), (grad_h2_in, grad_h2), (qrot_in, qrot), (krot_in, krot), (value_in, value), (raw_in, raw))
+        )
+    ]
+    early = fetch[:2] + lane_copies(cot_in, cot, [f_sem.at[6 + k] for k in range(4)], to)
     plane_barrier(to, z_partners())
     places = [to[k, 0]["dp"] for k in range(4)]
     rows, width = x2.shape
     wide = width // 4
-    tiles = grads.shape[1] // 256
     q_cols = qrot.shape[1]
     n_heads = q_cols // 128
     step = rows // CHUNKS
     rate = 128 ** (-0.5)
-    order = lambda i: i // 2 + (tiles // 2) * (i % 2)
-    tile = lambda t: pl.ds(pl.multiple_of(t * 256, 256), 256)
 
     def give(i):
         src = out_part.at[pl.ds(pl.multiple_of(rows + i * step, step), step)]
@@ -1050,51 +1213,27 @@
         pltpu.make_async_copy(qkv_in, qkv, w_sem.at[1]),
         pltpu.make_async_copy(out_part.at[pl.ds(0, rows)], own_out, w_sem.at[2]),
     ]
-    for w in weights:
+    for w in [weights[2]] + early + [weights[0]] + fetch[2:] + [weights[1]]:
         w.start()
 
     def load_probs(h):
         return pltpu.make_async_copy(probs.at[h], pbuf.at[h % 2], p_sem.at[h % 2])
 
-    def loads(u, first):
-        m, t = u // tiles, order(u % tiles)
-        slot = u % 2
-        return (
-            pltpu.make_async_copy(
-                grads.at[m, tile(t), pl.ds((3 - first) * wide, wide)], load_a.at[slot], l_sem.at[slot, 0]
-            ),
-            pltpu.make_async_copy(got.at[m, tile(t), pl.ds(wide, wide)], load_b.at[slot], l_sem.at[slot, 1]),
-        )
-
-    def by_half(u, f):
-        for first in (1, 2):
-
-            @pl.when((u % tiles) % 2 == first - 1)
-            def _(first=first):
-                f(first)
-
-    def start_loads(u):
-        by_half(u, lambda first: [x.start() for x in loads(u, first)])
-
-    def pass_on(u, first):
-        m, t = u // tiles, order(u % tiles)
-        return remote(on_buf.at[u], got2.at[m, tile(t)], s_send.at[u], s_recv.at[u], to[3 - first, 0])
-
-    def second_tile(u):
-        def f(first):
-            for x in loads(u, first):
-                x.wait()
-            on_buf[u] = (load_a[u % 2].astype(f32) + load_b[u % 2].astype(f32)).astype(bf16)
-            pass_on(u, first).start()
-
-        by_half(u, f)
-
-        @pl.when(u + 2 < 3 * tiles)
-        def _():
-            start_loads(u + 2)
-
-    start_loads(0)
-    start_loads(1)
+    def up_move(t, j, first):
+        came = lambda t, cols: got_up.at[tile(t), cols]
+        return first_exchange(2, t, j, first, grads, came, u_send.at[t, j], u_recv.at[t, j], to, wide)
+
+    def up_moves(i, f):
+        t = turn(i)
+        by_half(t, lambda first: [f(up_move(t, j, first)) for j in range(2)])
+
+    over(6, lambda i: up_moves(i, lambda x: x.start()))
+    at = lambda ref: lambda u, cols=pl.ds(0, wide): ref.at[u // 6, tile(turn(u % 6)), cols]
+    start, second_tile, second_done = second_exchange(
+        12, at(grads), at(got), at(got2), load_a, load_b, on_buf, l_sem, s_send, s_recv, to, wide
+    )
+    start(0)
+    start(1)
     load_probs(0).start()
     gain_query, gain_key = gain_vectors(gains, gain_rows)
     gain_grads[...] = jnp.zeros_like(gain_grads)
@@ -1159,9 +1298,14 @@
         grad_h1[:, r] = nt(grad_qkv[...], qkv[r]).astype(bf16)
 
     def work(i):
-        @pl.when(i < 3 * tiles)
+        @pl.when(i < 12)
         def _():
             second_tile(i)
+
+        @pl.when(i == 0)
+        def _():
+            for x in early:
+                x.wait()
 
         @pl.when(i < 4)
         def _():
@@ -1171,6 +1315,8 @@
         @pl.when(i == 4)
         def _():
             weights[0].wait()
+            for x in fetch[2:]:
+                x.wait()
 
         @pl.when((i >= 4) & (i < 6))
         def _():
@@ -1210,7 +1356,8 @@
         own_out, in_buf, mid_buf, own_out, summed, line, "tensor", rows, ready, finish, work, 11 + n_heads
     )
     over(CHUNKS, lambda i: give(i).wait_send())
-    over(3 * tiles, lambda u: by_half(u, lambda first: pass_on(u, first).wait()))
+    second_done()
+    over(6, lambda i: up_moves(i, lambda x: x.wait()))
 
 
 def attention_back_call(grad_h2, x2, cot, qrot, krot, value, raw, gains, cos, sin, probs, wo, qkv, out_part, grads, got):
@@ -1221,7 +1368,6 @@
     vmem, anyspace = pl.BlockSpec(memory_space=pltpu.VMEM), pl.BlockSpec(memory_space=pl.ANY)
     shape = jax.ShapeDtypeStruct
     dma = pltpu.SemaphoreType.DMA
-    tiles = tall // 256
     big = pltpu.VMEM((rows, width), bf16)
     return pl.pallas_call(
         attention_back_kernel,
@@ -1232,11 +1378,20 @@
             shape((rows, qkv_cols), bf16),
             shape((rows, width), bf16),
             shape((8, width), f32),
-            shape((3, tall, wide), bf16),
+            shape((2, tall, wide), bf16),
+            shape((tall, 2 * wide), bf16),
         ],
-        in_specs=[vmem] * 10 + [anyspace] * 6,
-        out_specs=[vmem] * 6 + [anyspace],
+        in_specs=[vmem] * 3 + [anyspace] * 13,
+        out_specs=[vmem] * 6 + [anyspace] * 2,
         scratch_shapes=[
+            big,
+            pltpu.VMEM((rows, width), f32),
+            big,
+            pltpu.VMEM((rows, q_cols), bf16),
+            pltpu.VMEM((rows, 128), bf16),
+            pltpu.VMEM((rows, 128), bf16),
+            pltpu.VMEM((rows, qkv_cols), f32),
+            dma((10,)),
             pltpu.VMEM((width, q_cols), bf16),
             pltpu.VMEM((width, qkv_cols), bf16),
             big, big, big, big, big,
@@ -1247,8 +1402,9 @@
             pltpu.VMEM((2, width), f32),
             pltpu.VMEM((2, 256, wide), bf16),
             pltpu.VMEM((2, 256, wide), bf16),
-            pltpu.VMEM((3 * tiles, 256, wide), bf16),
-            dma((3,)), dma((2,)), dma((2, 2)), dma((CHUNKS,)), dma((CHUNKS,)), dma((3 * tiles,)), dma((3 * tiles,)),
+            pltpu.VMEM((12, 256, wide), bf16),
+            dma((3,)), dma((2,)), dma((2, 2)), dma((CHUNKS,)), dma((CHUNKS,)), dma((12,)), dma((12,)),
+            dma((6, 2)), dma((6, 2)),
         ]
         + line_sems(),
         compiler_params=pltpu.CompilerParams(
@@ -1256,16 +1412,27 @@
         ),
         cost_estimate=pl.CostEstimate(flops=9 * 10**9, bytes_accessed=60 * 10**6, transcendentals=10**5),
         name="attention_backward",
-    )(grad_h2, x2, cot, qrot, krot, value, raw, gains, cos, sin, probs, wo, qkv, out_part, grads, got)
+    )(gains, cos, sin, grad_h2, x2, cot, qrot, krot, value, raw, probs, wo, qkv, out_part, grads, got)
 
 
 def last_kernel(
-    part, dx2, tokens, grad_qkv, low, att, gains, gain_grads,
-    tokens_grad, qkv_shard, wo_shard, gain_sum,
-    h1, in_buf, mid_buf, half_sum, summed, gain_rows, wo_all, qkv_all, wo_core, qkv_core, wo_one, qkv_one, wo_two, qkv_two,
-    ga, z_got, g_out, g_got,
+    gains, gain_grads, part_in, dx2_in, tokens_in, grad_qkv_in, low_in, att_in, grads, got_up,
+    tokens_grad, q_shard, k_shard, v_shard, wo_shard, gain_sum, got2_up,
+    part, dx2, tokens, grad_qkv, low, att, f_sem, h1, in_buf, mid_buf, half_sum, summed, gain_rows, wo_all, qkv_all, wo_core, qkv_core, wo_one, qkv_one, wo_two, qkv_two,
+    ga, z_got, g_out, g_got, load_a, load_b, on_buf, l_sem, s_send, s_recv,
     z_send, z_recv, c_send, c_recv, f_send, f_recv, t_send, t_recv, g_send, g_recv, *line,
 ):
+    fetch = [
+        pltpu.make_async_copy(src, dst, f_sem.at[i])
+        for i, (src, dst) in enumerate(
+            (
+                (part_in, part), (tokens_in, tokens), (low_in, low), (att_in, att), (grad_qkv_in, grad_qkv),
+                (dx2_in, dx2),
+            )
+        )
+    ]
+    for x in fetch:
+        x.start()
     c = lax.axis_index("expert")
     to = plane_partners()
     zs = z_partners()
@@ -1281,6 +1448,13 @@
 
     for j in range(3):
         z_move(j).start()
+    up_at = lambda ref: lambda u, cols=pl.ds(0, wide): ref.at[tile(turn(u)), cols]
+    start, second_tile, second_done = second_exchange(
+        6, lambda u, cols: grads.at[2, tile(turn(u)), cols], up_at(got_up), up_at(got2_up),
+        load_a, load_b, on_buf, l_sem, s_send, s_recv, to, wide,
+    )
+    start(0)
+    start(1)
     gain_vectors(gains, gain_rows)
     ga[...] = jnp.zeros_like(ga)
 
@@ -1340,7 +1514,13 @@
     def work(i):
         @pl.when(i == 0)
         def _():
+            for x in fetch[1:]:
+                x.wait()
             over(rows // 64, hidden_one)
+
+        @pl.when(i < 6)
+        def _():
+            second_tile(i)
 
         for n, k in enumerate((3, 1, 2, 0)):
 
@@ -1373,6 +1553,7 @@
         for k in range(4):
             tokens_grad[r, pl.ds(pl.multiple_of(places[k] * wide, wide), wide)] = d[:, k * wide : (k + 1) * wide]
 
+    fetch[0].wait()
     line_sum_work(part, in_buf, mid_buf, half_sum, summed, line, "tensor", rows, lambda k: None, finish, work, 20)
 
     head_rows = gain_grads[1:3, 0:128]
@@ -1394,18 +1575,26 @@
 
     for j in range(len(others)):
         gain_move(j).start()
-    for m, shard in ((0, wo_shard), (1, qkv_shard)):
+    q_cols, k_cols = q_shard.shape[1], k_shard.shape[1]
+    shards = (
+        ((wo_shard, 0),),
+        ((q_shard, 0), (k_shard, q_cols), (v_shard, q_cols + k_cols)),
+    )
+    for m in range(2):
         full, two = mats[m][2], mats[m][5]
         for h in range(2):
             add_first(m, h, 0, 0)
             second_move(m, h).wait_recv()
             r = pl.ds(pl.multiple_of(c * piece + h * half, half), half)
-            shard[h * half : (h + 1) * half] = full[r].astype(f32) + two[h].astype(f32)
+            for shard, col in shards[m]:
+                cols = pl.ds(col, shard.shape[1])
+                shard[h * half : (h + 1) * half] = full[r, cols].astype(f32) + two[h, :, cols].astype(f32)
     total = g_out[0, pl.ds(c, 1)].reshape(8, 128)
     for j in range(len(others)):
         gain_move(j).wait_recv()
         total += g_got[j]
     gain_sum[...] = total
+    second_done()
     for m in range(2):
         for k in range(4):
             core_move(m, k).wait_send()
@@ -1417,7 +1606,7 @@
         gain_move(j).wait_send()
 
 
-def last_call(part, dx2, tokens, grad_qkv, low, att, gains, gain_grads):
+def last_call(part, dx2, tokens, grad_qkv, low, att, gains, gain_grads, grads, got_up):
     rows, width = tokens.shape
     q_cols, qkv_cols = att.shape[1], grad_qkv.shape[1]
     piece = width // 8
@@ -1430,13 +1619,25 @@
         last_kernel,
         out_shape=[
             shape((rows, width), f32),
-            shape((piece, qkv_cols), f32),
+            shape((piece, q_cols), f32),
+            shape((piece, (qkv_cols - q_cols) // 2), f32),
+            shape((piece, (qkv_cols - q_cols) // 2), f32),
             shape((piece, q_cols), f32),
             shape((8, 128), f32),
+            shape((got_up.shape[0], width // 4), bf16),
         ],
-        in_specs=[vmem] * 8,
-        out_specs=[vmem] * 4,
-        scratch_shapes=[big, big, big, big, big, pltpu.VMEM((2, width), f32)]
+        in_specs=[vmem] * 2 + [pl.BlockSpec(memory_space=pl.ANY)] * 8,
+        out_specs=[vmem] * 6 + [pl.BlockSpec(memory_space=pl.ANY)],
+        scratch_shapes=[
+            big,
+            pltpu.VMEM((rows, width), f32),
+            big,
+            pltpu.VMEM((rows, qkv_cols), bf16),
+            big,
+            pltpu.VMEM((rows, q_cols), bf16),
+            dma((6,)),
+        ]
+        + [big, big, big, big, big, pltpu.VMEM((2, width), f32)]
         + both(width)
         + both(4, piece)
         + both(2, 2, piece // 2)
@@ -1446,6 +1647,10 @@
             pltpu.VMEM((3, 8, 128), f32),
             pltpu.VMEM((4, 2, 8, 128), f32),
             pltpu.VMEM((7, 8, 128), f32),
+            pltpu.VMEM((2, 256, width // 4), bf16),
+            pltpu.VMEM((2, 256, width // 4), bf16),
+            pltpu.VMEM((6, 256, width // 4), bf16),
+            dma((2, 2)), dma((6,)), dma((6,)),
             dma((3,)), dma((3,)), dma((2, 4)), dma((2, 4)), dma((2, 2, 2)), dma((2, 2, 2)), dma((2, 2)), dma((2, 2)),
             dma((7,)), dma((7,)),
         ]
@@ -1455,7 +1660,7 @@
         ),
         cost_estimate=pl.CostEstimate(flops=5 * 10**9, bytes_accessed=40 * 10**6, transcendentals=10**5),
         name="input_gradients",
-    )(part, dx2, tokens, grad_qkv, low, att, gains, gain_grads)
+    )(gains, gain_grads, part, dx2, tokens, grad_qkv, low, att, grads, got_up)
 
 
 def local_fast(
@@ -1506,55 +1711,50 @@
     cos2 = jnp.concatenate([cosine_table[:, 0], cosine_table[:, 0]], 1)
     sin2 = jnp.concatenate([-sine_table[:, 0], sine_table[:, 0]], 1)
     key_ok = (jnp.arange(rows, dtype=jnp.int32) < length).astype(f32)[None]
-    inputs_low = lane(tokens)
-    inputs = inputs_low.astype(f32)
+    own_experts = [w.reshape(flat, part) for w in (gate_weight, up_weight, down_weight)]
     (
-        mixed_rows, hidden_all, attended_low, rotated_query, key_rot, value_low, raw, prob_low,
-        gains, gate_full, up_full, down_full, full_qkv, full_output,
+        inputs_low, upstream_other, table, mixed_rows, hidden_all, attended_low, rotated_query, key_rot, value_low, raw,
+        prob_low, gains, gate_full, up_full, down_full, full_qkv, full_output,
     ) = forward_call(
-        inputs_low,
-        jnp.concatenate([query_weight, key_matrix, value_matrix], 1),
+        tokens,
+        cotangent,
+        route_ids,
+        route_weight,
+        query_weight,
+        key_matrix,
+        value_matrix,
         output_weight,
-        gate_weight.reshape(flat, part),
-        up_weight.reshape(flat, part),
-        down_weight.reshape(flat, part),
+        *own_experts,
         gains_own,
         cos2,
         sin2,
         key_ok,
     )
-    experts = jnp.arange(group * n_ex, dtype=jnp.int32)
-    table = jnp.zeros((rows, group * n_ex), f32)
-    for c in range(route_ids.shape[1]):
-        table = table + jnp.where(
-            route_ids[:, c, None] == experts[None, :], route_weight[:, c, None], 0.0
+    grad_hidden_two, expert_out, grads, got = expert_call(
+        hidden_all, cotangent, upstream_other, table, *own_experts, gate_full, up_full, down_full
+    )
+    output, grad_mixed, grad_proj_low, grad_qkv_low, grad_hidden_one, gain_grads, got2, got_up = attention_back_call(
+        grad_hidden_two, mixed_rows, cotangent, rotated_query, key_rot, value_low, raw, gains, cos2, sin2,
+        prob_low, full_output, full_qkv, expert_out, grads, got,
+    )
+    tokens_grad, query_shard, key_shard, value_shard, output_shard, gain_sum, got2_up = last_call(
+        grad_hidden_one, grad_mixed, inputs_low, grad_qkv_low, grad_proj_low, attended_low, gains, gain_grads,
+        grads, got_up,
+    )
+    down_shard, gate_shard, up_shard = (
+        (grads[m, :, :part].astype(f32) + first[:, :part].astype(f32) + second.astype(f32)).reshape(
+            group, hidden, part
         )
-    table = jnp.concatenate(xor_gather(table, "expert"), 0)
-    mine = lax.dynamic_slice_in_dim(table, me_ex * group, group, 1)
-    mine = jnp.pad(mine, ((0, 0), (0, 128 - group)))
-    upstream_low = lane(cotangent)
-    upstream_all = jnp.concatenate(xor_gather(upstream_low, "expert"), 0)
-
-    grad_hidden_two, expert_out, grads, got = expert_call(
-        hidden_all, upstream_all, mine, gate_full, up_full, down_full
-    )
-    output, grad_mixed, grad_proj_low, grad_qkv_low, grad_hidden_one, gain_grads, got2 = attention_back_call(
-        grad_hidden_two, mixed_rows, upstream_low, rotated_query, key_rot, value_low, raw, gains, cos2, sin2,
-        prob_low, full_output, full_qkv, expert_out, grads, got,
-    )
-    tokens_grad, qkv_shard, output_shard, gain_sum = last_call(
-        grad_hidden_one, grad_mixed, inputs_low, grad_qkv_low, grad_proj_low, attended_low, gains, gain_grads
-    )
-    shards = grads[:, :, :part].astype(f32) + got[:, :, :part].astype(f32) + got2.astype(f32)
-    down_shard, gate_shard, up_shard = (x.reshape(group, hidden, part) for x in shards)
+        for m, (first, second) in enumerate(((got[0], got2[0]), (got[1], got2[1]), (got_up, got2_up)))
+    )
     own_head = lambda row: lax.dynamic_slice_in_dim(gain_sum[row], own_place, nq, 0)
     return (
         output,
         tokens_grad,
         gain_sum[0:2].reshape(-1),
-        qkv_shard[:, :q_cols],
-        qkv_shard[:, q_cols : q_cols + k_cols],
-        qkv_shard[:, q_cols + k_cols :],
+        query_shard,
+        key_shard,
+        value_shard,
         output_shard,
         own_head(4),
         own_head(5),

time: 581 us -> 503 us (0.87)
  Pallas kernels: 520 us -> 463 us
  other arithmetic: 24.7 us -> 15.5 us
  local copies, waits for them, and re-layouts: 26 us -> 18 us
    pallas_call x1, Pallas kernels: 210 us -> 160 us  [forward_call(): pl.pallas_call(forward_kernel, out_shape=[o[0] for o in outs], in_specs=[...]
    concatenate x5 -> x1, other arithmetic: 14.9 us -> 0.84 us  [local_fast(): sin2 = jnp.concatenate([-sine_table[:, 0], sine_table[:, 0]], 1)]
    squeeze x0 -> x1, local copies, waits for them, and re-layouts: none -> 6.29 us  [local_fast(): got[0]]
    slice x4 -> x0, local copies, waits for them, and re-layouts: 6.04 us -> none  [the longest x1 2.31 us: local_fast(): qkv_shard[:, :q_cols]]
  transfers between devices with their start and end apart: 2 -> 0, of which waited for: 0 -> 0; matrix products, arithmetic and copies ran while one was open for 3% -> 0% of each run, Pallas kernels for 37% -> 0%
where the time goes in v2:
time: 503 us; the launch traced here: 498 us
  Pallas kernels  463 us (92%)
  local copies, waits for them, and re-layouts  18 us (4%)
  other arithmetic  15.5 us (3%)
    pallas_call x1, Pallas kernels, forward_call(): pl.pallas_call(forward_kernel, out_shape=[o[0] for o in outs], in_specs=[...  160 us
    pallas_call x1, Pallas kernels, expert_call(): pl.pallas_call(expert_kernel, out_shape=[shape((rows, width), bf16), shap...  148 us
    pallas_call x1, Pallas kernels, attention_back_call(): pl.pallas_call(attention_back_kernel, out_shape=[shape((rows, width), bf1...  78.1 us
    pallas_call x1, Pallas kernels, last_call(): pl.pallas_call(last_kernel, out_shape=[shape((rows, width), f32), shape((...  76.6 us

profile of v2, /device:TPU:0, one launch (start us, length us, event | category | flops | bytes accessed | tf_op | source)
XLA Modules:
  0.0 497.9 jit_solution(13036401340569106263)
XLA Ops:
  1.3 0.7 bitcast_convert_fusion.1
  2.0 0.7 bitcast_convert_fusion
  2.6 0.1 dynamic_update_slice.8
  2.7 0.1 dynamic_update_slice.9
  2.9 0.7 bitcast_convert_fusion.3
  3.5 0.7 bitcast_convert_fusion.2
  4.2 0.6 concatenate.9.gains_own
  4.8 0.6 compare_convert_fusion.key_ok
  5.4 1.6 copy.29.ids
  6.9 1.6 copy.30.weight
  8.5 1.0 fusion.3
  9.5 0.8 pad_maximum_fusion.1.sin
  10.3 0.8 pad_maximum_fusion.cos
  11.2 160.5 %forward_to_experts.1 = (bf16[512,2048]{1,0:T(8,128)(2,1)}, bf16[512,2048]{1,0:T(8,128)(2,1)}, f32[1024,128]{1,0:T(8,128)}, f32[512,2048]{1,0:T(8,128)}, bf16[10...) custom-call(bf16[512,2048]{1,0:T(8,128)(2,1)} %tokens_in.1, ...), custom_call_target="tpu_custom_call" | custom-call | flops 8000000000 | bytes 60000000 | tf_op jit(solution)/shard_map/forward_to_experts/pallas_call | solution.py:745
  171.6 147.7 %experts.1 = (bf16[512,2048]{1,0:T(8,128)(2,1)}, bf16[1024,2048]{1,0:T(8,128)(2,1)}, bf16[3,1536,2048]{2,1,0:T(8,128)(2,1)}, bf16[2,1536,1024]{2,1,0:T(8,128)(2,1)}) custom-call(bf16[1024,2048]{1,0:T(8,128)(2,1)} %get-tuple-element.50.h2, bf16[512,2048]{1,0:T(8,128)(2,1)} %cot_in.3, bf16[512,2048]{1,0:T(8,128)(2,1)} %get-tuple-element.51.g_other, ...), custom_call_target="tpu_custom_call" | custom-call | flops 57999998976 | bytes 60000000 | tf_op jit(solution)/shard_map/experts/pallas_call | solution.py:1122
  319.3 78.1 %attention_backward.1 = (bf16[512,2048]{1,0:T(8,128)(2,1)}, f32[512,2048]{1,0:T(8,128)}, bf16[512,2048]{1,0:T(8,128)(2,1)}, bf16[512,1280]{1,0:T(8,128)(2,1)}, b...) custom-call(f32[4,2,8,128]{3,2,1,0:T(8,128)} %get-tuple-element.49.gai, ...), custom_call_target="tpu_custom_call" | custom-call | flops 8999999488 | bytes 60000000 | tf_op jit(solution)/shard_map/attention_backward/pallas_call | solution.py:1372
  397.5 6.3 %slice_bitcast_fusion = (bf16[1536,1024]{1,0:T(8,128)(2,1)}, bf16[1536,1024]{1,0:T(8,128)(2,1)}) fusion(bf16[2,1536,1024]{2,1,0:T(8,128)(2,1)} %get-tuple-element.67.got), kind=kLoop, calls=%fused_computation.6 | loop fusion | bytes 12582912 | tf_op jit(solution)/shard_map/squeeze | solution.py:1748
  403.8 76.6 %input_gradients.1 = (f32[512,2048]{1,0:T(8,128)}, f32[256,1024]{1,0:T(8,128)}, f32[256,128]{1,0:T(8,128)}, f32[256,128]{1,0:T(8,128)}, f32[256,1024]{1,0:T(8,12...) custom-call(f32[4,2,8,128]{3,2,1,0:T(8,128)} %get-tuple-element.49.gains, f32[8,2048]{1,0:T(8,128)} %get-tuple-element.69.gain_grads, ...), custom_call_target="tpu_custom_call" | custom-call | flops 5000000000 | bytes 40000000 | tf_op jit(solution)/shard_map/input_gradients/pallas_call | solution.py:1618
  480.4 0.0 copy-start.6
  480.4 0.0 copy-start.1
  480.4 9.6 %convert_add_fusion = (f32[1536,512]{1,0:T(8,128)}, f32[1536,512]{1,0:T(8,128)}, f32[1536,512]{1,0:T(8,128)}) fusion(bf16[1536,1024]{1,0:T(8,128)(2,1)} %get-tuple-element.88, bf16[2,1536,512]{2,1,0:T(8,128)(2,1)} %get-tuple-element.83, bf16[3,1536,2048]{2,1,0:T(8,128)(2,1)} %get-tuple-element.66.grads, bf16[1536,1024]{1,0:T(8,128)(2,1)} %get-tuple-element.89, ...), kind=kLoop, calls=%fused_computation | loop fusion | flops 11796480 | bytes 23592960 | tf_op jit(solution)/shard_map/add | solution.py:1745
  490.0 0.0 copy-start
  490.0 0.0 copy-done.6
  490.0 0.6 slice_bitcast_fusion.2
  490.6 0.6 dynamic-slice_bitcast_fusion
  491.1 0.0 copy-done.1
  491.1 1.3 copy.40
  492.5 0.0 copy-done
  492.5 0.0 copy-start.3
  492.5 0.0 copy-start.5
  492.5 0.0 copy-start.4
  492.5 2.0 copy.41
  494.5 0.0 copy-done.3
  494.5 0.0 copy-start.2
  494.5 1.0 copy.42
  495.5 0.0 copy-done.5
  495.5 0.7 copy.43
  496.1 0.0 copy-done.4
  496.1 0.7 copy.44
  496.8 0.0 copy-done.2
  496.8 1.0 copy.45
  (5 shorter events, 0.0 us)
Async XLA Ops:
  480.4 9.6 %copy-start.6 = (f32[8,128]{1,0:T(8,128)S(1)}, f32[8,128]{1,0:T(8,128)}, u32[]{:S(2)}) copy-start(f32[8,128]{1,0:T(8,128)} %get-tuple-element.78) | copy-start | bytes 12292
  480.4 10.8 %copy-start.1 = (bf16[512,2048]{1,0:T(8,128)(2,1)S(1)}, bf16[512,2048]{1,0:T(8,128)(2,1)}, u32[]{:S(2)}) copy-start(bf16[512,2048]{1,0:T(8,128)(2,1)} %get-tuple-element.112) | copy-start | bytes 6291460
  490.0 2.5 copy-start
  492.5 2.0 copy-start.3
  492.5 3.0 copy-start.5
  492.5 3.7 copy-start.4
  494.5 2.3 copy-start.2

commit v3 on v2

--- a/solution.py
+++ b/solution.py
@@ -1,5 +1,6 @@
 import jax
 import jax.numpy as jnp
+import numpy as np
 from jax import lax
 from jax.experimental import pallas as pl
 from jax.experimental.pallas import tpu as pltpu
@@ -15,6 +16,14 @@
 
 def rms_scale(values):
     return lax.rsqrt(jnp.mean(values * values, axis=-1, keepdims=True) + epsilon)
+
+
+def rope_lanes(rows):
+    half = HEAD_SIZE // 2
+    frequency = np.power(np.float32(1000000.0), -(np.arange(half, dtype=np.float32) * np.float32(2.0 / HEAD_SIZE)))
+    angles = np.arange(rows, dtype=np.float32)[:, None] * frequency[None, :]
+    cos, sin = np.cos(angles), np.sin(angles)
+    return np.concatenate([cos, cos], 1), np.concatenate([-sin, sin], 1)
 
 
 def rope_tables(rows):
@@ -372,6 +381,7 @@
 
 
 CHUNKS = 16
+SECOND = (12, 18)
 
 
 def line_roles(axis):
@@ -476,9 +486,9 @@
 
 
 def forward_kernel(
-    tokens_in, cot_in, ids, weight, q_own, k_own, v_own, wo_own, gate_own, up_own, down_own, gains_own, cos, sin, key_ok,
+    tokens_in, cot_in, ids, weight, lengths, q_own, k_own, v_own, wo_own, gate_own, up_own, down_own, gains_in, cos, sin,
     tokens, cot, table, x2, h2, att, qrot, krot, value, raw, probs, gains, gate, up, down, qkv_out, wo_out,
-    qkv, wo, h1, proj, in_buf, mid_buf, part, summed, gain_rows,
+    qkv, wo, h1, proj, in_buf, mid_buf, part, summed, gain_rows, gains_own,
     w_send, w_recv, core_send, core_recv, g_send, g_recv, h_send, h_recv, own_sem, out_sem, r_send, r_recv, t_sem, *line,
 ):
     c = lax.axis_index("expert")
@@ -581,6 +591,9 @@
         x.start()
     for k in range(4):
         cot_away(k).start()
+    gains_own[...] = gains_in[...]
+    shift = (lax.axis_index("dp") * 2 + c) * (128 // 8)
+    gains_own[4:6] = pltpu.roll(gains_in[...], shift, 1)[4:6]
     for x in own_qkv:
         x.wait()
     begin(0)
@@ -588,11 +601,11 @@
         gain_move(j).start()
     gains[pl.ds(0, 1), pl.ds(c, 1)] = gains_own[...].reshape(1, 1, 8, 128)
     core_move(0, 0).start()
-    lane_index = lax.broadcasted_iota(jnp.int32, (rows, 128), 1)
-    routes = jnp.zeros((rows, 128), f32)
-    for j in range(ids.shape[1]):
-        routes += jnp.where(lane_index == ids[:, j : j + 1], weight[:, j : j + 1], 0.0)
-    table[0:rows] = routes
+    expert = lax.broadcasted_iota(jnp.int32, (128, rows), 0)
+    routes = jnp.zeros((128, rows), f32)
+    for j in range(ids.shape[0]):
+        routes += jnp.where(expert == ids[j : j + 1], weight[j : j + 1], 0.0)
+    table[0:rows] = routes.T
     table_away().start()
     for k in range(4):
         fetch[k].wait()
@@ -647,6 +660,7 @@
     krot[...] = spin(unit(raw[:, pl.ds(q_cols, 128)]) * gain_key).astype(bf16)
     value[...] = raw[:, pl.ds(q_cols + 128, 128)].astype(bf16)
     block = rows // 2
+    length = lengths[0]
 
     def head(h):
         col = pl.ds(pl.multiple_of(h * 128, 128), 128)
@@ -656,7 +670,7 @@
             s = nt(qrot[r, col], krot[0:n]) * 128 ** (-0.5)
             row = lax.broadcasted_iota(jnp.int32, (block, n), 0) + i * block
             key = lax.broadcasted_iota(jnp.int32, (block, n), 1)
-            s = jnp.where((key <= row) & (key_ok[:, 0:n] > 0), s, -1e30)
+            s = jnp.where((key <= row) & (key < length), s, -1e30)
             e = jnp.exp(s - jnp.max(s, axis=-1, keepdims=True))
             p = (e / jnp.sum(e, axis=-1, keepdims=True)).astype(bf16)
             probs[h, r, 0:n] = p
@@ -714,7 +728,7 @@
         gain_move(j).wait_send()
 
 
-def forward_call(tokens, cot, ids, weight, q_own, k_own, v_own, wo_own, gate_own, up_own, down_own, gains_own, cos, sin, key_ok):
+def forward_call(tokens, cot, ids, weight, lengths, q_own, k_own, v_own, wo_own, gate_own, up_own, down_own, gains, cos, sin):
     rows, width = tokens.shape
     q_cols = q_own.shape[1]
     qkv_cols = q_cols + k_own.shape[1] + v_own.shape[1]
@@ -745,13 +759,18 @@
     return pl.pallas_call(
         forward_kernel,
         out_shape=[o[0] for o in outs],
-        in_specs=[anyspace] * 2 + [vmem] * 2 + [anyspace] * 7 + [vmem] * 4,
+        in_specs=[anyspace] * 2
+        + [vmem] * 2
+        + [pl.BlockSpec(memory_space=pltpu.SMEM)]
+        + [anyspace] * 7
+        + [vmem] * 3,
         out_specs=[o[1] for o in outs],
         scratch_shapes=[
             pltpu.VMEM((width, qkv_cols), bf16),
             pltpu.VMEM((width, q_cols), bf16),
             big, big, big, big, big, big,
             pltpu.VMEM((2, width), f32),
+            pltpu.VMEM((8, 128), f32),
             dma((5, 6)), dma((5, 6)), dma((2, 4)), dma((2, 4)), dma((7,)), dma((7,)),
             dma((CHUNKS,)), dma((CHUNKS,)), dma((8,)), dma((2,)), dma((5,)), dma((5,)), dma((4,)),
         ] + line_sems(),
@@ -760,7 +779,7 @@
         ),
         cost_estimate=pl.CostEstimate(flops=8 * 10**9, bytes_accessed=60 * 10**6, transcendentals=2 * 10**6),
         name="forward_to_experts",
-    )(tokens, cot, ids, weight, q_own, k_own, v_own, wo_own, gate_own, up_own, down_own, gains_own, cos, sin, key_ok)
+    )(tokens, cot, ids, weight, lengths, q_own, k_own, v_own, wo_own, gate_own, up_own, down_own, gains, cos, sin)
 
 
 def turn(i):
@@ -821,7 +840,7 @@
 
 def expert_kernel(
     h2, g_own, g_other, mine, gate_own, up_own, down_own, gate_in, up_in, down_in,
-    grad_h2, out, grads, got,
+    grad_h2, out, out_other, grads, got,
     g, g_sem, gate, up, down, acts, drow, rbuf, in_buf, mid_buf, stage,
     load_sem, rest_sem, w_send, w_recv, x_send, x_recv, s_send, s_recv, keep_sem, out_sem, *line,
 ):
@@ -905,47 +924,54 @@
         acts[2, :, tile(i)] = (grad_act * silu).astype(bf16)
         acts[1, :, tile(i)] = (grad_act * up_value * sig * (1.0 + gate_value * (1.0 - sig))).astype(bf16)
 
-    def parts(v):
-        return v // 6, (v % 6) // 2, 1 - v % 2
-
-    def keep(v, ab):
-        m, q, s = parts(v)
+    early_unit = lambda e: (e // 4, (e % 4) // 2, 1 - e % 2, e)
+    last_unit = lambda e: (e // 2, 2, 1 - e % 2, 8 + e)
+    up_unit = lambda e: (2, e // 2, 1 - e % 2, 12 + e)
+
+    def keep(unit, ab):
+        m, q, s, n = unit
         cols = pl.ds(pl.multiple_of(s * 2 * wide, 2 * wide), 2 * wide)
         return pltpu.make_async_copy(
-            stage.at[v % 2, pl.ds(ab * 256, 256)], grads.at[m, tile(q + 3 * ab), cols], keep_sem.at[v % 2, ab]
+            stage.at[n % 2, pl.ds(ab * 256, 256)], grads.at[m, tile(q + 3 * ab), cols], keep_sem.at[n % 2, ab]
         )
 
     def send(m, t, j, first):
         came = lambda t, cols: got.at[m, tile(t), cols]
         return first_exchange(m, t, j, first, grads, came, s_send.at[m, t, j], s_recv.at[m, t, j], to, wide)
 
-    def flush(v):
-        m, q, s = parts(v)
+    def flush(unit, goes=True):
+        m, q, s, n = unit
         for ab in range(2):
-            keep(v, ab).wait()
-
-        @pl.when((m < 2) & (s == 1))
+            keep(unit, ab).wait()
+
+        @pl.when(goes & (s == 1))
         def _():
             send(m, q, 1, 1).start()
             send(m, q + 3, 0, 2).start()
             send(m, q + 3, 1, 2).start()
 
-        @pl.when((m < 2) & (s == 0))
+        @pl.when(goes & (s == 0))
         def _():
             send(m, q, 0, 1).start()
 
-    def grad_unit(v, rhs):
-        m, q, s = parts(v)
+    def grad_unit(unit, rhs):
+        m, q, s, n = unit
         low = acts[m, :, pl.ds(pl.multiple_of(q * 512, 512), 512)]
-        for n in range(2):
-            cols = pl.ds(pl.multiple_of((2 * s + n) * wide, wide), wide)
-            stage[v % 2, :, n * wide : (n + 1) * wide] = tn(low, rhs[:, cols]).astype(bf16)
+        for b in range(2):
+            cols = pl.ds(pl.multiple_of((2 * s + b) * wide, wide), wide)
+            stage[n % 2, :, b * wide : (b + 1) * wide] = tn(low, rhs[:, cols]).astype(bf16)
         for ab in range(2):
-            keep(v, ab).start()
-
-        @pl.when(v > 0)
-        def _():
-            flush(v - 1)
+            keep(unit, ab).start()
+
+    def early_grads(rhs):
+        def one(e):
+            grad_unit(early_unit(e), rhs)
+
+            @pl.when(e > 0)
+            def _():
+                flush(early_unit(e - 1))
+
+        return one
 
     def early_tile(i):
         for x in (load_own, load_rest):
@@ -960,12 +986,14 @@
         drow[:, col] = (nn(acts[1, :, 0:late], gate[0:late, col]) + nn(acts[2, :, 0:late], up[0:late, col])).astype(bf16)
 
     over(width // 256, early_rows)
-    over(2, lambda v: grad_unit(v, g))
+    over(2, early_grads(g))
     for j in range(3):
         for n in (0, 1):
             shard_move(j, n).wait_recv()
             shard_move(j, 4 + n).start()
-    over(4, lambda v: grad_unit(v, g), 2)
+    over(4, early_grads(g), 2)
+    over(8, early_grads(h2), 4)
+    flush(early_unit(7))
     for i in (4, 5):
         for j in range(3):
             load_own(i, j).wait()
@@ -997,43 +1025,56 @@
         r = pl.ds(pl.multiple_of(c * step, step), step)
         drow[r] = (drow[r].astype(f32) + rbuf[r].astype(f32)).astype(bf16)
 
-    def out_copy(j):
+    def out_copies(j):
         col = pl.ds(pl.multiple_of(j * 256, 256), 256)
-        return pltpu.make_async_copy(gate.at[pl.ds(0, 2 * rows), col], out.at[:, col], out_sem.at[j])
+        return (
+            pltpu.make_async_copy(gate.at[pl.ds(0, rows), col], out.at[:, col], out_sem.at[0, j]),
+            remote(
+                gate.at[pl.ds(rows, rows), col], out_other.at[:, col], out_sem.at[1, j], out_sem.at[2, j], to[0, 1]
+            ),
+        )
 
     def work(i):
         @pl.when(i < 2)
         def _():
-            grad_unit(4 + i, g)
-
-        @pl.when((i >= 2) & (i < 14))
-        def _():
-            grad_unit(4 + i, h2)
-
-        @pl.when(i == 14)
-        def _():
-            flush(17)
-
-        @pl.when(i >= 14)
-        def _():
-            j = i - 14
+            grad_unit(last_unit(i), g)
+
+        @pl.when((i >= 2) & (i < 4))
+        def _():
+            grad_unit(last_unit(i), h2)
+
+        @pl.when((i >= 4) & (i < 10))
+        def _():
+            grad_unit(up_unit(i - 4), h2)
+
+        @pl.when((i >= 1) & (i < 5))
+        def _():
+            flush(last_unit(i - 1))
+
+        @pl.when((i >= 5) & (i < 11))
+        def _():
+            flush(up_unit(i - 5), i < 7)
+
+        @pl.when(i >= 10)
+        def _():
+            j = i - 10
             col = pl.ds(pl.multiple_of(j * 256, 256), 256)
             gate[0 : 2 * rows, col] = nn(acts[0], down[:, col]).astype(bf16)
-            out_copy(j).start()
+            for x in out_copies(j):
+                x.start()
 
     line_sum_work(
         drow, in_buf, mid_buf, drow, grad_h2, line, "tensor", rows, add_other, lambda r, c: None, work,
-        14 + width // 256,
-    )
-    over(width // 256, lambda j: out_copy(j).wait())
+        10 + width // 256,
+    )
+    over(width // 256, lambda j: [x.wait() for x in out_copies(j)])
     over(CHUNKS, lambda i: give(i).wait_send())
     for j in range(3):
         for n in range(6):
             shard_move(j, n).wait_send()
-    for m in range(2):
-        for t in range(6):
-            for j in range(2):
-                send(m, t, j, 1 + t // 3).wait()
+    for m, t in [(m, t) for m in range(2) for t in range(6)] + [(2, 0), (2, 3)]:
+        for j in range(2):
+            send(m, t, j, 1 + t // 3).wait()
 
 
 def line_sum_work(x_ref, in_buf, mid_buf, part, out_ref, sems, axis, n_rows, ready, finish, work, n_work):
@@ -1123,12 +1164,13 @@
         expert_kernel,
         out_shape=[
             shape((rows, width), bf16),
-            shape((2 * rows, width), bf16),
+            shape((rows, width), bf16),
+            shape((rows, width), bf16),
             shape((3, tall, width), bf16),
-            shape((2, tall, width // 2), bf16),
+            shape((3, tall, width // 2), bf16),
         ],
         in_specs=[vmem, anyspace, anyspace, vmem] + [anyspace] * 6,
-        out_specs=[vmem, anyspace, anyspace, anyspace],
+        out_specs=[vmem, anyspace, anyspace, anyspace, anyspace],
         scratch_shapes=[pltpu.VMEM((2 * rows, width), bf16), dma((5,))]
         + [pltpu.VMEM((tall, width), bf16)] * 3
         + [
@@ -1138,8 +1180,8 @@
             pltpu.VMEM((rows, width), bf16),
             pltpu.VMEM((rows, width), bf16),
             pltpu.VMEM((2, 512, width // 2), bf16),
-            dma((6, 3)), dma((4, 3)), dma((3, 6)), dma((3, 6)), dma((CHUNKS,)), dma((CHUNKS,)), dma((2, 6, 2)), dma((2, 6, 2)),
-            dma((2, 2)), dma((width // 256,)),
+            dma((6, 3)), dma((4, 3)), dma((3, 6)), dma((3, 6)), dma((CHUNKS,)), dma((CHUNKS,)), dma((3, 6, 2)), dma((3, 6, 2)),
+            dma((2, 2)), dma((3, width // 256)),
         ]
         + line_sems(),
         compiler_params=pltpu.CompilerParams(
@@ -1179,11 +1221,11 @@
 
 
 def attention_back_kernel(
-    gains, cos, sin, grad_h2_in, x2_in, cot_in, qrot_in, krot_in, value_in, raw_in, probs, wo_in, qkv_in, out_part,
-    grads, got,
-    output, dx2, low, grad_qkv, grad_h1, gain_grads, got2, got_up,
-    grad_h2, x2, cot, qrot, krot, value, raw, f_sem, wo, qkv, own_out, rbuf, in_buf, mid_buf, summed, datt, pbuf, dk, dv, gain_rows, load_a, load_b, on_buf,
-    w_sem, p_sem, l_sem, x_send, x_recv, s_send, s_recv, u_send, u_recv, *line,
+    gains, cos, sin, grad_h2_in, x2_in, cot_in, qrot_in, krot_in, value_in, raw_in, probs, wo_in, qkv_in, out_own, out_other,
+    grads, _,
+    output, dx2_out, low_out, grad_qkv, grad_h1, gain_grads, got2, got,
+    grad_h2, x2, cot, qrot, krot, value, raw, f_sem, dx2, low, wo, qkv, own_out, rbuf, in_buf, mid_buf, summed, datt, pbuf, dk, dv, gain_rows, load_a, load_b, on_buf,
+    w_sem, p_sem, l_sem, s_send, s_recv, u_send, u_recv, *line,
 ):
     to = plane_partners()
     fetch = [
@@ -1202,32 +1244,31 @@
     step = rows // CHUNKS
     rate = 128 ** (-0.5)
 
-    def give(i):
-        src = out_part.at[pl.ds(pl.multiple_of(rows + i * step, step), step)]
-        dst = rbuf.at[pl.ds(pl.multiple_of(i * step, step), step)]
-        return remote(src, dst, x_send.at[i], x_recv.at[i], to[0, 1])
-
-    over(CHUNKS, lambda i: give(i).start())
     weights = [
         pltpu.make_async_copy(wo_in, wo, w_sem.at[0]),
         pltpu.make_async_copy(qkv_in, qkv, w_sem.at[1]),
-        pltpu.make_async_copy(out_part.at[pl.ds(0, rows)], own_out, w_sem.at[2]),
+        pltpu.make_async_copy(out_own, own_out, w_sem.at[2]),
+        pltpu.make_async_copy(out_other, rbuf, w_sem.at[3]),
     ]
-    for w in [weights[2]] + early + [weights[0]] + fetch[2:] + [weights[1]]:
+    flushes = [
+        pltpu.make_async_copy(dx2, dx2_out, w_sem.at[4]),
+        pltpu.make_async_copy(low, low_out, w_sem.at[5]),
+    ]
+    for w in weights[2:] + early + [weights[0]] + fetch[2:] + [weights[1]]:
         w.start()
 
     def load_probs(h):
         return pltpu.make_async_copy(probs.at[h], pbuf.at[h % 2], p_sem.at[h % 2])
 
     def up_move(t, j, first):
-        came = lambda t, cols: got_up.at[tile(t), cols]
+        came = lambda t, cols: got.at[2, tile(t), cols]
         return first_exchange(2, t, j, first, grads, came, u_send.at[t, j], u_recv.at[t, j], to, wide)
 
     def up_moves(i, f):
         t = turn(i)
         by_half(t, lambda first: [f(up_move(t, j, first)) for j in range(2)])
 
-    over(6, lambda i: up_moves(i, lambda x: x.start()))
+    over(6, lambda i: up_moves(i, lambda x: x.start()), 2)
     at = lambda ref: lambda u, cols=pl.ds(0, wide): ref.at[u // 6, tile(turn(u % 6)), cols]
     start, second_tile, second_done = second_exchange(
         12, at(grads), at(got), at(got2), load_a, load_b, on_buf, l_sem, s_send, s_recv, to, wide
@@ -1315,6 +1356,8 @@
         @pl.when(i == 4)
         def _():
             weights[0].wait()
+            for x in flushes:
+                x.start()
             for x in fetch[2:]:
                 x.wait()
 
@@ -1342,8 +1385,8 @@
         @pl.when(c == 0)
         def _():
             weights[2].wait()
-
-        give(c).wait_recv()
+            weights[3].wait()
+
         r = pl.ds(pl.multiple_of(c * step, step), step)
         own_out[r] = (own_out[r].astype(f32) + rbuf[r].astype(f32)).astype(bf16)
 
@@ -1355,12 +1398,13 @@
     line_sum_work(
         own_out, in_buf, mid_buf, own_out, summed, line, "tensor", rows, ready, finish, work, 11 + n_heads
     )
-    over(CHUNKS, lambda i: give(i).wait_send())
+    for x in flushes:
+        x.wait()
     second_done()
-    over(6, lambda i: up_moves(i, lambda x: x.wait()))
-
-
-def attention_back_call(grad_h2, x2, cot, qrot, krot, value, raw, gains, cos, sin, probs, wo, qkv, out_part, grads, got):
+    over(6, lambda i: up_moves(i, lambda x: x.wait()), 2)
+
+
+def attention_back_call(grad_h2, x2, cot, qrot, krot, value, raw, gains, cos, sin, probs, wo, qkv, out_own, out_other, grads, got):
     rows, width = x2.shape
     q_cols, qkv_cols = wo.shape[1], qkv.shape[1]
     tall = grads.shape[1]
@@ -1379,10 +1423,10 @@
             shape((rows, width), bf16),
             shape((8, width), f32),
             shape((2, tall, wide), bf16),
-            shape((tall, 2 * wide), bf16),
+            shape(got.shape, bf16),
         ],
-        in_specs=[vmem] * 3 + [anyspace] * 13,
-        out_specs=[vmem] * 6 + [anyspace] * 2,
+        in_specs=[vmem] * 3 + [anyspace] * 14,
+        out_specs=[vmem, anyspace, anyspace] + [vmem] * 3 + [anyspace] * 2,
         scratch_shapes=[
             big,
             pltpu.VMEM((rows, width), f32),
@@ -1392,6 +1436,8 @@
             pltpu.VMEM((rows, 128), bf16),
             pltpu.VMEM((rows, qkv_cols), f32),
             dma((10,)),
+            pltpu.VMEM((rows, width), f32),
+            big,
             pltpu.VMEM((width, q_cols), bf16),
             pltpu.VMEM((width, qkv_cols), bf16),
             big, big, big, big, big,
@@ -1403,22 +1449,23 @@
             pltpu.VMEM((2, 256, wide), bf16),
             pltpu.VMEM((2, 256, wide), bf16),
             pltpu.VMEM((12, 256, wide), bf16),
-            dma((3,)), dma((2,)), dma((2, 2)), dma((CHUNKS,)), dma((CHUNKS,)), dma((12,)), dma((12,)),
+            dma((6,)), dma((2,)), dma((2, 2)), dma((12,)), dma((12,)),
             dma((6, 2)), dma((6, 2)),
         ]
         + line_sems(),
+        input_output_aliases={16: 7},
         compiler_params=pltpu.CompilerParams(
             collective_id=3, has_side_effects=True, vmem_limit_bytes=62 * 2**20
         ),
         cost_estimate=pl.CostEstimate(flops=9 * 10**9, bytes_accessed=60 * 10**6, transcendentals=10**5),
         name="attention_backward",
-    )(gains, cos, sin, grad_h2, x2, cot, qrot, krot, value, raw, probs, wo, qkv, out_part, grads, got)
+    )(gains, cos, sin, grad_h2, x2, cot, qrot, krot, value, raw, probs, wo, qkv, out_own, out_other, grads, got)
 
 
 def last_kernel(
-    gains, gain_grads, part_in, dx2_in, tokens_in, grad_qkv_in, low_in, att_in, grads, got_up,
-    tokens_grad, q_shard, k_shard, v_shard, wo_shard, gain_sum, got2_up,
-    part, dx2, tokens, grad_qkv, low, att, f_sem, h1, in_buf, mid_buf, half_sum, summed, gain_rows, wo_all, qkv_all, wo_core, qkv_core, wo_one, qkv_one, wo_two, qkv_two,
+    gains, gain_grads, part_in, dx2_in, tokens_in, grad_qkv_in, low_in, att_in, grads, got,
+    tokens_grad_out, q_shard, k_shard, v_shard, wo_shard, gain_sum, got2_up,
+    tokens_grad, d_sem, part, dx2, tokens, grad_qkv, low, att, f_sem, h1, in_buf, mid_buf, half_sum, summed, gain_rows, wo_all, qkv_all, wo_core, qkv_core, wo_one, qkv_one, wo_two, qkv_two,
     ga, z_got, g_out, g_got, load_a, load_b, on_buf, l_sem, s_send, s_recv,
     z_send, z_recv, c_send, c_recv, f_send, f_recv, t_send, t_recv, g_send, g_recv, *line,
 ):
@@ -1448,9 +1495,9 @@
 
     for j in range(3):
         z_move(j).start()
-    up_at = lambda ref: lambda u, cols=pl.ds(0, wide): ref.at[tile(turn(u)), cols]
+    up_at = lambda ref: lambda u, cols: ref.at[2, tile(turn(u)), cols]
     start, second_tile, second_done = second_exchange(
-        6, lambda u, cols: grads.at[2, tile(turn(u)), cols], up_at(got_up), up_at(got2_up),
+        6, up_at(grads), up_at(got), lambda u: got2_up.at[tile(turn(u))],
         load_a, load_b, on_buf, l_sem, s_send, s_recv, to, wide,
     )
     start(0)
@@ -1482,17 +1529,15 @@
         left, right, full = mats[m][:3]
         full[block(k, core)] = tn(left[:, block(k, core)], right[...]).astype(bf16)
 
-    def away(k):
-        for m in range(2):
-            product(m, k, 1 - c)
-            core_move(m, k).start()
-
-    def home(k):
-        for m in range(2):
-            product(m, k, c)
-            full, came = mats[m][2:4]
-            core_move(m, k).wait_recv()
-            full[block(k, c)] = (full[block(k, c)].astype(f32) + came[k].astype(f32)).astype(bf16)
+    def away(m, k):
+        product(m, k, 1 - c)
+        core_move(m, k).start()
+
+    def home(m, k):
+        product(m, k, c)
+        full, came = mats[m][2:4]
+        core_move(m, k).wait_recv()
+        full[block(k, c)] = (full[block(k, c)].astype(f32) + came[k].astype(f32)).astype(bf16)
 
     def slot(m, k, h):
         return mats[m][2].at[pl.ds(pl.multiple_of((k * 2 + c) * piece + h * half, half), half)]
@@ -1522,27 +1567,30 @@
         def _():
             second_tile(i)
 
-        for n, k in enumerate((3, 1, 2, 0)):
-
-            @pl.when(i == 1 + n)
-            def _(k=k):
-                away(k)
-
-            @pl.when(i == 5 + n)
-            def _(k=k, n=n):
-                home(k)
-                if n in (1, 2):
-                    for m in range(2):
-                        for j in range(2):
-                            first_move(m, n - 1, j).start()
-
-        for h in range(2):
-
-            @pl.when(i == 17 + h)
-            def _(h=h):
-                for m in range(2):
+        for m in range(2):
+            for n, ks in enumerate(((3, 1), (2, 0))):
+
+                @pl.when(i == 1 + 4 * m + n)
+                def _(m=m, ks=ks):
+                    for k in ks:
+                        away(m, k)
+
+                @pl.when(i == 3 + 4 * m + n)
+                def _(m=m, n=n, ks=ks):
+                    for k in ks:
+                        home(m, k)
+                    for j in range(2):
+                        first_move(m, n, j).start()
+
+            @pl.when(i == SECOND[m])
+            def _(m=m):
+                for h in range(2):
                     add_first(m, h, 1, 2 - h)
                     second_move(m, h).start()
+
+    def give_back(i):
+        r = pl.ds(pl.multiple_of(i * (rows // CHUNKS), rows // CHUNKS), rows // CHUNKS)
+        return pltpu.make_async_copy(tokens_grad.at[r], tokens_grad_out.at[r], d_sem.at[i])
 
     def finish(r, i):
         grad = summed[r].astype(f32)
@@ -1552,6 +1600,7 @@
         d = dx2[r] + scale * (n - normed * jnp.mean(n * normed, axis=-1, keepdims=True))
         for k in range(4):
             tokens_grad[r, pl.ds(pl.multiple_of(places[k] * wide, wide), wide)] = d[:, k * wide : (k + 1) * wide]
+        give_back(i).start()
 
     fetch[0].wait()
     line_sum_work(part, in_buf, mid_buf, half_sum, summed, line, "tensor", rows, lambda k: None, finish, work, 20)
@@ -1595,6 +1644,7 @@
         total += g_got[j]
     gain_sum[...] = total
     second_done()
+    over(CHUNKS, lambda i: give_back(i).wait())
     for m in range(2):
         for k in range(4):
             core_move(m, k).wait_send()
@@ -1606,7 +1656,7 @@
         gain_move(j).wait_send()
 
 
-def last_call(part, dx2, tokens, grad_qkv, low, att, gains, gain_grads, grads, got_up):
+def last_call(part, dx2, tokens, grad_qkv, low, att, gains, gain_grads, grads, got):
     rows, width = tokens.shape
     q_cols, qkv_cols = att.shape[1], grad_qkv.shape[1]
     piece = width // 8
@@ -1624,11 +1674,13 @@
             shape((piece, (qkv_cols - q_cols) // 2), f32),
             shape((piece, q_cols), f32),
             shape((8, 128), f32),
-            shape((got_up.shape[0], width // 4), bf16),
+            shape((got.shape[1], width // 4), bf16),
         ],
         in_specs=[vmem] * 2 + [pl.BlockSpec(memory_space=pl.ANY)] * 8,
-        out_specs=[vmem] * 6 + [pl.BlockSpec(memory_space=pl.ANY)],
+        out_specs=[pl.BlockSpec(memory_space=pl.ANY)] + [vmem] * 5 + [pl.BlockSpec(memory_space=pl.ANY)],
         scratch_shapes=[
+            pltpu.VMEM((rows, width), f32),
+            dma((CHUNKS,)),
             big,
             pltpu.VMEM((rows, width), f32),
             big,
@@ -1660,7 +1712,7 @@
         ),
         cost_estimate=pl.CostEstimate(flops=5 * 10**9, bytes_accessed=40 * 10**6, transcendentals=10**5),
         name="input_gradients",
-    )(gains, gain_grads, part, dx2, tokens, grad_qkv, low, att, grads, got_up)
+    )(gains, gain_grads, part, dx2, tokens, grad_qkv, low, att, grads, got)
 
 
 def local_fast(
@@ -1696,21 +1748,12 @@
     heads_query, heads_key = q_cols // HEAD_SIZE, k_cols // HEAD_SIZE
     per_group = heads_query // heads_key
     own_place = (me_dp * n_ex + me_ex) * nq
-    placed = lambda v: lax.dynamic_update_slice(jnp.zeros((128,), f32), v.astype(f32), (own_place,))
+    fill = jnp.zeros((128 - nq,), bf16)
     gains_own = jnp.concatenate(
-        [
-            attention_norm.astype(f32).reshape(-1, 128),
-            experts_norm.astype(f32).reshape(-1, 128),
-            placed(query_norm)[None],
-            placed(key_norm)[None],
-            jnp.zeros((2, 128), f32),
-        ],
-        0,
-    )
-    cosine_table, sine_table = rope_tables(rows)
-    cos2 = jnp.concatenate([cosine_table[:, 0], cosine_table[:, 0]], 1)
-    sin2 = jnp.concatenate([-sine_table[:, 0], sine_table[:, 0]], 1)
-    key_ok = (jnp.arange(rows, dtype=jnp.int32) < length).astype(f32)[None]
+        [attention_norm, experts_norm, query_norm, fill, key_norm, fill, jnp.zeros((256,), bf16)]
+    )
+    gains_own = gains_own.reshape(8, 128).astype(f32)
+    cos2, sin2 = rope_lanes(rows)
     own_experts = [w.reshape(flat, part) for w in (gate_weight, up_weight, down_weight)]
     (
         inputs_low, upstream_other, table, mixed_rows, hidden_all, attended_low, rotated_query, key_rot, value_low, raw,
@@ -1718,8 +1761,9 @@
     ) = forward_call(
         tokens,
         cotangent,
-        route_ids,
-        route_weight,
+        route_ids.T,
+        route_weight.T,
+        lengths,
         query_weight,
         key_matrix,
         value_matrix,
@@ -1728,24 +1772,21 @@
         gains_own,
         cos2,
         sin2,
-        key_ok,
-    )
-    grad_hidden_two, expert_out, grads, got = expert_call(
+    )
+    grad_hidden_two, out_own, out_other, grads, got = expert_call(
         hidden_all, cotangent, upstream_other, table, *own_experts, gate_full, up_full, down_full
     )
-    output, grad_mixed, grad_proj_low, grad_qkv_low, grad_hidden_one, gain_grads, got2, got_up = attention_back_call(
+    output, grad_mixed, grad_proj_low, grad_qkv_low, grad_hidden_one, gain_grads, got2, got = attention_back_call(
         grad_hidden_two, mixed_rows, cotangent, rotated_query, key_rot, value_low, raw, gains, cos2, sin2,
-        prob_low, full_output, full_qkv, expert_out, grads, got,
+        prob_low, full_output, full_qkv, out_own, out_other, grads, got,
     )
     tokens_grad, query_shard, key_shard, value_shard, output_shard, gain_sum, got2_up = last_call(
         grad_hidden_one, grad_mixed, inputs_low, grad_qkv_low, grad_proj_low, attended_low, gains, gain_grads,
-        grads, got_up,
+        grads, got,
     )
     down_shard, gate_shard, up_shard = (
-        (grads[m, :, :part].astype(f32) + first[:, :part].astype(f32) + second.astype(f32)).reshape(
-            group, hidden, part
-        )
-        for m, (first, second) in enumerate(((got[0], got2[0]), (got[1], got2[1]), (got_up, got2_up)))
+        (grads[m, :, :part].astype(f32) + got[m, :, :part].astype(f32) + last.astype(f32)).reshape(group, hidden, part)
+        for m, last in enumerate((got2[0], got2[1], got2_up))
     )
     own_head = lambda row: lax.dynamic_slice_in_dim(gain_sum[row], own_place, nq, 0)
     return (

time: 503 us -> 470 us (0.934)
  Pallas kernels: 463 us -> 443 us
  local copies, waits for them, and re-layouts: 18 us -> 10.5 us
    pallas_call x1, Pallas kernels: 78.1 us -> 68.9 us  [attention_back_call(): pl.pallas_call(attention_back_kernel, out_shape=[shape((rows, width), bf1...]
    pallas_call x1, Pallas kernels: 76.6 us -> 69.7 us  [last_call(): pl.pallas_call(last_kernel, out_shape=[shape((rows, width), f32), shape((...]
    squeeze x1 -> x0, local copies, waits for them, and re-layouts: 6.29 us -> none  [local_fast(): got[0]]
    add x1 -> x2, other arithmetic: 9.57 us -> 10.1 us  [local_fast(): grads[m, :, :part].astype(f32) + got[m, :, :part].astype(f32)]
where the time goes in v3:
time: 470 us; the launch traced here: 466 us
  Pallas kernels  443 us (94%)
  other arithmetic  10.7 us (2%)
  local copies, waits for them, and re-layouts  10.5 us (2%)
    pallas_call x1, Pallas kernels, forward_call(): pl.pallas_call(forward_kernel, out_shape=[o[0] for o in outs], in_specs=[...  160 us
    pallas_call x1, Pallas kernels, expert_call(): pl.pallas_call(expert_kernel, out_shape=[shape((rows, width), bf16), shap...  144 us
    pallas_call x1, Pallas kernels, last_call(): pl.pallas_call(last_kernel, out_shape=[shape((rows, width), f32), shape((...  69.7 us
    pallas_call x1, Pallas kernels, attention_back_call(): pl.pallas_call(attention_back_kernel, out_shape=[shape((rows, width), bf1...  68.9 us
    add x2, other arithmetic, local_fast(): grads[m, :, :part].astype(f32) + got[m, :, :part].astype(f32)  10.1 us

profile of v3, /device:TPU:0, one launch (start us, length us, event | category | flops | bytes accessed | tf_op | source)
XLA Modules:
  0.0 466.4 jit_solution(13064158092460710673)
XLA Ops:
  0.7 2.8 concatenate.3
  3.4 0.6 bitcast_convert_fusion.gains_in
  4.7 160.4 %forward_to_experts.1 = (bf16[512,2048]{1,0:T(8,128)(2,1)}, bf16[512,2048]{1,0:T(8,128)(2,1)}, f32[1024,128]{1,0:T(8,128)}, f32[512,2048]{1,0:T(8,128)}, bf16[10...) custom-call(bf16[512,2048]{1,0:T(8,128)(2,1)} %tokens_in.1, ...), custom_call_target="tpu_custom_call" | custom-call | flops 8000000000 | bytes 60000000 | tf_op jit(solution)/shard_map/forward_to_experts/pallas_call | solution.py:759
  165.1 144.3 %experts.1 = (bf16[512,2048]{1,0:T(8,128)(2,1)}, bf16[512,2048]{1,0:T(8,128)(2,1)}, bf16[512,2048]{1,0:T(8,128)(2,1)}, bf16[3,1536,2048]{2,1,0:T(8,128)(2,1)}, bf16[3,1536,1024]{2,1,0:T(8,128)(2,1)}) custom-call(bf16[1024,2048]{1,0:T(8,128)(2,1)} %get-tuple-element.51.h2, bf16[512,2048]{1,0:T(8,128)(2,1)} %cot_in.3, ...), custom_call_target="tpu_custom_call" | custom-call | flops 57999998976 | bytes 60000000 | tf_op jit(solution)/shard_map/experts/pallas_call | solution.py:1163
  309.4 68.9 %attention_backward.1 = (bf16[512,2048]{1,0:T(8,128)(2,1)}, f32[512,2048]{1,0:T(8,128)}, bf16[512,2048]{1,0:T(8,128)(2,1)}, bf16[512,1280]{1,0:T(8,128)(2,1)}, b...) custom-call(f32[4,2,8,128]{3,2,1,0:T(8,128)} %get-tuple-element.50.g, ...), custom_call_target="tpu_custom_call", output_to_operand_aliasing={{7}: (16, {})} | custom-call | flops 8999999488 | bytes 60000000 | tf_op jit(solution)/shard_map/attention_backward/pallas_call | solution.py:1416
  378.4 69.7 %input_gradients.1 = (f32[512,2048]{1,0:T(8,128)}, f32[256,1024]{1,0:T(8,128)}, f32[256,128]{1,0:T(8,128)}, f32[256,128]{1,0:T(8,128)}, f32[256,1024]{1,0:T(8,12...) custom-call(f32[4,2,8,128]{3,2,1,0:T(8,128)} %get-tuple-element.50.gains, f32[8,2048]{1,0:T(8,128)} %get-tuple-element.71.gain_grads, ...), custom_call_target="tpu_custom_call" | custom-call | flops 5000000000 | bytes 40000000 | tf_op jit(solution)/shard_map/input_gradients/pallas_call | solution.py:1668
  448.1 0.0 copy-start.1
  448.1 4.8 %bitcast_add_fusion = f32[1536,512]{1,0:T(8,128)} fusion(bf16[1536,512]{1,0:T(8,128)(2,1)} %get-tuple-element.86, bf16[3,1536,1024]{2,1,0:T(8,128)(2,1)} %get-tuple-element.78.got, bf16[3,1536,2048]{2,1,0:T(8,128)(2,1)} %get-tuple-element.68.grads), kind=kLoop, calls=%fused_computation | loop fusion | flops 3932160 | bytes 7864320 | tf_op jit(solution)/shard_map/add | solution.py:1788
  452.9 0.0 copy-done.1
  452.9 0.0 copy-start.7
  452.9 0.0 copy-start.2
  452.9 5.3 %convert_add_fusion = (f32[1,1536,512]{2,1,0:T(8,128)}, f32[1,1536,512]{2,1,0:T(8,128)}) fusion(bf16[2,1536,512]{2,1,0:T(8,128)(2,1)S(1)} %copy-done.1, bf16[3,1536,1024]{2,1,0:T(8,128)(2,1)} %get-tuple-element.78.got, bf16[3,1536,2048]{2,1,0:T(8,128)(2,1)} %get-tuple-element.68.grads), kind=kLoop, calls=%fused_computation.1 | loop fusion | flops 7864320 | bytes 15728640 | tf_op jit(solution)/shard_map/add | solution.py:1788
  458.2 0.0 copy-done.7
  458.2 0.0 copy-start
  458.2 0.6 dynamic-slice_bitcast_fusion
  458.8 0.6 slice_bitcast_fusion
  459.4 0.0 copy-done.2
  459.4 1.3 copy.40
  460.7 0.0 copy-done
  460.7 0.0 copy-start.4
  460.7 0.0 copy-start.6
  460.7 0.0 copy-start.5
  460.7 2.0 copy.41
  462.7 0.0 copy-done.4
  462.7 0.0 copy-start.3
  462.7 1.0 copy.42
  463.7 0.0 copy-done.6
  463.7 0.7 copy.43
  464.4 0.0 copy-done.5
  464.4 0.7 copy.44
  465.0 0.0 copy-done.3
  465.0 1.0 copy.45
  (3 shorter events, 0.0 us)
Async XLA Ops:
  448.1 4.8 %copy-start.1 = (bf16[2,1536,512]{2,1,0:T(8,128)(2,1)S(1)}, bf16[2,1536,512]{2,1,0:T(8,128)(2,1)}, u32[]{:S(2)}) copy-start(bf16[2,1536,512]{2,1,0:T(8,128)(2,1)} %get-tuple-element.85) | copy-start | bytes 9437188
  452.9 5.3 %copy-start.7 = (f32[8,128]{1,0:T(8,128)S(1)}, f32[8,128]{1,0:T(8,128)}, u32[]{:S(2)}) copy-start(f32[8,128]{1,0:T(8,128)} %get-tuple-element.80) | copy-start | bytes 12292
  452.9 6.5 %copy-start.2 = (bf16[512,2048]{1,0:T(8,128)(2,1)S(1)}, bf16[512,2048]{1,0:T(8,128)(2,1)}, u32[]{:S(2)}) copy-start(bf16[512,2048]{1,0:T(8,128)(2,1)} %get-tuple-element.108) | copy-start | bytes 6291460
  458.2 2.5 copy-start
  460.7 2.0 copy-start.4
  460.7 3.0 copy-start.6
  460.7 3.7 copy-start.5
  462.7 2.3 copy-start.3

commit v4 on v3

--- a/solution.py
+++ b/solution.py
@@ -487,8 +487,9 @@
 
 def forward_kernel(
     tokens_in, cot_in, ids, weight, lengths, q_own, k_own, v_own, wo_own, gate_own, up_own, down_own, gains_in, cos, sin,
-    tokens, cot, table, x2, h2, att, qrot, krot, value, raw, probs, gains, gate, up, down, qkv_out, wo_out,
-    qkv, wo, h1, proj, in_buf, mid_buf, part, summed, gain_rows, gains_own,
+    tokens_out, cot, table, x2_out, h2_out, att_out, qrot_out, krot_out, value_out, raw_out, probs_out, gains, gate, up,
+    down, qkv_out, wo_out,
+    tokens, x2, h2, att, qrot, krot, value, raw, probs, save_sem, qkv, wo, h1, proj, in_buf, mid_buf, part, summed, gain_rows, gains_own,
     w_send, w_recv, core_send, core_recv, g_send, g_recv, h_send, h_recv, own_sem, out_sem, r_send, r_recv, t_sem, *line,
 ):
     c = lax.axis_index("expert")
@@ -509,6 +510,15 @@
     def _():
         pl.semaphore_wait(barrier, len(others) + 1)
 
+    saves = [
+        pltpu.make_async_copy(src, dst, save_sem.at[i])
+        for i, (src, dst) in enumerate(
+            (
+                (tokens, tokens_out), (qrot, qrot_out), (krot, krot_out), (value, value_out), (raw, raw_out),
+                (probs, probs_out), (att, att_out), (x2, x2_out), (h2, h2_out),
+            )
+        )
+    ]
     rows, width = tokens.shape
     piece = wo_own.shape[0]
     half = piece // 2
@@ -678,6 +688,8 @@
         probs[h, 0:block, block:] = jnp.zeros((block, block), bf16)
 
     over(q_cols // 128, head)
+    for x in saves[:7]:
+        x.start()
     for k, waits in ((1, (3,)), (2, (2,)), (3, (4, 5))):
         for i in waits:
             move(1, i).wait_recv()
@@ -710,11 +722,15 @@
     line_sum_steps(proj, in_buf, mid_buf, part, summed, line, "tensor", finish)
     pass_on(3)
     pass_on(4)
+    saves[7].start()
     over(CHUNKS, lambda i: give(i).wait())
+    saves[8].start()
     for m in (2, 3, 4):
         arrived(m)
     save_qkv.wait()
     save_wo.wait()
+    for x in saves:
+        x.wait()
     for k in range(4):
         cot_away(k).wait()
     table_away().wait()
@@ -735,22 +751,17 @@
     tall = gate_own.shape[0]
     vmem, anyspace = pl.BlockSpec(memory_space=pltpu.VMEM), pl.BlockSpec(memory_space=pl.ANY)
     shape = jax.ShapeDtypeStruct
+    tokens_shape, x2_shape, h2_shape = ((rows, width), bf16), ((rows, width), f32), ((2 * rows, width), bf16)
+    att_shape, head_shape = ((rows, q_cols), bf16), ((rows, 128), bf16)
+    raw_shape, probs_shape = ((rows, qkv_cols), f32), ((q_cols // 128, rows, rows), bf16)
+    kept = [tokens_shape, x2_shape, h2_shape, att_shape, att_shape, head_shape, head_shape, raw_shape, probs_shape]
     outs = [
-        (shape((rows, width), bf16), vmem),
+        (shape(*tokens_shape), anyspace),
         (shape((rows, width), bf16), anyspace),
         (shape((2 * rows, 128), f32), vmem),
-        (shape((rows, width), f32), vmem),
-        (shape((2 * rows, width), bf16), vmem),
-        (shape((rows, q_cols), bf16), vmem),
-        (shape((rows, q_cols), bf16), vmem),
-        (shape((rows, 128), bf16), vmem),
-        (shape((rows, 128), bf16), vmem),
-        (shape((rows, qkv_cols), f32), vmem),
-        (shape((q_cols // 128, rows, rows), bf16), vmem),
+        *[(shape(*k), anyspace) for k in kept[1:]],
         (shape((4, 2, 8, 128), f32), vmem),
-        (shape((tall, width), bf16), anyspace),
-        (shape((tall, width), bf16), anyspace),
-        (shape((tall, width), bf16), anyspace),
+        *[(shape((tall, width), bf16), anyspace)] * 3,
         (shape((width, qkv_cols), bf16), anyspace),
         (shape((width, q_cols), bf16), anyspace),
     ]
@@ -765,7 +776,9 @@
         + [anyspace] * 7
         + [vmem] * 3,
         out_specs=[o[1] for o in outs],
-        scratch_shapes=[
+        scratch_shapes=[pltpu.VMEM(*k) for k in kept]
+        + [
+            dma((9,)),
             pltpu.VMEM((width, qkv_cols), bf16),
             pltpu.VMEM((width, q_cols), bf16),
             big, big, big, big, big, big,
@@ -839,9 +852,9 @@
 
 
 def expert_kernel(
-    h2, g_own, g_other, mine, gate_own, up_own, down_own, gate_in, up_in, down_in,
+    h2_in, g_own, g_other, mine_in, gate_own, up_own, down_own, gate_in, up_in, down_in,
     grad_h2, out, out_other, grads, got,
-    g, g_sem, gate, up, down, acts, drow, rbuf, in_buf, mid_buf, stage,
+    g, g_sem, h2, mine, gate, up, down, acts, drow, rbuf, in_buf, mid_buf, stage, late_gate, late_up,
     load_sem, rest_sem, w_send, w_recv, x_send, x_recv, s_send, s_recv, keep_sem, out_sem, *line,
 ):
     to = plane_partners()
@@ -896,7 +909,9 @@
         )
 
     load_g = lane_copies(g_own, g.at[pl.ds(0, rows)], [g_sem.at[k] for k in range(4)], to) + [
-        pltpu.make_async_copy(g_other, g.at[pl.ds(rows, rows)], g_sem.at[4])
+        pltpu.make_async_copy(g_other, g.at[pl.ds(rows, rows)], g_sem.at[4]),
+        pltpu.make_async_copy(h2_in, h2, g_sem.at[5]),
+        pltpu.make_async_copy(mine_in, mine, g_sem.at[6]),
     ]
     for x in load_g:
         x.start()
@@ -907,7 +922,10 @@
     for x in load_g:
         x.wait()
 
-    def hidden_tile(i):
+    def gate_up(i):
+        return nt(h2[...], gate[tile(i)]), nt(h2[...], up[tile(i)])
+
+    def hidden_tile(i, gate_value, up_value):
         t = turn(i)
         first = (t * 256) // units
         edge = (first + 1) * units - t * 256
@@ -915,8 +933,6 @@
         pick = lambda e: jnp.sum(jnp.where(lanes == e + first_expert, mine[...], 0.0), axis=1, keepdims=True)
         column = lax.broadcasted_iota(jnp.int32, (2 * rows, 256), 1)
         scale = jnp.where(column < edge, pick(first), pick(first + 1))
-        gate_value = nt(h2[...], gate[tile(i)])
-        up_value = nt(h2[...], up[tile(i)])
         grad_act = nt(g[...], down[tile(i)]) * scale
         sig = jax.nn.sigmoid(gate_value)
         silu = gate_value * sig
@@ -977,7 +993,7 @@
         for x in (load_own, load_rest):
             for j in range(3):
                 x(i, j).wait()
-        hidden_tile(i)
+        hidden_tile(i, *gate_up(i))
 
     over(4, early_tile)
 
@@ -997,10 +1013,17 @@
     for i in (4, 5):
         for j in range(3):
             load_own(i, j).wait()
-    for j in range(3):
+    for j in (0, 1):
         for n in (2, 3, 4, 5):
             shard_move(j, n).wait_recv()
-    over(6, hidden_tile, 4)
+
+    def late_gate_up(i):
+        late_gate[i - 4], late_up[i - 4] = gate_up(i)
+
+    over(6, late_gate_up, 4)
+    for n in (2, 3, 4, 5):
+        shard_move(2, n).wait_recv()
+    over(6, lambda i: hidden_tile(i, late_gate[i - 4], late_up[i - 4]), 4)
 
     step = rows // CHUNKS
 
@@ -1169,9 +1192,14 @@
             shape((3, tall, width), bf16),
             shape((3, tall, width // 2), bf16),
         ],
-        in_specs=[vmem, anyspace, anyspace, vmem] + [anyspace] * 6,
+        in_specs=[anyspace] * 10,
         out_specs=[vmem, anyspace, anyspace, anyspace, anyspace],
-        scratch_shapes=[pltpu.VMEM((2 * rows, width), bf16), dma((5,))]
+        scratch_shapes=[
+            pltpu.VMEM((2 * rows, width), bf16),
+            dma((7,)),
+            pltpu.VMEM((2 * rows, width), bf16),
+            pltpu.VMEM(mine.shape, f32),
+        ]
         + [pltpu.VMEM((tall, width), bf16)] * 3
         + [
             pltpu.VMEM((3, 2 * rows, tall), bf16),
@@ -1180,6 +1208,8 @@
             pltpu.VMEM((rows, width), bf16),
             pltpu.VMEM((rows, width), bf16),
             pltpu.VMEM((2, 512, width // 2), bf16),
+            pltpu.VMEM((2, 2 * rows, 256), f32),
+            pltpu.VMEM((2, 2 * rows, 256), f32),
             dma((6, 3)), dma((4, 3)), dma((3, 6)), dma((3, 6)), dma((CHUNKS,)), dma((CHUNKS,)), dma((3, 6, 2)), dma((3, 6, 2)),
             dma((2, 2)), dma((3, width // 256)),
         ]

time: 470 us -> 458 us (0.974)
  Pallas kernels: 443 us -> 430 us
    pallas_call x1, Pallas kernels: 144 us -> 138 us  [expert_call(): pl.pallas_call(expert_kernel, out_shape=[shape((rows, width), bf16), shap...]
    pallas_call x1, Pallas kernels: 160 us -> 154 us  [forward_call(): pl.pallas_call(forward_kernel, out_shape=[o[0] for o in outs], in_specs=[...]
where the time goes in v4:
time: 458 us; the launch traced here: 454 us
  Pallas kernels  430 us (94%)
  other arithmetic  10.7 us (2%)
  local copies, waits for them, and re-layouts  10.5 us (2%)
    pallas_call x1, Pallas kernels, forward_call(): pl.pallas_call(forward_kernel, out_shape=[o[0] for o in outs], in_specs=[...  154 us
    pallas_call x1, Pallas kernels, expert_call(): pl.pallas_call(expert_kernel, out_shape=[shape((rows, width), bf16), shap...  138 us
    pallas_call x1, Pallas kernels, last_call(): pl.pallas_call(last_kernel, out_shape=[shape((rows, width), f32), shape((...  69.1 us
    pallas_call x1, Pallas kernels, attention_back_call(): pl.pallas_call(attention_back_kernel, out_shape=[shape((rows, width), bf1...  68.9 us
    add x2, other arithmetic, local_fast(): grads[m, :, :part].astype(f32) + got[m, :, :part].astype(f32)  10.1 us

profile of v4, /device:TPU:0, one launch (start us, length us, event | category | flops | bytes accessed | tf_op | source)
XLA Modules:
  0.0 453.5 jit_solution(10282079656078805182)
XLA Ops:
  0.7 2.8 concatenate.3
  3.4 0.6 bitcast_convert_fusion.gains_in
  4.7 154.3 %forward_to_experts.1 = (bf16[512,2048]{1,0:T(8,128)(2,1)}, bf16[512,2048]{1,0:T(8,128)(2,1)}, f32[1024,128]{1,0:T(8,128)}, f32[512,2048]{1,0:T(8,128)}, bf16[10...) custom-call(bf16[512,2048]{1,0:T(8,128)(2,1)} %tokens_in.1, ...), custom_call_target="tpu_custom_call" | custom-call | flops 8000000000 | bytes 60000000 | tf_op jit(solution)/shard_map/forward_to_experts/pallas_call | solution.py:770
  159.0 138.1 %experts.1 = (bf16[512,2048]{1,0:T(8,128)(2,1)}, bf16[512,2048]{1,0:T(8,128)(2,1)}, bf16[512,2048]{1,0:T(8,128)(2,1)}, bf16[3,1536,2048]{2,1,0:T(8,128)(2,1)}, bf16[3,1536,1024]{2,1,0:T(8,128)(2,1)}) custom-call(bf16[1024,2048]{1,0:T(8,128)(2,1)} %get-tuple-element.51.h2_in, bf16[512,2048]{1,0:T(8,128)(2,1)} %cot_in.3, ...), custom_call_target="tpu_custom_call" | custom-call | flops 57999998976 | bytes 60000000 | tf_op jit(solution)/shard_map/experts/pallas_call | solution.py:1186
  297.1 68.9 %attention_backward.1 = (bf16[512,2048]{1,0:T(8,128)(2,1)}, f32[512,2048]{1,0:T(8,128)}, bf16[512,2048]{1,0:T(8,128)(2,1)}, bf16[512,1280]{1,0:T(8,128)(2,1)}, b...) custom-call(f32[4,2,8,128]{3,2,1,0:T(8,128)} %get-tuple-element.50.g, ...), custom_call_target="tpu_custom_call", output_to_operand_aliasing={{7}: (16, {})} | custom-call | flops 8999999488 | bytes 60000000 | tf_op jit(solution)/shard_map/attention_backward/pallas_call | solution.py:1446
  366.0 69.1 %input_gradients.1 = (f32[512,2048]{1,0:T(8,128)}, f32[256,1024]{1,0:T(8,128)}, f32[256,128]{1,0:T(8,128)}, f32[256,128]{1,0:T(8,128)}, f32[256,1024]{1,0:T(8,12...) custom-call(f32[4,2,8,128]{3,2,1,0:T(8,128)} %get-tuple-element.50.gains, f32[8,2048]{1,0:T(8,128)} %get-tuple-element.71.gain_grads, ...), custom_call_target="tpu_custom_call" | custom-call | flops 5000000000 | bytes 40000000 | tf_op jit(solution)/shard_map/input_gradients/pallas_call | solution.py:1698
  435.1 0.0 copy-start.1
  435.2 4.8 %bitcast_add_fusion = f32[1536,512]{1,0:T(8,128)} fusion(bf16[1536,512]{1,0:T(8,128)(2,1)} %get-tuple-element.86, bf16[3,1536,1024]{2,1,0:T(8,128)(2,1)} %get-tuple-element.78.got, bf16[3,1536,2048]{2,1,0:T(8,128)(2,1)} %get-tuple-element.68.grads), kind=kLoop, calls=%fused_computation | loop fusion | flops 3932160 | bytes 7864320 | tf_op jit(solution)/shard_map/add | solution.py:1818
  440.0 0.0 copy-done.1
  440.0 0.0 copy-start.7
  440.0 0.0 copy-start.2
  440.0 5.3 %convert_add_fusion = (f32[1,1536,512]{2,1,0:T(8,128)}, f32[1,1536,512]{2,1,0:T(8,128)}) fusion(bf16[2,1536,512]{2,1,0:T(8,128)(2,1)S(1)} %copy-done.1, bf16[3,1536,1024]{2,1,0:T(8,128)(2,1)} %get-tuple-element.78.got, bf16[3,1536,2048]{2,1,0:T(8,128)(2,1)} %get-tuple-element.68.grads), kind=kLoop, calls=%fused_computation.1 | loop fusion | flops 7864320 | bytes 15728640 | tf_op jit(solution)/shard_map/add | solution.py:1818
  445.3 0.0 copy-done.7
  445.3 0.0 copy-start
  445.3 0.6 dynamic-slice_bitcast_fusion
  445.9 0.6 slice_bitcast_fusion
  446.5 0.0 copy-done.2
  446.5 1.3 copy.40
  447.8 0.0 copy-done
  447.8 0.0 copy-start.4
  447.8 0.0 copy-start.6
  447.8 0.0 copy-start.5
  447.8 2.0 copy.41
  449.8 0.0 copy-done.4
  449.8 0.0 copy-start.3
  449.8 1.0 copy.42
  450.8 0.0 copy-done.6
  450.8 0.7 copy.43
  451.5 0.0 copy-done.5
  451.5 0.7 copy.44
  452.1 0.0 copy-done.3
  452.1 1.0 copy.45
  (3 shorter events, 0.0 us)
Async XLA Ops:
  435.1 4.8 %copy-start.1 = (bf16[2,1536,512]{2,1,0:T(8,128)(2,1)S(1)}, bf16[2,1536,512]{2,1,0:T(8,128)(2,1)}, u32[]{:S(2)}) copy-start(bf16[2,1536,512]{2,1,0:T(8,128)(2,1)} %get-tuple-element.85) | copy-start | bytes 9437188
  440.0 5.3 %copy-start.7 = (f32[8,128]{1,0:T(8,128)S(1)}, f32[8,128]{1,0:T(8,128)}, u32[]{:S(2)}) copy-start(f32[8,128]{1,0:T(8,128)} %get-tuple-element.80) | copy-start | bytes 12292
  440.0 6.5 %copy-start.2 = (bf16[512,2048]{1,0:T(8,128)(2,1)S(1)}, bf16[512,2048]{1,0:T(8,128)(2,1)}, u32[]{:S(2)}) copy-start(bf16[512,2048]{1,0:T(8,128)(2,1)} %get-tuple-element.108) | copy-start | bytes 6291460
  445.3 2.5 copy-start
  447.8 2.0 copy-start.4
  447.8 3.0 copy-start.6
  447.8 3.7 copy-start.5
  449.8 2.3 copy-start.3

commit v5 on v4

--- a/solution.py
+++ b/solution.py
@@ -1493,9 +1493,9 @@
 
 
 def last_kernel(
-    gains, gain_grads, part_in, dx2_in, tokens_in, grad_qkv_in, low_in, att_in, grads, got,
-    tokens_grad_out, q_shard, k_shard, v_shard, wo_shard, gain_sum, got2_up,
-    tokens_grad, d_sem, part, dx2, tokens, grad_qkv, low, att, f_sem, h1, in_buf, mid_buf, half_sum, summed, gain_rows, wo_all, qkv_all, wo_core, qkv_core, wo_one, qkv_one, wo_two, qkv_two,
+    gains, gain_grads, part_in, dx2_in, tokens_in, grad_qkv_in, low_in, att_in, grads, got, got2,
+    tokens_grad_out, q_shard, k_shard, v_shard, wo_shard, gain_sum, got2_up, down_shard, gate_shard,
+    f_in, f_out, fi_sem, fo_sem, tokens_grad, d_sem, part, dx2, tokens, grad_qkv, low, att, f_sem, h1, in_buf, mid_buf, half_sum, summed, gain_rows, wo_all, qkv_all, wo_core, qkv_core, wo_one, qkv_one, wo_two, qkv_two,
     ga, z_got, g_out, g_got, load_a, load_b, on_buf, l_sem, s_send, s_recv,
     z_send, z_recv, c_send, c_recv, f_send, f_recv, t_send, t_recv, g_send, g_recv, *line,
 ):
@@ -1532,6 +1532,41 @@
     )
     start(0)
     start(1)
+
+    def final_loads(u):
+        at = (u // 6, tile(u % 6), pl.ds(0, wide))
+        return [
+            pltpu.make_async_copy(src.at[at], f_in.at[u % 2, j], fi_sem.at[u % 2, j])
+            for j, src in enumerate((grads, got, got2))
+        ]
+
+    def final_out(u, f):
+        for m, shard in enumerate((down_shard, gate_shard)):
+
+            @pl.when(u // 6 == m)
+            def _(shard=shard):
+                f(pltpu.make_async_copy(f_out.at[u % 2], shard.at[tile(u % 6)], fo_sem.at[u % 2]))
+
+    def final_tile(u):
+        for x in final_loads(u):
+            x.wait()
+
+        @pl.when(u >= 2)
+        def _():
+            final_out(u - 2, lambda x: x.wait())
+
+        a, b, c = (f_in[u % 2, j].astype(f32) for j in range(3))
+        f_out[u % 2] = a + b + c
+        final_out(u, lambda x: x.start())
+
+        @pl.when(u + 2 < 12)
+        def _():
+            for x in final_loads(u + 2):
+                x.start()
+
+    for u in range(2):
+        for x in final_loads(u):
+            x.start()
     gain_vectors(gains, gain_rows)
     ga[...] = jnp.zeros_like(ga)
 
@@ -1592,6 +1627,10 @@
             for x in fetch[1:]:
                 x.wait()
             over(rows // 64, hidden_one)
+
+        @pl.when(i >= 8)
+        def _():
+            final_tile(i - 8)
 
         @pl.when(i < 6)
         def _():
@@ -1674,6 +1713,7 @@
         total += g_got[j]
     gain_sum[...] = total
     second_done()
+    over(12, lambda u: final_out(u, lambda x: x.wait()), 10)
     over(CHUNKS, lambda i: give_back(i).wait())
     for m in range(2):
         for k in range(4):
@@ -1686,7 +1726,7 @@
         gain_move(j).wait_send()
 
 
-def last_call(part, dx2, tokens, grad_qkv, low, att, gains, gain_grads, grads, got):
+def last_call(part, dx2, tokens, grad_qkv, low, att, gains, gain_grads, grads, got, got2):
     rows, width = tokens.shape
     q_cols, qkv_cols = att.shape[1], grad_qkv.shape[1]
     piece = width // 8
@@ -1705,10 +1745,16 @@
             shape((piece, q_cols), f32),
             shape((8, 128), f32),
             shape((got.shape[1], width // 4), bf16),
+            shape((got.shape[1], width // 4), f32),
+            shape((got.shape[1], width // 4), f32),
         ],
-        in_specs=[vmem] * 2 + [pl.BlockSpec(memory_space=pl.ANY)] * 8,
-        out_specs=[pl.BlockSpec(memory_space=pl.ANY)] + [vmem] * 5 + [pl.BlockSpec(memory_space=pl.ANY)],
+        in_specs=[vmem] * 2 + [pl.BlockSpec(memory_space=pl.ANY)] * 9,
+        out_specs=[pl.BlockSpec(memory_space=pl.ANY)] + [vmem] * 5 + [pl.BlockSpec(memory_space=pl.ANY)] * 3,
         scratch_shapes=[
+            pltpu.VMEM((2, 3, 256, width // 4), bf16),
+            pltpu.VMEM((2, 256, width // 4), f32),
+            dma((2, 3)),
+            dma((2,)),
             pltpu.VMEM((rows, width), f32),
             dma((CHUNKS,)),
             big,
@@ -1742,7 +1788,7 @@
         ),
         cost_estimate=pl.CostEstimate(flops=5 * 10**9, bytes_accessed=40 * 10**6, transcendentals=10**5),
         name="input_gradients",
-    )(gains, gain_grads, part, dx2, tokens, grad_qkv, low, att, grads, got)
+    )(gains, gain_grads, part, dx2, tokens, grad_qkv, low, att, grads, got, got2)
 
 
 def local_fast(
@@ -1810,14 +1856,12 @@
         grad_hidden_two, mixed_rows, cotangent, rotated_query, key_rot, value_low, raw, gains, cos2, sin2,
         prob_low, full_output, full_qkv, out_own, out_other, grads, got,
     )
-    tokens_grad, query_shard, key_shard, value_shard, output_shard, gain_sum, got2_up = last_call(
+    tokens_grad, query_shard, key_shard, value_shard, output_shard, gain_sum, got2_up, down_shard, gate_shard = last_call(
         grad_hidden_one, grad_mixed, inputs_low, grad_qkv_low, grad_proj_low, attended_low, gains, gain_grads,
-        grads, got,
-    )
-    down_shard, gate_shard, up_shard = (
-        (grads[m, :, :part].astype(f32) + got[m, :, :part].astype(f32) + last.astype(f32)).reshape(group, hidden, part)
-        for m, last in enumerate((got2[0], got2[1], got2_up))
-    )
+        grads, got, got2,
+    )
+    up_shard = grads[2, :, :part].astype(f32) + got[2, :, :part].astype(f32) + got2_up.astype(f32)
+    down_shard, gate_shard, up_shard = (x.reshape(group, hidden, part) for x in (down_shard, gate_shard, up_shard))
     own_head = lambda row: lax.dynamic_slice_in_dim(gain_sum[row], own_place, nq, 0)
     return (
         output,

time: 458 us -> 457 us (level)
  other arithmetic: 10.7 us -> 5.4 us
  local copies, waits for them, and re-layouts: 10.5 us -> 15.3 us
    add x2 -> x1, other arithmetic: 10.1 us -> 4.8 us  [local_fast(): grads[2, :, :part].astype(f32) + got[2, :, :part].astype(f32)]
    unnamed x22 -> x26, local copies, waits for them, and re-layouts: 6.62 us -> 11.4 us
where the time goes in v5:
time: 457 us; the launch traced here: 454 us
  Pallas kernels  431 us (94%)
  local copies, waits for them, and re-layouts  15.3 us (3%)
  other arithmetic  5.4 us (1%)
    pallas_call x1, Pallas kernels, forward_call(): pl.pallas_call(forward_kernel, out_shape=[o[0] for o in outs], in_specs=[...  154 us
    pallas_call x1, Pallas kernels, expert_call(): pl.pallas_call(expert_kernel, out_shape=[shape((rows, width), bf16), shap...  138 us
    pallas_call x1, Pallas kernels, last_call(): pl.pallas_call(last_kernel, out_shape=[shape((rows, width), f32), shape((...  69.5 us
    pallas_call x1, Pallas kernels, attention_back_call(): pl.pallas_call(attention_back_kernel, out_shape=[shape((rows, width), bf1...  69 us
    unnamed x26, local copies, waits for them, and re-layouts  11.4 us

profile of v5, /device:TPU:0, one launch (start us, length us, event | category | flops | bytes accessed | tf_op | source)
XLA Modules:
  0.0 453.5 jit_solution(13911378972109269157)
XLA Ops:
  0.7 2.8 concatenate.3
  3.4 0.6 bitcast_convert_fusion.gains_in
  4.7 154.4 %forward_to_experts.1 = (bf16[512,2048]{1,0:T(8,128)(2,1)}, bf16[512,2048]{1,0:T(8,128)(2,1)}, f32[1024,128]{1,0:T(8,128)}, f32[512,2048]{1,0:T(8,128)}, bf16[10...) custom-call(bf16[512,2048]{1,0:T(8,128)(2,1)} %tokens_in.1, ...), custom_call_target="tpu_custom_call" | custom-call | flops 8000000000 | bytes 60000000 | tf_op jit(solution)/shard_map/forward_to_experts/pallas_call | solution.py:770
  159.0 138.1 %experts.1 = (bf16[512,2048]{1,0:T(8,128)(2,1)}, bf16[512,2048]{1,0:T(8,128)(2,1)}, bf16[512,2048]{1,0:T(8,128)(2,1)}, bf16[3,1536,2048]{2,1,0:T(8,128)(2,1)}, bf16[3,1536,1024]{2,1,0:T(8,128)(2,1)}) custom-call(bf16[1024,2048]{1,0:T(8,128)(2,1)} %get-tuple-element.53.h2_in, bf16[512,2048]{1,0:T(8,128)(2,1)} %cot_in.3, ...), custom_call_target="tpu_custom_call" | custom-call | flops 57999998976 | bytes 60000000 | tf_op jit(solution)/shard_map/experts/pallas_call | solution.py:1186
  297.1 69.0 %attention_backward.1 = (bf16[512,2048]{1,0:T(8,128)(2,1)}, f32[512,2048]{1,0:T(8,128)}, bf16[512,2048]{1,0:T(8,128)(2,1)}, bf16[512,1280]{1,0:T(8,128)(2,1)}, b...) custom-call(f32[4,2,8,128]{3,2,1,0:T(8,128)} %get-tuple-element.52.g, ...), custom_call_target="tpu_custom_call", output_to_operand_aliasing={{7}: (16, {})} | custom-call | flops 8999999488 | bytes 60000000 | tf_op jit(solution)/shard_map/attention_backward/pallas_call | solution.py:1446
  366.2 69.5 %input_gradients.1 = (f32[512,2048]{1,0:T(8,128)}, f32[256,1024]{1,0:T(8,128)}, f32[256,128]{1,0:T(8,128)}, f32[256,128]{1,0:T(8,128)}, f32[256,1024]{1,0:T(8,12...) custom-call(f32[4,2,8,128]{3,2,1,0:T(8,128)} %get-tuple-element.52.gains, ...), custom_call_target="tpu_custom_call" | custom-call | flops 5000000000 | bytes 40000000 | tf_op jit(solution)/shard_map/input_gradients/pallas_call | solution.py:1738
  435.6 0.0 copy-start.8
  435.6 0.0 copy-start.3
  435.7 4.8 %bitcast_add_fusion = f32[1536,512]{1,0:T(8,128)} fusion(bf16[1536,512]{1,0:T(8,128)(2,1)} %get-tuple-element.89, bf16[3,1536,1024]{2,1,0:T(8,128)(2,1)} %get-tuple-element.80.got, bf16[3,1536,2048]{2,1,0:T(8,128)(2,1)} %get-tuple-element.70.grads), kind=kLoop, calls=%fused_computation | loop fusion | flops 3932160 | bytes 7864320 | tf_op jit(solution)/shard_map/add | solution.py:1863
  440.5 0.0 copy-done.8
  440.5 0.0 copy-start
  440.5 0.6 dynamic-slice_bitcast_fusion
  441.1 0.6 slice_bitcast_fusion
  441.6 0.0 copy-done.3
  441.6 1.3 copy.42
  443.0 0.0 copy-done
  443.0 0.0 copy-start.5
  443.0 0.0 copy-start.7
  443.0 0.0 copy-start.6
  443.0 0.0 copy-start.4
  443.0 2.1 copy.43
  445.1 0.0 copy-done.5
  445.1 0.0 copy-start.2
  445.1 1.0 copy.44
  446.1 0.0 copy-done.7
  446.1 0.7 copy.45
  446.7 0.0 copy-done.6
  446.8 0.7 copy.46
  447.4 0.0 copy-done.4
  447.4 1.0 copy.47
  448.4 0.0 copy-done.2
  448.4 0.0 copy-start.1
  448.4 1.7 copy.48
  450.0 1.4 copy-done.1
  451.4 1.7 copy.49
  (3 shorter events, 0.0 us)
Async XLA Ops:
  435.6 4.8 %copy-start.8 = (f32[8,128]{1,0:T(8,128)S(1)}, f32[8,128]{1,0:T(8,128)}, u32[]{:S(2)}) copy-start(f32[8,128]{1,0:T(8,128)} %get-tuple-element.83) | copy-start | bytes 12292
  435.6 6.0 %copy-start.3 = (bf16[512,2048]{1,0:T(8,128)(2,1)S(1)}, bf16[512,2048]{1,0:T(8,128)(2,1)}, u32[]{:S(2)}) copy-start(bf16[512,2048]{1,0:T(8,128)(2,1)} %get-tuple-element.110) | copy-start | bytes 6291460
  440.5 2.5 copy-start
  443.0 2.2 copy-start.5
  443.0 3.1 copy-start.7
  443.0 3.8 copy-start.6
  443.0 4.4 copy-start.4
  445.1 3.3 copy-start.2
  448.4 3.0 copy-start.1
